TPU v7x, 32 devices: a whole 2x2x4 slice. The times are simulated.
32 devices in a mesh: groups: 2 (over y), ctx: 4 (over z), exp: 4 (over x, core).
Axes of the slice: x: 2, y: 2, z: 4, core: 2. Of those that a mesh axis runs over, the one named last changes fastest.
Arguments:
- queries: bfloat16 [1024, 2048], P(('groups', 'ctx'), 'exp'), parts along dimension 0, may hold values from -10 to 10
- keys: bfloat16 [4096, 512], P(('groups', 'ctx'), 'exp'), parts along dimension 0, may hold values from -10 to 10
- values: bfloat16 [4096, 512], P(('groups', 'ctx'), 'exp'), parts along dimension 0, may hold values from -6 to 6
- out_weight: bfloat16 [2048, 4096], P('exp', 'ctx'), may hold values from -0.125 to 0.125
- residual: bfloat16 [1024, 4096], P(('groups', 'ctx'), 'exp'), parts along dimension 0, may hold values from -2 to 2
- router: float32 [4096, 4], replicated, may hold values from -0.09375 to 0.09375
- routes: int32 [1024, 2], P(('groups', 'ctx')), parts along dimension 0, may hold values from 0 to 3, all different within a row; in each aligned block of 128 rows (0 to 127, 128 to 255, ...) at most 64 rows name the same one
- order: int32 [1024], P(('groups', 'ctx')), parts along dimension 0, may hold values from 0 to 511, each once
- expert_gate: bfloat16 [4, 4096, 7168], P('exp', None, 'ctx'), may hold values from -0.09375 to 0.09375
- expert_up: bfloat16 [4, 4096, 7168], P('exp', None, 'ctx'), may hold values from -0.09375 to 0.09375
- expert_down: bfloat16 [4, 7168, 4096], P('exp', 'ctx'), may hold values from -0.0625 to 0.0625
Outputs:
- layer_output: bfloat16 [1024, 4096], P(('groups', 'ctx', 'exp')), parts along dimension 0
There are 2 independent parts, one for each index of `groups`. A program takes and returns all parts, laid end to end along the dimension named above; an argument that names none is the same for every part. Nothing has to cross between parts.
Inputs may be any that keep to these rules, and one draw needn't show every extreme that they name: `routes`: in the 128 rows of one index of ctx, no expert is named by more than 64 rows, a bound that some block reaches; a row names two different experts.
All inputs are finite; a program needn't handle non-finite values.
Results may differ from a plain program's by a relative error of at most 0.022.
Values may be sent and summed in bfloat16 or wider, within the bound.
No kernel may reach another device: no remote copies, remote signals or barrier semaphores. Data moves between devices by JAX's collectives and lax.ppermute only.
A program may use at most 128 MiB of HBM per device.

v0:
```python
import math

import jax
import jax.numpy as jnp
from jax import lax
from jax.sharding import PartitionSpec as P


def normalize(stream):
    return (stream * lax.rsqrt(jnp.mean(stream * stream, axis=1, keepdims=True) + 1e-05)).astype(
        jnp.bfloat16
    )


def local(
    queries,
    keys,
    values,
    out_weight,
    residual,
    router,
    routes,
    order,
    expert_gate,
    expert_up,
    expert_down,
):
    tok_rows = queries.shape[0]
    head_dim = keys.shape[1]
    head_count = queries.shape[1] // head_dim
    ctx_count = lax.axis_size("ctx")
    exp_count = lax.axis_size("exp")
    context_length = keys.shape[0] * ctx_count
    visible_end = context_length - tok_rows * ctx_count + order
    score_scale = 1.0 / math.sqrt(head_dim)
    query_blocks = queries.reshape(tok_rows, head_count, head_dim)
    keys_all, values_all, weight_rows = (
        lax.all_gather(keys, "ctx", axis=0, tiled=True),
        lax.all_gather(values, "ctx", axis=0, tiled=True),
        lax.all_gather(out_weight, "ctx", axis=1, tiled=True),
    )
    score = (
        jnp.einsum("tqd,jd->qtj", query_blocks, keys_all, preferred_element_type=jnp.float32)
        * score_scale
    )
    key_positions = jnp.arange(keys_all.shape[0], dtype=jnp.int32)
    visible = key_positions[None, None, :] <= visible_end[None, :, None]
    score, visible = (jnp.where(visible, score, -1e30), visible)
    highest = jnp.max(score, axis=2, keepdims=True)
    weight = jnp.where(visible, jnp.exp(score - highest), 0.0)
    total = jnp.sum(weight, axis=2)
    summed = jnp.einsum(
        "qtj,jd->tqd", weight.astype(jnp.bfloat16), values_all, preferred_element_type=jnp.float32
    )
    attended = (
        (summed / total.T[:, :, None]).astype(jnp.bfloat16).reshape(tok_rows, head_count * head_dim)
    )
    partial_value = jnp.dot(attended, weight_rows, preferred_element_type=jnp.float32)
    column_width = residual.shape[1]
    column_start = lax.axis_index("exp") * column_width
    own_columns = lax.dynamic_slice_in_dim(
        partial_value, column_start, column_width, 1
    ) + residual.astype(jnp.float32)
    partial_value = lax.dynamic_update_slice_in_dim(partial_value, own_columns, column_start, 1)
    share = tok_rows // exp_count
    share_start = lax.axis_index("exp") * share
    stream = lax.psum(partial_value.astype(jnp.bfloat16), "exp").astype(jnp.float32)
    normed = normalize(stream)
    own_stream = lax.dynamic_slice_in_dim(stream, share_start, share, 0)
    logits = jnp.dot(normed.astype(jnp.float32), router, precision=lax.Precision.HIGHEST)
    expert_ids = jnp.arange(router.shape[1], dtype=jnp.int32)
    lookup = (routes[:, :, None] == expert_ids[None, None, :]).astype(jnp.float32)
    chosen = jnp.sum(lookup * logits[:, None, :], axis=2)
    first = jax.nn.sigmoid(chosen[:, 0] - chosen[:, 1])
    second = jax.nn.sigmoid(chosen[:, 1] - chosen[:, 0])
    gates = jnp.stack([first, second], axis=1)
    mine = lax.axis_index("exp")
    named = routes == mine
    used = jnp.any(named, axis=1)
    weight_rows_gate = jnp.sum(jnp.where(named, gates, 0.0), axis=1)
    capacity = tok_rows // 2
    slot = jnp.cumsum(used.astype(jnp.int32)) - 1
    picker = (
        (slot[None, :] == jnp.arange(capacity, dtype=jnp.int32)[:, None]) & used[None, :]
    ).astype(jnp.float32)
    local_rows = jnp.dot(
        picker.astype(jnp.bfloat16), normed, preferred_element_type=jnp.float32
    ).astype(jnp.bfloat16)
    slot_gate = jnp.dot(picker, weight_rows_gate, precision=lax.Precision.HIGHEST)
    gate_here = expert_gate[0]
    up_here = expert_up[0]
    down_here = expert_down[0]
    piece = lax.all_gather(local_rows, "ctx", axis=0, tiled=True)
    gate_proj = jnp.dot(piece, gate_here, preferred_element_type=jnp.float32)
    up_proj = jnp.dot(piece, up_here, preferred_element_type=jnp.float32)
    act = (jax.nn.silu(gate_proj) * up_proj).astype(jnp.bfloat16)
    partial_rows = jnp.dot(act, down_here, preferred_element_type=jnp.float32).astype(jnp.bfloat16)
    expert_out = lax.psum_scatter(
        partial_rows.astype(jnp.float32).astype(jnp.bfloat16),
        "ctx",
        scatter_dimension=0,
        tiled=True,
    ).astype(jnp.float32)
    spread = picker.T * slot_gate[None, :]
    contribution = jnp.dot(spread, expert_out, precision=lax.Precision.HIGHEST)
    own_mixture = lax.psum_scatter(
        contribution.astype(jnp.bfloat16), "exp", scatter_dimension=0, tiled=True
    ).astype(jnp.float32)
    return (own_stream + own_mixture).astype(jnp.bfloat16)


def solution(mesh):
    return jax.shard_map(
        local,
        mesh=mesh,
        in_specs=(
            P(("groups", "ctx"), "exp"),
            P(("groups", "ctx"), "exp"),
            P(("groups", "ctx"), "exp"),
            P("exp", "ctx"),
            P(("groups", "ctx"), "exp"),
            P(),
            P(("groups", "ctx"), None),
            P(("groups", "ctx")),
            P("exp", None, "ctx"),
            P("exp", None, "ctx"),
            P("exp", "ctx", None),
        ),
        out_specs=P(("groups", "ctx", "exp"), None),
        check_vma=False,
    )
```

profile of v0, /device:TPU:0, one launch (start us, length us, event | category | flops | bytes accessed | tf_op | source)
XLA Modules:
  0.0 293.3 jit_solution(13088340451972554788)
XLA Ops:
  6.5 0.7 all-gather.3.cloned.1.call-update
  7.3 1.0 copy.25
  8.3 19.5 %all_gather.13 = bf16[2048,128]{0,1:T(8,128)(2,1)S(1)} all-gather(bf16[512,128]{0,1:T(8,128)(2,1)S(1)} %copy.25), channel_id=1, replica_groups=mesh['groups'=2,'ctx'=4,'exp'=4] {'ctx'}, dimensions={0}, use_global_device_ids=true | all-gather | bytes 655360 | tf_op jit(solution)/shard_map/all_gather | solution.py:39
  27.8 22.7 %all_gather.12 = bf16[2048,128]{1,0:T(8,128)(2,1)S(1)} all-gather(bf16[512,128]{1,0:T(8,128)(2,1)} %param.12), channel_id=1, replica_groups=mesh['groups'=2,'ctx'=4,'exp'=4] {'ctx'}, dimensions={0}, use_global_device_ids=true | all-gather | bytes 655360 | tf_op jit(solution)/shard_map/all_gather | solution.py:38
  50.5 0.7 broadcast_add_fusion
  51.2 0.2 iota_compare_fusion
  51.4 1.8 fusion.82
  53.2 1.9 fusion.28
  55.1 47.0 %all-gather.3.cloned.1.call-done = bf16[512,4096]{1,0:T(8,128)(2,1)} async-done(((bf16[512,1024]{1,0:T(8,128)(2,1)}), bf16[512,4096]{1,0:T(8,128)(2,1)}) %all-gather.3.cloned.1.call-update) | async-done | bytes 4194320 | tf_op jit(solution)/shard_map/all_gather | solution.py:40
  102.1 2.9 fusion.87
  105.1 0.1 add_dynamic-update-slice_fusion
  105.2 1.1 convert_element_type.66
  106.3 0.0 all-gather.5.cloned.1.call-start
  106.4 0.1 copy.27
  106.5 0.2 reduce-window.8
  106.7 0.1 add_reduce_fusion
  106.8 34.4 %all-reduce.2.cloned.1.call-done = bf16[128,4096]{1,0:T(8,128)(2,1)} async-done(((bf16[128,4096]{1,0:T(8,128)(2,1)}), bf16[128,4096]{1,0:T(8,128)(2,1)}) %all-reduce.2.cloned.1.call-update) | async-done | bytes 1048592 | tf_op jit(solution)/shard_map/psum | solution.py:67
  141.2 1.5 multiply_reduce_fusion
  142.7 2.4 convolution_convert_fusion.1
  145.2 0.2 reduce-scatter.3.cloned.1.call-start
  145.4 46.2 %all-gather.5.cloned.1.call-done = bf16[256,4096]{1,0:T(8,128)(2,1)} async-done(((bf16[64,4096]{1,0:T(8,128)(2,1)}), bf16[256,4096]{1,0:T(8,128)(2,1)}) %all-gather.5.cloned.1.call-update) | async-done | bytes 2097168 | tf_op jit(solution)/shard_map/all_gather | solution.py:93
  191.7 8.5 %fusion.5 = f32[256,1792]{1,0:T(8,128)S(1)} fusion(bf16[256,4096]{1,0:T(8,128)(2,1)} %all-gather.5.cloned.1.call-done, bf16[1,4096,1792]{2,1,0:T(8,128)(2,1)} %param.19), kind=kOutput, calls=%fused_computation.5 | convolution fusion | flops 3758096384 | bytes 18612224 | tf_op jit(solution)/shard_map/dot_general | solution.py:94
  200.3 9.4 %fusion.14 = bf16[256,1792]{1,0:T(8,128)(2,1)S(1)} fusion(bf16[256,4096]{1,0:T(8,128)(2,1)S(1)} %copy-done.6, bf16[1,4096,1792]{2,1,0:T(8,128)(2,1)} %param.20, f32[256,1792]{1,0:T(8,128)S(1)} %fusion.5), kind=kOutput, calls=%fused_computation.14 | convolution fusion | flops 3760848896 | bytes 19529728 | tf_op jit(solution)/shard_map/dot_general | solution.py:95
  209.7 5.2 %fusion.7 = bf16[256,4096]{1,0:T(8,128)(2,1)} fusion(bf16[256,1792]{1,0:T(8,128)(2,1)S(1)} %fusion.14, bf16[1,1792,4096]{2,1,0:T(8,128)(2,1)S(1)} %bitcast.89), kind=kOutput, calls=%fused_computation.7 | convolution fusion | flops 3759144960 | bytes 17694720 | tf_op jit(solution)/shard_map/dot_general | solution.py:97
  214.9 0.0 reduce-scatter.5.cloned.1.call-start
  215.0 1.0 fusion.40
  216.1 0.1 convolution_bitcast_fusion
  216.2 41.5 %reduce-scatter.3.cloned.1.call-done = bf16[64,4096]{1,0:T(8,128)(2,1)} async-done(((bf16[256,4096]{1,0:T(8,128)(2,1)}), bf16[64,4096]{1,0:T(8,128)(2,1)}) %reduce-scatter.3.cloned.1.call-update) | async-done | bytes 524304 | tf_op jit(solution)/shard_map/reduce_scatter | solution.py:98
  257.7 3.1 %convolution_convert_fusion = bf16[128,4096]{1,0:T(8,128)(2,1)} fusion(bf16[64,4096]{1,0:T(8,128)(2,1)} %reduce-scatter.3.cloned.1.call-done, f32[64]{0:T(128)S(1)} %convolution_bitcast_fusion, s32[128]{0:T(128)S(1)} %add_reduce_fusion, pred[128]{0:T(512)(128)(4,1)S(1)} %fusion.81), kind=kOutput, calls=%fused_computation.8 | convolution fusion | flops 403202048 | bytes 1573760 | tf_op jit(solution)/shard_map/dot_general | solution.py:105
  260.7 0.2 convert_element_type.67
  261.0 24.1 %reduce-scatter.5.cloned.1.call-done = bf16[32,4096]{1,0:T(8,128)(2,1)} async-done(((bf16[128,4096]{1,0:T(8,128)(2,1)}), bf16[32,4096]{1,0:T(8,128)(2,1)}) %reduce-scatter.5.cloned.1.call-update) | async-done | bytes 262160 | tf_op jit(solution)/shard_map/reduce_scatter | solution.py:106
  285.1 1.7 add_convert_fusion
  (35 shorter events, 0.3 us)
Async XLA Ops:
  6.5 44.8 %copy-start = (bf16[128,512]{1,0:T(8,128)(2,1)S(1)}, bf16[128,512]{1,0:T(8,128)(2,1)}, u32[]{:S(2)}) copy-start(bf16[128,512]{1,0:T(8,128)(2,1)} %param.11) | copy-start | bytes 393220
  6.5 95.6 %all-gather.3.cloned.1.call-start = ((), (), s32[]{:S(2)}) async-start(), calls=%async_computation.2 | async-start | bytes 5242880 | tf_op jit(solution)/shard_map/all_gather | solution.py:40
  7.3 134.0 %all-reduce.2.cloned.1.call-start = ((), (), s32[]{:S(2)}) async-start(), calls=%async_computation.3 | async-start | bytes 2097152 | tf_op jit(solution)/shard_map/psum | solution.py:67
  55.1 50.0 %copy-start.3 = (bf16[128,1024]{1,0:T(8,128)(2,1)S(1)}, bf16[128,1024]{1,0:T(8,128)(2,1)}, u32[]{:S(2)}) copy-start(bf16[128,1024]{1,0:T(8,128)(2,1)} %param.15) | copy-start | bytes 786436
  105.1 1.3 copy-start.5
  106.3 85.3 %all-gather.5.cloned.1.call-start = ((), (), s32[]{:S(2)}) async-start(), calls=%async_computation.4 | async-start | bytes 2621440 | tf_op jit(solution)/shard_map/all_gather | solution.py:93
  145.2 112.5 %reduce-scatter.3.cloned.1.call-start = ((), (), s32[]{:S(2)}) async-start(), calls=%async_computation.5 | async-start | bytes 2621440 | tf_op jit(solution)/shard_map/reduce_scatter | solution.py:98
  191.7 8.6 %copy-start.6 = (bf16[256,4096]{1,0:T(8,128)(2,1)S(1)}, bf16[256,4096]{1,0:T(8,128)(2,1)}, u32[]{:S(2)}) copy-start(bf16[256,4096]{1,0:T(8,128)(2,1)} %all-gather.5.cloned.1.call-done) | copy-start | bytes 6291460
  191.7 18.0 %slice-start = ((s8[14680064]{0:T(1024)(128)(4,1)}), s8[4194304]{0:T(1024)(128)(4,1)S(1)}, s32[]{:S(2)}) async-start(s8[14680064]{0:T(1024)(128)(4,1)} %bitcast.88), calls=%async_computation.7 | async-start | bytes 8388608
  191.7 18.0 %slice-start.1 = ((s8[14680064]{0:T(1024)(128)(4,1)}), s8[4194304]{0:T(1024)(128)(4,1)S(1)}, s32[]{:S(2)}) async-start(s8[14680064]{0:T(1024)(128)(4,1)} %bitcast.88), calls=%async_computation.8 | async-start | bytes 8388608
  200.2 9.5 %slice-start.2 = ((s8[14680064]{0:T(1024)(128)(4,1)}), s8[4194304]{0:T(1024)(128)(4,1)S(1)}, s32[]{:S(2)}) async-start(s8[14680064]{0:T(1024)(128)(4,1)} %bitcast.88), calls=%async_computation.9 | async-start | bytes 8388608
  200.2 9.5 %slice-start.3 = ((s8[14680064]{0:T(1024)(128)(4,1)}), s8[2097152]{0:T(1024)(128)(4,1)S(1)}, s32[]{:S(2)}) async-start(s8[14680064]{0:T(1024)(128)(4,1)} %bitcast.88), calls=%async_computation.10 | async-start | bytes 4194304
  209.7 5.3 %copy-start.2 = (bf16[128,4096]{1,0:T(8,128)(2,1)S(1)}, bf16[128,4096]{1,0:T(8,128)(2,1)}, u32[]{:S(2)}) copy-start(bf16[128,4096]{1,0:T(8,128)(2,1)} %all-reduce.2.cloned.1.call-done) | copy-start | bytes 3145732
  209.7 5.3 %copy-start.4 = (f32[4096,4]{0,1:T(4,128)S(1)}, f32[4096,4]{0,1:T(4,128)}, u32[]{:S(2)}) copy-start(f32[4096,4]{0,1:T(4,128)} %param.16) | copy-start | bytes 196612
  214.9 71.9 %copy-start.1 = (bf16[128,512]{1,0:T(8,128)(2,1)S(1)}, bf16[128,512]{1,0:T(8,128)(2,1)}, u32[]{:S(2)}) copy-start(bf16[128,512]{1,0:T(8,128)(2,1)} %param.11) | copy-start | bytes 393220
  214.9 70.2 %reduce-scatter.5.cloned.1.call-start = ((), (), s32[]{:S(2)}) async-start(), calls=%async_computation.6 | async-start | bytes 1310720 | tf_op jit(solution)/shard_map/reduce_scatter | solution.py:106
Sparse Core Ops, SparseCore 0:
  8.9 93.1 all-gather.2
  106.4 34.7 all-reduce.1
  145.3 46.3 all-gather.4
  215.0 42.5 reduce-scatter.2
  260.9 24.1 reduce-scatter.4
where the time goes:
time: 294 us; the launch traced here: 293 us
  waiting for transfers between devices  194 us (66%)
  blocking collectives  42.2 us (14%)
  matrix products  36.3 us (12%)
  between operations  13.4 us (5%)
  other arithmetic  5.87 us (2%)
    all_gather x1, waiting for transfers between devices, local(): lax.all_gather(out_weight, 'ctx', axis=1, tiled=True)  47 us
    all_gather x1, waiting for transfers between devices, local(): piece = lax.all_gather(local_rows, 'ctx', axis=0, tiled=True)  46.2 us
    reduce_scatter x1, waiting for transfers between devices, local(): lax.psum_scatter(partial_rows.astype(jnp.float32).astype(jnp.bfloat16), '...  41.5 us
    psum x1, waiting for transfers between devices, local(): lax.psum(partial_value.astype(jnp.bfloat16), 'exp').astype(jnp.float32)  34.4 us
    reduce_scatter x1, waiting for transfers between devices, local(): lax.psum_scatter(contribution.astype(jnp.bfloat16), 'exp', scatter_dimens...  24.1 us
    all_gather x1, blocking collectives, local(): lax.all_gather(keys, 'ctx', axis=0, tiled=True)  22.7 us
    all_gather x1, blocking collectives, local(): lax.all_gather(values, 'ctx', axis=0, tiled=True)  19.5 us
    dot_general x1, matrix products, local(): up_proj = jnp.dot(piece, up_here, preferred_element_type=jnp.float32)  9.4 us
  transfers between devices with their start and end apart: 5, of which 5 were waited for; matrix products, arithmetic and copies ran while one was open for 3% of the time, Pallas kernels for 0%

commit v1 on v0

v1 whole, which is shorter than its diff:
```python
import math

import jax
import jax.numpy as jnp
from jax import lax
from jax.sharding import PartitionSpec as P


def rotation(count, step):
    return [(i, (i + step) % count) for i in range(count)]


def gather_rotated(block, count):
    return [block] + [lax.ppermute(block, "ctx", rotation(count, k)) for k in range(1, count)]


def picker_of(named, capacity):
    slot = jnp.cumsum(named.astype(jnp.int32)) - 1
    places = jnp.arange(capacity, dtype=jnp.int32)
    return (slot[None, :] == places[:, None]) & named[None, :]


def local(
    queries,
    keys,
    values,
    out_weight,
    residual,
    router,
    routes,
    order,
    expert_gate,
    expert_up,
    expert_down,
):
    bf16, f32 = jnp.bfloat16, jnp.float32
    tok = queries.shape[0]
    head_dim = keys.shape[1]
    heads = queries.shape[1] // head_dim
    span = keys.shape[0]
    ctx_count = lax.axis_size("ctx")
    exp_count = lax.axis_size("exp")
    c = lax.axis_index("ctx")
    e = lax.axis_index("exp")
    width = out_weight.shape[1]
    features = width * ctx_count
    capacity = tok // 2
    per_share = ctx_count // exp_count
    levels = exp_count.bit_length() - 1

    routes_all = gather_rotated(routes, ctx_count)
    routes_stacked = jnp.stack(routes_all)
    pieces = residual.reshape(tok, per_share, width)
    residual_blocks = []
    for t in range(per_share):
        perm = []
        for ci in range(ctx_count):
            for ei in range(exp_count):
                to = (ei * per_share + (t + ci) % per_share, ci // per_share)
                perm.append((ci * exp_count + ei, to[0] * exp_count + to[1]))
        piece = lax.dynamic_index_in_dim(pieces, (t + c) % per_share, 1, keepdims=False)
        residual_blocks.append(lax.ppermute(piece, ("ctx", "exp"), perm))
    if per_share > 1:
        stacked = jnp.stack(residual_blocks)
        residual_blocks = [
            lax.dynamic_index_in_dim(stacked, (c - j) % per_share, 0, keepdims=False)
            for j in range(per_share)
        ]

    visible_end = span * ctx_count - tok * ctx_count + order
    keys_all = jnp.concatenate(gather_rotated(keys, ctx_count))
    values_all = jnp.concatenate(gather_rotated(values, ctx_count))
    positions = jnp.concatenate(
        [((c - k) % ctx_count) * span + jnp.arange(span, dtype=jnp.int32) for k in range(ctx_count)]
    )
    query_blocks = queries.reshape(tok, heads, head_dim)
    score = jnp.einsum(
        "tqd,jd->qtj", query_blocks, keys_all, preferred_element_type=f32
    ) * (1.0 / math.sqrt(head_dim))
    visible = positions[None, None, :] <= visible_end[None, :, None]
    score = jnp.where(visible, score, -1e30)
    highest = jnp.max(score, axis=2, keepdims=True)
    weight = jnp.where(visible, jnp.exp(score - highest), 0.0)
    total = jnp.sum(weight, axis=2)
    summed = jnp.einsum(
        "qtj,jd->tqd", weight.astype(bf16), values_all, preferred_element_type=f32
    )
    attended = (summed / total.T[:, :, None]).astype(bf16).reshape(tok, heads * head_dim)

    attended_all = jnp.stack(gather_rotated(attended, ctx_count))

    def share_of(index):
        rows = [
            lax.dynamic_index_in_dim(
                attended_all, (c - (index * per_share + j)) % ctx_count, 0, keepdims=False
            )
            for j in range(per_share)
        ]
        return jnp.concatenate(rows)

    low = e % 2
    half = exp_count // 2
    away = jnp.concatenate([share_of(1 - low + 2 * i) for i in range(half)])
    near = jnp.concatenate([share_of(low + 2 * i) for i in range(half)])
    sent = jnp.dot(away, out_weight, preferred_element_type=f32).astype(bf16)
    came = lax.ppermute(sent, "exp", [(i, i ^ 1) for i in range(exp_count)])
    acc = jnp.dot(near, out_weight, preferred_element_type=f32) + came.astype(f32)
    rows = per_share * tok
    for level in range(1, levels):
        bit = (e >> level) % 2
        half = half // 2
        acc = acc.reshape(half, 2, rows, width)
        sent = lax.dynamic_index_in_dim(acc, 1 - bit, 1, keepdims=False).astype(bf16)
        came = lax.ppermute(sent, "exp", [(i, i ^ (1 << level)) for i in range(exp_count)])
        acc = lax.dynamic_index_in_dim(acc, bit, 1, keepdims=False) + came.astype(f32)
    stream = acc.reshape(per_share, tok, width) + jnp.stack(residual_blocks).astype(f32)
    stream = stream.astype(bf16)

    pickers = []
    for k in range(exp_count):
        for j in range(per_share):
            block = lax.dynamic_index_in_dim(
                routes_stacked, (c - (e * per_share + j)) % ctx_count, 0, keepdims=False
            )
            pickers.append(picker_of(jnp.any(block == (e ^ k), axis=1), capacity).astype(bf16))
    turns = sorted(range(ctx_count), key=lambda k: min(k, ctx_count - k))
    chunks = {}
    for k in turns:
        chunk = lax.ppermute(stream, "ctx", rotation(ctx_count, k)) if k else stream
        pieces = []
        for m in range(exp_count):
            picked = [
                jnp.dot(pickers[m * per_share + j], chunk[j], preferred_element_type=f32)
                for j in range(per_share)
            ]
            piece = jnp.concatenate(picked).astype(bf16)
            if m:
                piece = lax.ppermute(piece, "exp", [(i, i ^ m) for i in range(exp_count)])
            pieces.append(piece)
        chunks[k] = jnp.concatenate(pieces)

    gate_here, up_here, down_here = expert_gate[0], expert_up[0], expert_down[0]
    gate_proj = up_proj = squares = logits = 0.0
    for k in turns:
        chunk = chunks[k]
        start = ((c - k) % ctx_count) * width
        gate_rows = lax.dynamic_slice_in_dim(gate_here, start, width, 0)
        up_rows = lax.dynamic_slice_in_dim(up_here, start, width, 0)
        router_rows = lax.dynamic_slice_in_dim(router, start, width, 0)
        gate_proj += jnp.dot(chunk, gate_rows, preferred_element_type=f32)
        up_proj += jnp.dot(chunk, up_rows, preferred_element_type=f32)
        squares += jnp.sum(jnp.square(chunk.astype(f32)), axis=1, keepdims=True)
        logits += jnp.dot(chunk.astype(f32), router_rows, precision=lax.Precision.HIGHEST)
        gate_proj, up_proj, squares, logits = lax.optimization_barrier(
            (gate_proj, up_proj, squares, logits)
        )
    scale = lax.rsqrt(squares / features + 1e-05)
    act = (jax.nn.silu(gate_proj * scale) * (up_proj * scale)).astype(bf16)
    logits = logits * scale

    def rows_of(array, block):
        slot = ((e ^ (block // per_share)) * per_share + block % per_share) * capacity
        return lax.dynamic_slice_in_dim(array, slot, capacity, 0)

    own_rows = jnp.stack([rows_of(chunks[k], c) for k in range(ctx_count)])
    stream_rows = jnp.concatenate(
        [
            lax.dynamic_index_in_dim(own_rows, (c - a) % ctx_count, 0, keepdims=False)
            for a in range(ctx_count)
        ],
        axis=1,
    )

    experts = jnp.arange(router.shape[1], dtype=jnp.int32)
    mine = (experts == e).astype(f32)[None, :]
    own_share = tok // exp_count

    def contribution(k):
        block = (c + k) % ctx_count
        block_routes = routes_all[-k % ctx_count]
        picker = picker_of(jnp.any(block_routes == e, axis=1), capacity).astype(f32)
        other = jnp.sum(jnp.where(block_routes == e, 0, block_routes), axis=1)
        other_slot = jnp.dot(picker, (other[:, None] == experts[None, :]).astype(f32))
        gate = jax.nn.sigmoid(
            jnp.sum(rows_of(logits, block) * (mine - other_slot), axis=1, keepdims=True)
        )
        gives = gate * jnp.dot(rows_of(act, block), down_here, preferred_element_type=f32)
        if k == 0:
            gives += 0.5 * stream_rows.astype(f32)
        gives = gives.astype(bf16)
        spread = picker.T.astype(bf16).reshape(exp_count // 2, 2, own_share, capacity)

        def spread_rows(bit):
            pick = lax.dynamic_index_in_dim(spread, bit, 1, keepdims=False)
            return jnp.dot(
                pick.reshape(tok // 2, capacity), gives, preferred_element_type=f32
            )

        sent = spread_rows(1 - low).astype(bf16)
        came = lax.ppermute(sent, "exp", [(i, i ^ 1) for i in range(exp_count)])
        acc = spread_rows(low) + came.astype(f32)
        half = exp_count // 2
        for level in range(1, levels):
            bit = (e >> level) % 2
            half = half // 2
            acc = acc.reshape(half, 2, own_share, features)
            sent = lax.dynamic_index_in_dim(acc, 1 - bit, 1, keepdims=False).astype(bf16)
            came = lax.ppermute(sent, "exp", [(i, i ^ (1 << level)) for i in range(exp_count)])
            acc = lax.dynamic_index_in_dim(acc, bit, 1, keepdims=False) + came.astype(f32)
        return acc.reshape(own_share, features)

    output = 0.0
    for k in reversed(turns):
        part = contribution(k)
        if k:
            part = lax.ppermute(part.astype(bf16), "ctx", rotation(ctx_count, k)).astype(f32)
        output += part
    return output.astype(bf16)


def solution(mesh):
    return jax.shard_map(
        local,
        mesh=mesh,
        in_specs=(
            P(("groups", "ctx"), "exp"),
            P(("groups", "ctx"), "exp"),
            P(("groups", "ctx"), "exp"),
            P("exp", "ctx"),
            P(("groups", "ctx"), "exp"),
            P(),
            P(("groups", "ctx"), None),
            P(("groups", "ctx")),
            P("exp", None, "ctx"),
            P("exp", None, "ctx"),
            P("exp", "ctx", None),
        ),
        out_specs=P(("groups", "ctx", "exp"), None),
        check_vma=False,
    )
```

time: 294 us -> 167 us (0.57)
  waiting for transfers between devices: 194 us -> 50.4 us
  starting transfers between devices: 0.35 us -> 45.7 us
  blocking collectives: 42.2 us -> 0 us
  between operations: 13.4 us -> 1.38 us
  matrix products: 36.3 us -> 47.3 us
  other arithmetic: 5.87 us -> 16.6 us
  local copies, waits for them, and re-layouts: 1.18 us -> 5.16 us
    all_gather x2 -> x0, waiting for transfers between devices: 93.2 us -> none  [the longest x1 47 us: local(): lax.all_gather(out_weight, 'ctx', axis=1, tiled=True)]
    reduce_scatter x2 -> x0, waiting for transfers between devices: 65.6 us -> none  [the longest x1 41.5 us: local(): lax.psum_scatter(partial_rows.astype(jnp.float32).astype(jnp.bfloat16), '...]
    ppermute x0 -> x41, waiting for transfers between devices: none -> 50.4 us  [the longest x4 17.5 us: contribution(): lax.ppermute(sent, 'exp', [(i, i ^ 1 << level) for i in range(exp_count)])]
    ppermute x0 -> x41, starting transfers between devices: none -> 45.7 us  [the longest x12 21.8 us: gather_rotated(): lax.ppermute(block, 'ctx', rotation(count, k))]
    all_gather x2 -> x0, blocking collectives: 42.2 us -> none  [the longest x1 22.7 us: local(): lax.all_gather(keys, 'ctx', axis=0, tiled=True)]
    psum x1 -> x0, waiting for transfers between devices: 34.4 us -> none  [local(): lax.psum(partial_value.astype(jnp.bfloat16), 'exp').astype(jnp.float32)]
    dot_general x9 -> x47, matrix products: 34.5 us -> 43 us  [the longest x4 13.2 us: local(): gate_proj += jnp.dot(chunk, gate_rows, preferred_element_type=f32)]
  transfers between devices with their start and end apart: 5 -> 41, of which waited for: 5 -> 14; matrix products, arithmetic and copies ran while one was open for 3% -> 34% of each run, Pallas kernels for 0% -> 0%
where the time goes in v1:
time: 167 us
  waiting for transfers between devices  50.4 us (30%)
  matrix products  47.3 us (28%)
  starting transfers between devices  45.7 us (27%)
  other arithmetic  16.6 us (10%)
  local copies, waits for them, and re-layouts  5.16 us (3%)
    ppermute x12, starting transfers between devices, gather_rotated(): lax.ppermute(block, 'ctx', rotation(count, k))  21.8 us
    ppermute x4, waiting for transfers between devices, contribution(): lax.ppermute(sent, 'exp', [(i, i ^ 1 << level) for i in range(exp_count)])  17.5 us
    dot_general x4, matrix products, local(): gate_proj += jnp.dot(chunk, gate_rows, preferred_element_type=f32)  13.2 us
    ppermute x12, waiting for transfers between devices, gather_rotated(): lax.ppermute(block, 'ctx', rotation(count, k))  13 us
    dot_general x4, matrix products, contribution(): jnp.dot(rows_of(act, block), down_here, preferred_element_type=f32)  10.7 us
    ppermute x12, starting transfers between devices, local(): piece = lax.ppermute(piece, 'exp', [(i, i ^ m) for i in range(exp_count)])  9.98 us
    ppermute x3, waiting for transfers between devices, local(): lax.ppermute(part.astype(bf16), 'ctx', rotation(ctx_count, k)).astype(f32)  7.2 us
    dot_general x4, matrix products, local(): up_proj += jnp.dot(chunk, up_rows, preferred_element_type=f32)  6.79 us
  transfers between devices with their start and end apart: 41, of which 14 were waited for; matrix products, arithmetic and copies ran while one was open for 34% of the time, Pallas kernels for 0%

profile of v1, /device:TPU:0, one launch (start us, length us, event | category | flops | bytes accessed | tf_op | source)
XLA Modules:
  0.0 166.6 jit_solution(7870716214819400283)
XLA Ops:
  0.0 3.0 %collective-permute-start.6 = (bf16[512,128]{1,0:T(8,128)(2,1)}, bf16[512,128]{1,0:T(8,128)(2,1)S(1)}, u32[]{:S(2)}, u32[]{:S(2)}) collective-permute-start(bf16[512,128]{1,0:T(8,128)(2,1)} %param.12), channel_id=1, source_target_pairs={{0,4},{4,8},{8,12},{12,0},{1,5},{5,9},{9,13},{13,1},{2,6},{6,10},{... | collective-permute-start | bytes 393224 | tf_op jit(solution)/shard_map/ppermute | solution.py:14
  3.0 2.6 %collective-permute-start.7 = (bf16[512,128]{1,0:T(8,128)(2,1)}, bf16[512,128]{1,0:T(8,128)(2,1)S(1)}, u32[]{:S(2)}, u32[]{:S(2)}) collective-permute-start(bf16[512,128]{1,0:T(8,128)(2,1)} %param.12), channel_id=1, source_target_pairs={{0,8},{4,12},{8,0},{12,4},{1,9},{5,13},{9,1},{13,5},{2,10},{6,14},... | collective-permute-start | bytes 393224 | tf_op jit(solution)/shard_map/ppermute | solution.py:14
  13.8 3.5 %collective-permute-done = s32[128,2]{0,1:T(2,128)S(1)} collective-permute-done((s32[128,2]{0,1:T(2,128)}, s32[128,2]{0,1:T(2,128)S(1)}, u32[]{:S(2)}, u32[]{:S(2)}) %collective-permute-start) | collective-permute-done | bytes 1056 | tf_op jit(solution)/shard_map/ppermute | solution.py:14
  17.2 1.7 %collective-permute-start.2 = (s32[128,2]{0,1:T(2,128)}, s32[128,2]{0,1:T(2,128)S(1)}, u32[]{:S(2)}, u32[]{:S(2)}) collective-permute-start(s32[128,2]{0,1:T(2,128)} %param.17), channel_id=1, source_target_pairs={{0,12},{4,0},{8,4},{12,8},{1,13},{5,1},{9,5},{13,9},{2,14},{6,2},{... | collective-permute-start | bytes 3080 | tf_op jit(solution)/shard_map/ppermute | solution.py:14
  19.6 1.4 collective-permute-done.2
  25.8 3.0 %collective-permute-start.5 = (bf16[512,128]{0,1:T(8,128)(2,1)S(1)}, bf16[512,128]{0,1:T(8,128)(2,1)S(1)}, u32[]{:S(2)}, u32[]{:S(2)}) collective-permute-start(bf16[512,128]{0,1:T(8,128)(2,1)S(1)} %copy.26), channel_id=1, source_target_pairs={{0,12},{4,0},{8,4},{12,8},{1,13},{5,1},{9,5},{13,9},{2,14},{6,2},{... | collective-permute-start | bytes 393224 | tf_op jit(solution)/shard_map/ppermute | solution.py:14
  28.9 1.6 collective-permute-start.14
  30.5 4.3 %fusion.270 = (f32[4,128]{1,0:T(4,128)S(1)}, bf16[4,128,2048]{1,2,0:T(8,128)(2,1)}) fusion(pred[128,2048]{0,1:T(8,128)(4,1)S(1)} %broadcast_compare_fusion, bf16[512,128]{1,0:T(8,128)(2,1)S(1)} %collective-permute-done.8, bf16[512,128]{1,0:T(8,128)(2,1)S(1)} %collective-permute-done.7, bf16[512,128]{1,0:T(8,128)(2,1)S(1)} %collective-permute-done.6, ...), kind=kOutput, calls=%fused_computation.362 | convolution fusion | flops 276826112 | bytes 3016704 | tf_op jit(solution)/shard_map/sub | solution.py:83
  34.8 2.0 %fusion.90 = bf16[128,4,128]{0,2,1:T(8,128)(2,1)S(1)} fusion(bf16[4,128,2048]{1,2,0:T(8,128)(2,1)} %get-tuple-element.74, bf16[512,128]{0,1:T(8,128)(2,1)S(1)} %collective-permute-done.5, bf16[512,128]{0,1:T(8,128)(2,1)S(1)} %collective-permute-done.4, bf16[512,128]{0,1:T(8,128)(2,1)S(1)} %collective-permute-done.3, bf16[512,128]{0,1:T(8,128)(2,1)S(1)} %copy.26, ...), kind=kOutput, calls=%fused_computation.64 | convolution fusion | flops 270663680 | bytes 2754560 | tf_op jit(solution)/shard_map/qtj,jd->tqd/dot_general | solution.py:85
  36.9 6.1 %collective-permute-start.9 = (bf16[128,512]{0,1:T(8,128)(2,1)S(1)}, bf16[128,512]{0,1:T(8,128)(2,1)S(1)}, u32[]{:S(2)}, u32[]{:S(2)}) collective-permute-start(bf16[128,512]{0,1:T(8,128)(2,1)S(1)} %bitcast.307), channel_id=1, source_target_pairs={{0,4},{4,8},{8,12},{12,0},{1,5},{5,9},{9,13},{13,1},{2,6},{6,10},{... | collective-permute-start | bytes 393224 | tf_op jit(solution)/shard_map/ppermute | solution.py:14
  42.9 2.4 %collective-permute-start.11 = (bf16[128,512]{0,1:T(8,128)(2,1)S(1)}, bf16[128,512]{0,1:T(8,128)(2,1)S(1)}, u32[]{:S(2)}, u32[]{:S(2)}) collective-permute-start(bf16[128,512]{0,1:T(8,128)(2,1)S(1)} %bitcast.309), channel_id=1, source_target_pairs={{0,12},{4,0},{8,4},{12,8},{1,13},{5,1},{9,5},{13,9},{2,14},{6,2},{... | collective-permute-start | bytes 393224 | tf_op jit(solution)/shard_map/ppermute | solution.py:14
  46.3 8.0 %collective-permute-done.10 = bf16[128,512]{0,1:T(8,128)(2,1)S(1)} collective-permute-done((bf16[128,512]{0,1:T(8,128)(2,1)S(1)}, bf16[128,512]{0,1:T(8,128)(2,1)S(1)}, u32[]{:S(2)}, u32[]{:S(2)}) %collective-permute-start.10) | collective-permute-done | bytes 131104 | tf_op jit(solution)/shard_map/ppermute | solution.py:14
  55.0 1.4 fusion.256
  61.7 6.0 %collective-permute-done.13 = bf16[1,128,1024]{2,1,0:T(8,128)(2,1)S(1)} collective-permute-done((bf16[1,128,1024]{2,1,0:T(8,128)(2,1)S(1)}, bf16[1,128,1024]{2,1,0:T(8,128)(2,1)S(1)}, u32[]{:S(2)}, u32[]{:S(2)}) %collective-permute-start.13) | collective-permute-done | bytes 262176 | tf_op jit(solution)/shard_map/ppermute | solution.py:114
  68.9 2.6 %collective-permute-start.18 = (bf16[1,128,1024]{2,1,0:T(8,128)(2,1)S(1)}, bf16[1,128,1024]{2,1,0:T(8,128)(2,1)S(1)}, u32[]{:S(2)}, u32[]{:S(2)}) collective-permute-start(bf16[1,128,1024]{2,1,0:T(8,128)(2,1)S(1)} %fusion.109), channel_id=1, source_target_pairs={{0,4},{4,8},{8,12},{12,0},{1,5},{5,9},{9,13},{13,1},{2,6},{6,10},{... | collective-permute-start | bytes 786440 | tf_op jit(solution)/shard_map/ppermute | solution.py:129
  77.4 3.5 %collective-permute-done.16 = bf16[64,1024]{1,0:T(8,128)(2,1)S(1)} collective-permute-done((bf16[64,1024]{1,0:T(8,128)(2,1)S(1)}, bf16[64,1024]{1,0:T(8,128)(2,1)S(1)}, u32[]{:S(2)}, u32[]{:S(2)}) %collective-permute-start.16) | collective-permute-done | bytes 131104 | tf_op jit(solution)/shard_map/ppermute | solution.py:138
  80.9 2.0 %collective-permute-done.17 = bf16[64,1024]{1,0:T(8,128)(2,1)S(1)} collective-permute-done((bf16[64,1024]{1,0:T(8,128)(2,1)S(1)}, bf16[64,1024]{1,0:T(8,128)(2,1)S(1)}, u32[]{:S(2)}, u32[]{:S(2)}) %collective-permute-start.17) | collective-permute-done | bytes 131104 | tf_op jit(solution)/shard_map/ppermute | solution.py:138
  83.1 3.3 %fusion.49 = f32[256,1792]{1,0:T(8,128)S(1)} fusion(bf16[256,1024]{1,0:T(8,128)(2,1)S(1)} %get-tuple-element.48, bf16[1,4096,1792]{2,1,0:T(8,128)(2,1)} %param.20, s32[]{:T(128)S(6)} %select_n.277), kind=kOutput, calls=%fused_computation.37 | convolution fusion | flops 939524096 | bytes 6029316 | tf_op jit(solution)/shard_map/dot_general | solution.py:151
  86.4 3.3 %fusion.51 = f32[256,1792]{1,0:T(8,128)S(1)} fusion(bf16[256,1024]{1,0:T(8,128)(2,1)S(1)} %get-tuple-element.48, bf16[1,4096,1792]{2,1,0:T(8,128)(2,1)} %param.19, s32[]{:T(128)S(6)} %select_n.277), kind=kOutput, calls=%fused_computation.39 | convolution fusion | flops 939524096 | bytes 6029316 | tf_op jit(solution)/shard_map/dot_general | solution.py:150
  101.4 3.2 %fusion.61 = f32[256,1792]{1,0:T(8,128)S(1)} fusion(f32[256,1792]{1,0:T(8,128)S(1)} %fusion.51, bf16[256,1024]{1,0:T(8,128)(2,1)S(1)} %get-tuple-element.46, bf16[1,4096,1792]{2,1,0:T(8,128)(2,1)} %param.19, s32[]{:T(128)S(6)} %select_n.278), kind=kOutput, calls=%fused_computation.49 | convolution fusion | flops 939982848 | bytes 7864324 | tf_op jit(solution)/shard_map/dot_general | solution.py:150
  105.2 1.7 %collective-permute-start.29 = (bf16[64,1024]{1,0:T(8,128)(2,1)S(1)}, bf16[64,1024]{1,0:T(8,128)(2,1)S(1)}, u32[]{:S(2)}, u32[]{:S(2)}) collective-permute-start(bf16[64,1024]{1,0:T(8,128)(2,1)S(1)} %convolution_convert_fusion.5), channel_id=1, source_target_pairs={{0,3},{1,2},{2,1},{3,0},{4,7},{5,6},{6,5},{7,4},{8,11},{9,10},{10,... | collective-permute-start | bytes 393224 | tf_op jit(solution)/shard_map/ppermute | solution.py:138
  108.8 3.3 %fusion.67 = f32[256,1792]{1,0:T(8,128)S(1)} fusion(f32[256,1792]{1,0:T(8,128)S(1)} %fusion.61, bf16[256,1024]{1,0:T(8,128)(2,1)S(1)} %get-tuple-element.44, bf16[1,4096,1792]{2,1,0:T(8,128)(2,1)} %param.19, s32[]{:T(128)S(6)} %select_n.279), kind=kOutput, calls=%fused_computation.51 | convolution fusion | flops 939982848 | bytes 7864324 | tf_op jit(solution)/shard_map/dot_general | solution.py:150
  114.2 3.3 %fusion.73 = f32[256,1792]{1,0:T(8,128)S(1)} fusion(f32[256,1792]{1,0:T(8,128)S(1)} %fusion.67, bf16[256,1024]{1,0:T(8,128)(2,1)S(1)} %get-tuple-element.42, bf16[1,4096,1792]{2,1,0:T(8,128)(2,1)} %param.19, s32[]{:T(128)S(6)} %select_n.280), kind=kOutput, calls=%fused_computation.53 | convolution fusion | flops 939982848 | bytes 7864324 | tf_op jit(solution)/shard_map/dot_general | solution.py:150
  118.8 2.7 %fusion.33 = bf16[64,4096]{1,0:T(8,128)(2,1)S(1)} fusion(bf16[1,1792,4096]{2,1,0:T(8,128)(2,1)S(1)} %bitcast.294, f32[64]{0:T(128)S(1)} %add_divide_fusion.3, bf16[256,1792]{1,0:T(8,128)(2,1)S(1)} %multiply_convert_fusion, s32[]{:T(128)S(6)} %select_n.282), kind=kOutput, calls=%fused_computation.21 | convolution fusion | flops 940048384 | bytes 15434244 | tf_op jit(solution)/shard_map/dot_general | solution.py:187
  122.2 2.7 %fusion.30 = bf16[64,4096]{1,0:T(8,128)(2,1)S(1)} fusion(bf16[1,1792,4096]{2,1,0:T(8,128)(2,1)S(1)} %bitcast.294, f32[64]{0:T(128)S(1)} %add_divide_fusion.2, bf16[256,1792]{1,0:T(8,128)(2,1)S(1)} %multiply_convert_fusion, s32[]{:T(128)S(6)} %select_n.286), kind=kOutput, calls=%fused_computation.20 | convolution fusion | flops 940048384 | bytes 15434244 | tf_op jit(solution)/shard_map/dot_general | solution.py:187
  126.0 2.7 %fusion.27 = bf16[64,4096]{1,0:T(8,128)(2,1)S(1)} fusion(bf16[1,1792,4096]{2,1,0:T(8,128)(2,1)S(1)} %bitcast.294, f32[64]{0:T(128)S(1)} %add_divide_fusion.1, bf16[256,1792]{1,0:T(8,128)(2,1)S(1)} %multiply_convert_fusion, s32[]{:T(128)S(6)} %select_n.289), kind=kOutput, calls=%fused_computation.19 | convolution fusion | flops 940048384 | bytes 15434244 | tf_op jit(solution)/shard_map/dot_general | solution.py:187
  129.5 2.7 %fusion.24 = bf16[64,4096]{1,0:T(8,128)(2,1)S(1)} fusion(bf16[1,1792,4096]{2,1,0:T(8,128)(2,1)S(1)} %bitcast.294, bf16[64,1024]{1,0:T(8,128)(2,1)S(1)} %get-tuple-element.50, bf16[64,1024]{1,0:T(8,128)(2,1)S(1)} %get-tuple-element.51, bf16[64,1024]{1,0:T(8,128)(2,1)S(1)} %get-tuple-element.52, bf16[64,1024]{1,0:T(8,128)(2,1)S(1)} %get-tuple-element.49, ...), kind=kOutput, calls=%fused_computation.18 | convolution fusion | flops 942669824 | bytes 15958532 | tf_op jit(solution)/shard_map/dot_general | solution.py:187
  138.7 3.9 %collective-permute-done.31 = bf16[1,32,4096]{2,1,0:T(8,128)(2,1)S(1)} collective-permute-done((bf16[1,32,4096]{2,1,0:T(8,128)(2,1)S(1)}, bf16[1,32,4096]{2,1,0:T(8,128)(2,1)S(1)}, u32[]{:S(2)}, u32[]{:S(2)}) %collective-permute-start.31) | collective-permute-done | bytes 262176 | tf_op jit(solution)/shard_map/ppermute | solution.py:208
  143.2 5.0 %collective-permute-done.34 = bf16[1,32,4096]{2,1,0:T(8,128)(2,1)S(1)} collective-permute-done((bf16[1,32,4096]{2,1,0:T(8,128)(2,1)S(1)}, bf16[1,32,4096]{2,1,0:T(8,128)(2,1)S(1)}, u32[]{:S(2)}, u32[]{:S(2)}) %collective-permute-start.34) | collective-permute-done | bytes 262176 | tf_op jit(solution)/shard_map/ppermute | solution.py:208
  149.1 4.7 %collective-permute-done.37 = bf16[1,32,4096]{2,1,0:T(8,128)(2,1)S(1)} collective-permute-done((bf16[1,32,4096]{2,1,0:T(8,128)(2,1)S(1)}, bf16[1,32,4096]{2,1,0:T(8,128)(2,1)S(1)}, u32[]{:S(2)}, u32[]{:S(2)}) %collective-permute-start.37) | collective-permute-done | bytes 262176 | tf_op jit(solution)/shard_map/ppermute | solution.py:208
  154.7 3.8 %collective-permute-done.40 = bf16[1,32,4096]{2,1,0:T(8,128)(2,1)S(1)} collective-permute-done((bf16[1,32,4096]{2,1,0:T(8,128)(2,1)S(1)}, bf16[1,32,4096]{2,1,0:T(8,128)(2,1)S(1)}, u32[]{:S(2)}, u32[]{:S(2)}) %collective-permute-start.40) | collective-permute-done | bytes 262176 | tf_op jit(solution)/shard_map/ppermute | solution.py:208
  158.5 7.2 %collective-permute-done.35 = bf16[32,4096]{1,0:T(8,128)(2,1)S(1)} collective-permute-done((bf16[32,4096]{1,0:T(8,128)(2,1)S(1)}, bf16[32,4096]{1,0:T(8,128)(2,1)S(1)}, u32[]{:S(2)}, u32[]{:S(2)}) %collective-permute-start.35) | collective-permute-done | bytes 262176 | tf_op jit(solution)/shard_map/ppermute | solution.py:216
  (262 shorter events, 56.5 us)
Async XLA Ops:
  0.0 25.8 %collective-permute-start.6 = (bf16[512,128]{1,0:T(8,128)(2,1)}, bf16[512,128]{1,0:T(8,128)(2,1)S(1)}, u32[]{:S(2)}, u32[]{:S(2)}) collective-permute-start(bf16[512,128]{1,0:T(8,128)(2,1)} %param.12), channel_id=1, source_target_pairs={{0,4},{4,8},{8,12},{12,0},{1,5},{5,9},{9,13},{13,1},{2,6},{6,10},{... | collective-permute-start | bytes 393224 | tf_op jit(solution)/shard_map/ppermute | solution.py:14
  3.0 25.8 %collective-permute-start.7 = (bf16[512,128]{1,0:T(8,128)(2,1)}, bf16[512,128]{1,0:T(8,128)(2,1)S(1)}, u32[]{:S(2)}, u32[]{:S(2)}) collective-permute-start(bf16[512,128]{1,0:T(8,128)(2,1)} %param.12), channel_id=1, source_target_pairs={{0,8},{4,12},{8,0},{12,4},{1,9},{5,13},{9,1},{13,5},{2,10},{6,14},... | collective-permute-start | bytes 393224 | tf_op jit(solution)/shard_map/ppermute | solution.py:14
  5.6 24.8 %collective-permute-start.8 = (bf16[512,128]{1,0:T(8,128)(2,1)}, bf16[512,128]{1,0:T(8,128)(2,1)S(1)}, u32[]{:S(2)}, u32[]{:S(2)}) collective-permute-start(bf16[512,128]{1,0:T(8,128)(2,1)} %param.12), channel_id=1, source_target_pairs={{0,12},{4,0},{8,4},{12,8},{1,13},{5,1},{9,5},{13,9},{2,14},{6,2},{... | collective-permute-start | bytes 393224 | tf_op jit(solution)/shard_map/ppermute | solution.py:14
  7.0 12.0 %collective-permute-start.1 = (s32[128,2]{0,1:T(2,128)}, s32[128,2]{0,1:T(2,128)S(1)}, u32[]{:S(2)}, u32[]{:S(2)}) collective-permute-start(s32[128,2]{0,1:T(2,128)} %param.17), channel_id=1, source_target_pairs={{0,4},{4,8},{8,12},{12,0},{1,5},{5,9},{9,13},{13,1},{2,6},{6,10},{... | collective-permute-start | bytes 3080 | tf_op jit(solution)/shard_map/ppermute | solution.py:14
  7.6 9.6 %collective-permute-start = (s32[128,2]{0,1:T(2,128)}, s32[128,2]{0,1:T(2,128)S(1)}, u32[]{:S(2)}, u32[]{:S(2)}) collective-permute-start(s32[128,2]{0,1:T(2,128)} %param.17), channel_id=1, source_target_pairs={{0,8},{4,12},{8,0},{12,4},{1,9},{5,13},{9,1},{13,5},{2,10},{6,14},... | collective-permute-start | bytes 3080 | tf_op jit(solution)/shard_map/ppermute | solution.py:14
  19.0 15.8 %collective-permute-start.3 = (bf16[512,128]{0,1:T(8,128)(2,1)S(1)}, bf16[512,128]{0,1:T(8,128)(2,1)S(1)}, u32[]{:S(2)}, u32[]{:S(2)}) collective-permute-start(bf16[512,128]{0,1:T(8,128)(2,1)S(1)} %copy.26), channel_id=1, source_target_pairs={{0,4},{4,8},{8,12},{12,0},{1,5},{5,9},{9,13},{13,1},{2,6},{6,10},{... | collective-permute-start | bytes 393224 | tf_op jit(solution)/shard_map/ppermute | solution.py:14
  21.0 13.8 %collective-permute-start.4 = (bf16[512,128]{0,1:T(8,128)(2,1)S(1)}, bf16[512,128]{0,1:T(8,128)(2,1)S(1)}, u32[]{:S(2)}, u32[]{:S(2)}) collective-permute-start(bf16[512,128]{0,1:T(8,128)(2,1)S(1)} %copy.26), channel_id=1, source_target_pairs={{0,8},{4,12},{8,0},{12,4},{1,9},{5,13},{9,1},{13,5},{2,10},{6,14},... | collective-permute-start | bytes 393224 | tf_op jit(solution)/shard_map/ppermute | solution.py:14
  25.8 9.0 %collective-permute-start.5 = (bf16[512,128]{0,1:T(8,128)(2,1)S(1)}, bf16[512,128]{0,1:T(8,128)(2,1)S(1)}, u32[]{:S(2)}, u32[]{:S(2)}) collective-permute-start(bf16[512,128]{0,1:T(8,128)(2,1)S(1)} %copy.26), channel_id=1, source_target_pairs={{0,12},{4,0},{8,4},{12,8},{1,13},{5,1},{9,5},{13,9},{2,14},{6,2},{... | collective-permute-start | bytes 393224 | tf_op jit(solution)/shard_map/ppermute | solution.py:14
  28.9 32.8 %collective-permute-start.14 = (bf16[128,1024]{1,0:T(8,128)(2,1)}, bf16[128,1024]{1,0:T(8,128)(2,1)S(1)}, u32[]{:S(2)}, u32[]{:S(2)}) collective-permute-start(bf16[128,1024]{1,0:T(8,128)(2,1)} %param.15), channel_id=1, source_target_pairs={{0,0},{1,4},{2,8},{3,12},{4,1},{5,5},{6,9},{7,13},{8,2},{9,6},{10,... | collective-permute-start | bytes 786440 | tf_op jit(solution)/shard_map/ppermute | solution.py:62
  36.9 9.4 %collective-permute-start.9 = (bf16[128,512]{0,1:T(8,128)(2,1)S(1)}, bf16[128,512]{0,1:T(8,128)(2,1)S(1)}, u32[]{:S(2)}, u32[]{:S(2)}) collective-permute-start(bf16[128,512]{0,1:T(8,128)(2,1)S(1)} %bitcast.307), channel_id=1, source_target_pairs={{0,4},{4,8},{8,12},{12,0},{1,5},{5,9},{9,13},{13,1},{2,6},{6,10},{... | collective-permute-start | bytes 393224 | tf_op jit(solution)/shard_map/ppermute | solution.py:14
  42.9 11.4 %collective-permute-start.10 = (bf16[128,512]{0,1:T(8,128)(2,1)S(1)}, bf16[128,512]{0,1:T(8,128)(2,1)S(1)}, u32[]{:S(2)}, u32[]{:S(2)}) collective-permute-start(bf16[128,512]{0,1:T(8,128)(2,1)S(1)} %bitcast.308), channel_id=1, source_target_pairs={{0,8},{4,12},{8,0},{12,4},{1,9},{5,13},{9,1},{13,5},{2,10},{6,14},... | collective-permute-start | bytes 393224 | tf_op jit(solution)/shard_map/ppermute | solution.py:14
  42.9 11.4 %collective-permute-start.11 = (bf16[128,512]{0,1:T(8,128)(2,1)S(1)}, bf16[128,512]{0,1:T(8,128)(2,1)S(1)}, u32[]{:S(2)}, u32[]{:S(2)}) collective-permute-start(bf16[128,512]{0,1:T(8,128)(2,1)S(1)} %bitcast.309), channel_id=1, source_target_pairs={{0,12},{4,0},{8,4},{12,8},{1,13},{5,1},{9,5},{13,9},{2,14},{6,2},{... | collective-permute-start | bytes 393224 | tf_op jit(solution)/shard_map/ppermute | solution.py:14
  59.0 8.7 %collective-permute-start.13 = (bf16[1,128,1024]{2,1,0:T(8,128)(2,1)S(1)}, bf16[1,128,1024]{2,1,0:T(8,128)(2,1)S(1)}, u32[]{:S(2)}, u32[]{:S(2)}) collective-permute-start(bf16[1,128,1024]{2,1,0:T(8,128)(2,1)S(1)} %fusion.114), channel_id=1, source_target_pairs={{0,2},{1,3},{2,0},{3,1},{4,6},{5,7},{6,4},{7,5},{8,10},{9,11},{10,... | collective-permute-start | bytes 786440 | tf_op jit(solution)/shard_map/ppermute | solution.py:114
  68.9 21.5 %collective-permute-start.18 = (bf16[1,128,1024]{2,1,0:T(8,128)(2,1)S(1)}, bf16[1,128,1024]{2,1,0:T(8,128)(2,1)S(1)}, u32[]{:S(2)}, u32[]{:S(2)}) collective-permute-start(bf16[1,128,1024]{2,1,0:T(8,128)(2,1)S(1)} %fusion.109), channel_id=1, source_target_pairs={{0,4},{4,8},{8,12},{12,0},{1,5},{5,9},{9,13},{13,1},{2,6},{6,10},{... | collective-permute-start | bytes 786440 | tf_op jit(solution)/shard_map/ppermute | solution.py:129
  71.5 21.5 %collective-permute-start.22 = (bf16[1,128,1024]{2,1,0:T(8,128)(2,1)S(1)}, bf16[1,128,1024]{2,1,0:T(8,128)(2,1)S(1)}, u32[]{:S(2)}, u32[]{:S(2)}) collective-permute-start(bf16[1,128,1024]{2,1,0:T(8,128)(2,1)S(1)} %fusion.109), channel_id=1, source_target_pairs={{0,12},{4,0},{8,4},{12,8},{1,13},{5,1},{9,5},{13,9},{2,14},{6,2},{... | collective-permute-start | bytes 786440 | tf_op jit(solution)/shard_map/ppermute | solution.py:129
  75.5 7.4 %collective-permute-start.17 = (bf16[64,1024]{1,0:T(8,128)(2,1)S(1)}, bf16[64,1024]{1,0:T(8,128)(2,1)S(1)}, u32[]{:S(2)}, u32[]{:S(2)}) collective-permute-start(bf16[64,1024]{1,0:T(8,128)(2,1)S(1)} %convolution_convert_fusion.17), channel_id=1, source_target_pairs={{0,3},{1,2},{2,1},{3,0},{4,7},{5,6},{6,5},{7,4},{8,11},{9,10},{10,... | collective-permute-start | bytes 393224 | tf_op jit(solution)/shard_map/ppermute | solution.py:138
  76.9 18.6 %collective-permute-start.26 = (bf16[1,128,1024]{2,1,0:T(8,128)(2,1)S(1)}, bf16[1,128,1024]{2,1,0:T(8,128)(2,1)S(1)}, u32[]{:S(2)}, u32[]{:S(2)}) collective-permute-start(bf16[1,128,1024]{2,1,0:T(8,128)(2,1)S(1)} %fusion.109), channel_id=1, source_target_pairs={{0,8},{4,12},{8,0},{12,4},{1,9},{5,13},{9,1},{13,5},{2,10},{6,14},... | collective-permute-start | bytes 786440 | tf_op jit(solution)/shard_map/ppermute | solution.py:129
  93.2 12.0 %collective-permute-start.23 = (bf16[64,1024]{1,0:T(8,128)(2,1)S(1)}, bf16[64,1024]{1,0:T(8,128)(2,1)S(1)}, u32[]{:S(2)}, u32[]{:S(2)}) collective-permute-start(bf16[64,1024]{1,0:T(8,128)(2,1)S(1)} %convolution_convert_fusion.11), channel_id=1, source_target_pairs={{0,1},{1,0},{2,3},{3,2},{4,5},{5,4},{6,7},{7,6},{8,9},{9,8},{10,11... | collective-permute-start | bytes 393224 | tf_op jit(solution)/shard_map/ppermute | solution.py:138
  95.4 11.5 %collective-permute-start.24 = (bf16[64,1024]{1,0:T(8,128)(2,1)S(1)}, bf16[64,1024]{1,0:T(8,128)(2,1)S(1)}, u32[]{:S(2)}, u32[]{:S(2)}) collective-permute-start(bf16[64,1024]{1,0:T(8,128)(2,1)S(1)} %convolution_convert_fusion.10), channel_id=1, source_target_pairs={{0,2},{1,3},{2,0},{3,1},{4,6},{5,7},{6,4},{7,5},{8,10},{9,11},{10,... | collective-permute-start | bytes 393224 | tf_op jit(solution)/shard_map/ppermute | solution.py:138
  96.9 9.9 %collective-permute-start.25 = (bf16[64,1024]{1,0:T(8,128)(2,1)S(1)}, bf16[64,1024]{1,0:T(8,128)(2,1)S(1)}, u32[]{:S(2)}, u32[]{:S(2)}) collective-permute-start(bf16[64,1024]{1,0:T(8,128)(2,1)S(1)} %convolution_convert_fusion.9), channel_id=1, source_target_pairs={{0,3},{1,2},{2,1},{3,0},{4,7},{5,6},{6,5},{7,4},{8,11},{9,10},{10,... | collective-permute-start | bytes 393224 | tf_op jit(solution)/shard_map/ppermute | solution.py:138
  97.7 14.5 %collective-permute-start.27 = (bf16[64,1024]{1,0:T(8,128)(2,1)S(1)}, bf16[64,1024]{1,0:T(8,128)(2,1)S(1)}, u32[]{:S(2)}, u32[]{:S(2)}) collective-permute-start(bf16[64,1024]{1,0:T(8,128)(2,1)S(1)} %convolution_convert_fusion.7), channel_id=1, source_target_pairs={{0,1},{1,0},{2,3},{3,2},{4,5},{5,4},{6,7},{7,6},{8,9},{9,8},{10,11... | collective-permute-start | bytes 393224 | tf_op jit(solution)/shard_map/ppermute | solution.py:138
  98.8 13.4 %collective-permute-start.28 = (bf16[64,1024]{1,0:T(8,128)(2,1)S(1)}, bf16[64,1024]{1,0:T(8,128)(2,1)S(1)}, u32[]{:S(2)}, u32[]{:S(2)}) collective-permute-start(bf16[64,1024]{1,0:T(8,128)(2,1)S(1)} %convolution_convert_fusion.6), channel_id=1, source_target_pairs={{0,2},{1,3},{2,0},{3,1},{4,6},{5,7},{6,4},{7,5},{8,10},{9,11},{10,... | collective-permute-start | bytes 393224 | tf_op jit(solution)/shard_map/ppermute | solution.py:138
  105.2 7.0 %collective-permute-start.29 = (bf16[64,1024]{1,0:T(8,128)(2,1)S(1)}, bf16[64,1024]{1,0:T(8,128)(2,1)S(1)}, u32[]{:S(2)}, u32[]{:S(2)}) collective-permute-start(bf16[64,1024]{1,0:T(8,128)(2,1)S(1)} %convolution_convert_fusion.5), channel_id=1, source_target_pairs={{0,3},{1,2},{2,1},{3,0},{4,7},{5,6},{6,5},{7,4},{8,11},{9,10},{10,... | collective-permute-start | bytes 393224 | tf_op jit(solution)/shard_map/ppermute | solution.py:138
  121.8 11.2 %collective-permute-start.30 = (bf16[64,4096]{1,0:T(8,128)(2,1)S(1)}, bf16[64,4096]{1,0:T(8,128)(2,1)S(1)}, u32[]{:S(2)}, u32[]{:S(2)}) collective-permute-start(bf16[64,4096]{1,0:T(8,128)(2,1)S(1)} %convolution_convert_fusion.3), channel_id=1, source_target_pairs={{0,1},{1,0},{2,3},{3,2},{4,5},{5,4},{6,7},{7,6},{8,9},{9,8},{10,11... | collective-permute-start | bytes 1572872 | tf_op jit(solution)/shard_map/ppermute | solution.py:200
  125.1 9.1 %collective-permute-start.33 = (bf16[64,4096]{1,0:T(8,128)(2,1)S(1)}, bf16[64,4096]{1,0:T(8,128)(2,1)S(1)}, u32[]{:S(2)}, u32[]{:S(2)}) collective-permute-start(bf16[64,4096]{1,0:T(8,128)(2,1)S(1)} %convolution_convert_fusion.2), channel_id=1, source_target_pairs={{0,1},{1,0},{2,3},{3,2},{4,5},{5,4},{6,7},{7,6},{8,9},{9,8},{10,11... | collective-permute-start | bytes 1572872 | tf_op jit(solution)/shard_map/ppermute | solution.py:200
  133.3 9.2 %collective-permute-start.31 = (bf16[1,32,4096]{2,1,0:T(8,128)(2,1)S(1)}, bf16[1,32,4096]{2,1,0:T(8,128)(2,1)S(1)}, u32[]{:S(2)}, u32[]{:S(2)}) collective-permute-start(bf16[1,32,4096]{2,1,0:T(8,128)(2,1)S(1)} %fusion.115), channel_id=1, source_target_pairs={{0,2},{1,3},{2,0},{3,1},{4,6},{5,7},{6,4},{7,5},{8,10},{9,11},{10,... | collective-permute-start | bytes 786440 | tf_op jit(solution)/shard_map/ppermute | solution.py:208
  134.5 13.7 %collective-permute-start.34 = (bf16[1,32,4096]{2,1,0:T(8,128)(2,1)S(1)}, bf16[1,32,4096]{2,1,0:T(8,128)(2,1)S(1)}, u32[]{:S(2)}, u32[]{:S(2)}) collective-permute-start(bf16[1,32,4096]{2,1,0:T(8,128)(2,1)S(1)} %fusion.116), channel_id=1, source_target_pairs={{0,2},{1,3},{2,0},{3,1},{4,6},{5,7},{6,4},{7,5},{8,10},{9,11},{10,... | collective-permute-start | bytes 786440 | tf_op jit(solution)/shard_map/ppermute | solution.py:208
  136.2 17.6 %collective-permute-start.37 = (bf16[1,32,4096]{2,1,0:T(8,128)(2,1)S(1)}, bf16[1,32,4096]{2,1,0:T(8,128)(2,1)S(1)}, u32[]{:S(2)}, u32[]{:S(2)}) collective-permute-start(bf16[1,32,4096]{2,1,0:T(8,128)(2,1)S(1)} %fusion.117), channel_id=1, source_target_pairs={{0,2},{1,3},{2,0},{3,1},{4,6},{5,7},{6,4},{7,5},{8,10},{9,11},{10,... | collective-permute-start | bytes 786440 | tf_op jit(solution)/shard_map/ppermute | solution.py:208
  137.4 21.2 %collective-permute-start.40 = (bf16[1,32,4096]{2,1,0:T(8,128)(2,1)S(1)}, bf16[1,32,4096]{2,1,0:T(8,128)(2,1)S(1)}, u32[]{:S(2)}, u32[]{:S(2)}) collective-permute-start(bf16[1,32,4096]{2,1,0:T(8,128)(2,1)S(1)} %fusion.118), channel_id=1, source_target_pairs={{0,2},{1,3},{2,0},{3,1},{4,6},{5,7},{6,4},{7,5},{8,10},{9,11},{10,... | collective-permute-start | bytes 786440 | tf_op jit(solution)/shard_map/ppermute | solution.py:208
  142.6 15.9 %collective-permute-start.32 = (bf16[32,4096]{1,0:T(8,128)(2,1)S(1)}, bf16[32,4096]{1,0:T(8,128)(2,1)S(1)}, u32[]{:S(2)}, u32[]{:S(2)}) collective-permute-start(bf16[32,4096]{1,0:T(8,128)(2,1)S(1)} %fusion.119), channel_id=1, source_target_pairs={{0,8},{4,12},{8,0},{12,4},{1,9},{5,13},{9,1},{13,5},{2,10},{6,14},... | collective-permute-start | bytes 786440 | tf_op jit(solution)/shard_map/ppermute | solution.py:216
  148.3 17.5 %collective-permute-start.35 = (bf16[32,4096]{1,0:T(8,128)(2,1)S(1)}, bf16[32,4096]{1,0:T(8,128)(2,1)S(1)}, u32[]{:S(2)}, u32[]{:S(2)}) collective-permute-start(bf16[32,4096]{1,0:T(8,128)(2,1)S(1)} %fusion.120), channel_id=1, source_target_pairs={{0,12},{4,0},{8,4},{12,8},{1,13},{5,1},{9,5},{13,9},{2,14},{6,2},{... | collective-permute-start | bytes 786440 | tf_op jit(solution)/shard_map/ppermute | solution.py:216
  153.9 11.8 %collective-permute-start.38 = (bf16[32,4096]{1,0:T(8,128)(2,1)S(1)}, bf16[32,4096]{1,0:T(8,128)(2,1)S(1)}, u32[]{:S(2)}, u32[]{:S(2)}) collective-permute-start(bf16[32,4096]{1,0:T(8,128)(2,1)S(1)} %fusion.121), channel_id=1, source_target_pairs={{0,4},{4,8},{8,12},{12,0},{1,5},{5,9},{9,13},{13,1},{2,6},{6,10},{... | collective-permute-start | bytes 786440 | tf_op jit(solution)/shard_map/ppermute | solution.py:216
  (45 other events, 362.2 us)

commit v2 on v1

--- a/solution.py
+++ b/solution.py
@@ -70,6 +70,7 @@
     visible_end = span * ctx_count - tok * ctx_count + order
     keys_all = jnp.concatenate(gather_rotated(keys, ctx_count))
     values_all = jnp.concatenate(gather_rotated(values, ctx_count))
+    keys_all = lax.optimization_barrier(keys_all)
     positions = jnp.concatenate(
         [((c - k) % ctx_count) * span + jnp.arange(span, dtype=jnp.int32) for k in range(ctx_count)]
     )
@@ -77,7 +78,7 @@
     score = jnp.einsum(
         "tqd,jd->qtj", query_blocks, keys_all, preferred_element_type=f32
     ) * (1.0 / math.sqrt(head_dim))
-    visible = positions[None, None, :] <= visible_end[None, :, None]
+    visible = lax.optimization_barrier(positions[None, :] <= visible_end[:, None])[None]
     score = jnp.where(visible, score, -1e30)
     highest = jnp.max(score, axis=2, keepdims=True)
     weight = jnp.where(visible, jnp.exp(score - highest), 0.0)
@@ -123,6 +124,7 @@
                 routes_stacked, (c - (e * per_share + j)) % ctx_count, 0, keepdims=False
             )
             pickers.append(picker_of(jnp.any(block == (e ^ k), axis=1), capacity).astype(bf16))
+    pickers = lax.optimization_barrier(pickers)
     turns = sorted(range(ctx_count), key=lambda k: min(k, ctx_count - k))
     chunks = {}
     for k in turns:
@@ -175,7 +177,7 @@
     mine = (experts == e).astype(f32)[None, :]
     own_share = tok // exp_count
 
-    def contribution(k):
+    def contribution(k, gives):
         block = (c + k) % ctx_count
         block_routes = routes_all[-k % ctx_count]
         picker = picker_of(jnp.any(block_routes == e, axis=1), capacity).astype(f32)
@@ -184,7 +186,7 @@
         gate = jax.nn.sigmoid(
             jnp.sum(rows_of(logits, block) * (mine - other_slot), axis=1, keepdims=True)
         )
-        gives = gate * jnp.dot(rows_of(act, block), down_here, preferred_element_type=f32)
+        gives *= gate
         if k == 0:
             gives += 0.5 * stream_rows.astype(f32)
         gives = gives.astype(bf16)
@@ -198,6 +200,7 @@
 
         sent = spread_rows(1 - low).astype(bf16)
         came = lax.ppermute(sent, "exp", [(i, i ^ 1) for i in range(exp_count)])
+        first = came
         acc = spread_rows(low) + came.astype(f32)
         half = exp_count // 2
         for level in range(1, levels):
@@ -207,15 +210,27 @@
             sent = lax.dynamic_index_in_dim(acc, 1 - bit, 1, keepdims=False).astype(bf16)
             came = lax.ppermute(sent, "exp", [(i, i ^ (1 << level)) for i in range(exp_count)])
             acc = lax.dynamic_index_in_dim(acc, bit, 1, keepdims=False) + came.astype(f32)
-        return acc.reshape(own_share, features)
-
-    output = 0.0
-    for k in reversed(turns):
-        part = contribution(k)
-        if k:
-            part = lax.ppermute(part.astype(bf16), "ctx", rotation(ctx_count, k)).astype(f32)
-        output += part
-    return output.astype(bf16)
+        return acc.reshape(own_share, features), first
+
+    direct = [k for k in (1,) if k < ctx_count]
+    others = [k for k in reversed(turns) if k and k not in direct]
+    added, output, after = 0.0, 0.0, ()
+    for k in direct:
+        part = jnp.dot(rows_of(act, (c + k) % ctx_count), down_here, preferred_element_type=f32)
+        part = part.astype(bf16)
+        after += (part,)
+        added += lax.ppermute(part, "ctx", rotation(ctx_count, k)).astype(f32)
+    for k in others:
+        rows = rows_of(lax.optimization_barrier((act, after))[0], (c + k) % ctx_count)
+        gives = jnp.dot(rows, down_here, preferred_element_type=f32)
+        part, after = contribution(k, gives)
+        part = part.astype(bf16)
+        output += lax.ppermute(part, "ctx", rotation(ctx_count, k)).astype(f32)
+    rows = rows_of(lax.optimization_barrier((act, after))[0], c)
+    gives = jnp.dot(rows, down_here, preferred_element_type=f32)
+    gives = lax.optimization_barrier(gives)
+    part, _ = contribution(0, gives + added)
+    return (output + part).astype(bf16)
 
 
 def solution(mesh):

time: 167 us -> 154 us (0.922)
  matrix products: 47.3 us -> 41.8 us
  starting transfers between devices: 45.7 us -> 41.4 us
  local copies, waits for them, and re-layouts: 5.16 us -> 2.4 us
  other arithmetic: 16.6 us -> 14.2 us
  waiting for transfers between devices: 50.4 us -> 52.7 us
    ppermute x4 -> x3, waiting for transfers between devices: 17.5 us -> 7.35 us  [contribution(): lax.ppermute(sent, 'exp', [(i, i ^ 1 << level) for i in range(exp_count)])]
    ppermute x12, waiting for transfers between devices: 6.1 us -> 12.7 us  [local(): piece = lax.ppermute(piece, 'exp', [(i, i ^ m) for i in range(exp_count)])]
    dot_general x4, matrix products: 13.2 us -> 6.82 us  [local(): gate_proj += jnp.dot(chunk, gate_rows, preferred_element_type=f32)]
    ppermute x12, starting transfers between devices: 9.98 us -> 6.84 us  [local(): piece = lax.ppermute(piece, 'exp', [(i, i ^ m) for i in range(exp_count)])]
    ppermute x3, starting transfers between devices: 2.2 us -> 4.51 us  [the longest x2 4.45 us: local(): output += lax.ppermute(part, 'ctx', rotation(ctx_count, k)).astype(f32)]
    ppermute x3, waiting for transfers between devices: 0.69 us -> 2.82 us  [local(): chunk = lax.ppermute(stream, 'ctx', rotation(ctx_count, k)) if k else stream]
    ppermute x12, starting transfers between devices: 21.8 us -> 19.8 us  [gather_rotated(): lax.ppermute(block, 'ctx', rotation(count, k))]
    reduce_sum x4 -> x3, other arithmetic: 3.64 us -> 1.83 us  [contribution(): other = jnp.sum(jnp.where(block_routes == e, 0, block_routes), axis=1)]
  transfers between devices with their start and end apart: 41 -> 39, of which waited for: 14 -> 17; matrix products, arithmetic and copies ran while one was open for 34% -> 30% of each run, Pallas kernels for 0% -> 0%
where the time goes in v2:
time: 154 us
  waiting for transfers between devices  52.7 us (34%)
  matrix products  41.8 us (27%)
  starting transfers between devices  41.4 us (27%)
  other arithmetic  14.2 us (9%)
  local copies, waits for them, and re-layouts  2.4 us (2%)
    ppermute x12, starting transfers between devices, gather_rotated(): lax.ppermute(block, 'ctx', rotation(count, k))  19.8 us
    ppermute x12, waiting for transfers between devices, gather_rotated(): lax.ppermute(block, 'ctx', rotation(count, k))  13.9 us
    ppermute x12, waiting for transfers between devices, local(): piece = lax.ppermute(piece, 'exp', [(i, i ^ m) for i in range(exp_count)])  12.7 us
    dot_general x3, matrix products, local(): gives = jnp.dot(rows, down_here, preferred_element_type=f32)  8.09 us
    ppermute x1, waiting for transfers between devices, local(): lax.ppermute(sent, 'exp', [(i, i ^ 1 << level) for i in range(exp_count)])  7.69 us
    ppermute x3, waiting for transfers between devices, contribution(): lax.ppermute(sent, 'exp', [(i, i ^ 1 << level) for i in range(exp_count)])  7.35 us
    dot_general x4, matrix products, local(): up_proj += jnp.dot(chunk, up_rows, preferred_element_type=f32)  6.85 us
    ppermute x12, starting transfers between devices, local(): piece = lax.ppermute(piece, 'exp', [(i, i ^ m) for i in range(exp_count)])  6.84 us
  transfers between devices with their start and end apart: 39, of which 17 were waited for; matrix products, arithmetic and copies ran while one was open for 30% of the time, Pallas kernels for 0%

profile of v2, /device:TPU:0, one launch (start us, length us, event | category | flops | bytes accessed | tf_op | source)
XLA Modules:
  0.0 153.7 jit_solution(17872937808148566463)
XLA Ops:
  0.0 3.0 %collective-permute-start.6 = (bf16[512,128]{1,0:T(8,128)(2,1)}, bf16[512,128]{1,0:T(8,128)(2,1)S(1)}, u32[]{:S(2)}, u32[]{:S(2)}) collective-permute-start(bf16[512,128]{1,0:T(8,128)(2,1)} %param.12), channel_id=1, source_target_pairs={{0,4},{4,8},{8,12},{12,0},{1,5},{5,9},{9,13},{13,1},{2,6},{6,10},{... | collective-permute-start | bytes 393224 | tf_op jit(solution)/shard_map/ppermute | solution.py:14
  3.0 2.6 %collective-permute-start.7 = (bf16[512,128]{1,0:T(8,128)(2,1)}, bf16[512,128]{1,0:T(8,128)(2,1)S(1)}, u32[]{:S(2)}, u32[]{:S(2)}) collective-permute-start(bf16[512,128]{1,0:T(8,128)(2,1)} %param.12), channel_id=1, source_target_pairs={{0,8},{4,12},{8,0},{12,4},{1,9},{5,13},{9,1},{13,5},{2,10},{6,14},... | collective-permute-start | bytes 393224 | tf_op jit(solution)/shard_map/ppermute | solution.py:14
  5.7 1.8 %collective-permute-start = (s32[128,2]{0,1:T(2,128)}, s32[128,2]{0,1:T(2,128)S(1)}, u32[]{:S(2)}, u32[]{:S(2)}) collective-permute-start(s32[128,2]{0,1:T(2,128)} %param.17), channel_id=1, source_target_pairs={{0,8},{4,12},{8,0},{12,4},{1,9},{5,13},{9,1},{13,5},{2,10},{6,14},... | collective-permute-start | bytes 3080 | tf_op jit(solution)/shard_map/ppermute | solution.py:14
  7.5 1.9 %collective-permute-start.2 = (s32[128,2]{0,1:T(2,128)}, s32[128,2]{0,1:T(2,128)S(1)}, u32[]{:S(2)}, u32[]{:S(2)}) collective-permute-start(s32[128,2]{0,1:T(2,128)} %param.17), channel_id=1, source_target_pairs={{0,12},{4,0},{8,4},{12,8},{1,13},{5,1},{9,5},{13,9},{2,14},{6,2},{... | collective-permute-start | bytes 3080 | tf_op jit(solution)/shard_map/ppermute | solution.py:14
  16.8 2.0 %collective-permute-start.4 = (bf16[512,128]{0,1:T(8,128)(2,1)S(1)}, bf16[512,128]{0,1:T(8,128)(2,1)S(1)}, u32[]{:S(2)}, u32[]{:S(2)}) collective-permute-start(bf16[512,128]{0,1:T(8,128)(2,1)S(1)} %copy.29), channel_id=1, source_target_pairs={{0,8},{4,12},{8,0},{12,4},{1,9},{5,13},{9,1},{13,5},{2,10},{6,14},... | collective-permute-start | bytes 393224 | tf_op jit(solution)/shard_map/ppermute | solution.py:14
  26.1 4.2 %fusion.204 = (f32[4,128]{1,0:T(4,128)S(1)}, bf16[4,128,2048]{1,2,0:T(8,128)(2,1)}) fusion(pred[128,2048]{0,1:T(8,128)(4,1)S(1)} %broadcast_compare_fusion, bf16[2048,128]{1,0:T(8,128)(2,1)S(1)} %pad_maximum_fusion, bf16[128,512]{1,0:T(8,128)(2,1)} %param.11), kind=kOutput, calls=%fused_computation.302 | convolution fusion | flops 274728960 | bytes 3016704 | tf_op jit(solution)/shard_map/sub | solution.py:84
  30.3 5.1 %collective-permute-done.4 = bf16[512,128]{0,1:T(8,128)(2,1)S(1)} collective-permute-done((bf16[512,128]{0,1:T(8,128)(2,1)S(1)}, bf16[512,128]{0,1:T(8,128)(2,1)S(1)}, u32[]{:S(2)}, u32[]{:S(2)}) %collective-permute-start.4) | collective-permute-done | bytes 131104 | tf_op jit(solution)/shard_map/ppermute | solution.py:14
  35.4 2.0 %fusion.78 = bf16[128,4,128]{0,2,1:T(8,128)(2,1)S(1)} fusion(bf16[4,128,2048]{1,2,0:T(8,128)(2,1)} %get-tuple-element.84, bf16[512,128]{0,1:T(8,128)(2,1)S(1)} %collective-permute-done.5, bf16[512,128]{0,1:T(8,128)(2,1)S(1)} %collective-permute-done.4, bf16[512,128]{0,1:T(8,128)(2,1)S(1)} %collective-permute-done.3, bf16[512,128]{0,1:T(8,128)(2,1)S(1)} %copy.29, ...), kind=kOutput, calls=%fused_computation.59 | convolution fusion | flops 270663680 | bytes 2754560 | tf_op jit(solution)/shard_map/qtj,jd->tqd/dot_general | solution.py:86
  37.5 3.4 %collective-permute-start.9 = (bf16[128,512]{0,1:T(8,128)(2,1)S(1)}, bf16[128,512]{0,1:T(8,128)(2,1)S(1)}, u32[]{:S(2)}, u32[]{:S(2)}) collective-permute-start(bf16[128,512]{0,1:T(8,128)(2,1)S(1)} %bitcast.293), channel_id=1, source_target_pairs={{0,4},{4,8},{8,12},{12,0},{1,5},{5,9},{9,13},{13,1},{2,6},{6,10},{... | collective-permute-start | bytes 393224 | tf_op jit(solution)/shard_map/ppermute | solution.py:14
  40.9 2.4 %collective-permute-start.11 = (bf16[128,512]{0,1:T(8,128)(2,1)S(1)}, bf16[128,512]{0,1:T(8,128)(2,1)S(1)}, u32[]{:S(2)}, u32[]{:S(2)}) collective-permute-start(bf16[128,512]{0,1:T(8,128)(2,1)S(1)} %bitcast.295), channel_id=1, source_target_pairs={{0,12},{4,0},{8,4},{12,8},{1,13},{5,1},{9,5},{13,9},{2,14},{6,2},{... | collective-permute-start | bytes 393224 | tf_op jit(solution)/shard_map/ppermute | solution.py:14
  45.1 7.1 %collective-permute-done.10 = bf16[128,512]{0,1:T(8,128)(2,1)S(1)} collective-permute-done((bf16[128,512]{0,1:T(8,128)(2,1)S(1)}, bf16[128,512]{0,1:T(8,128)(2,1)S(1)}, u32[]{:S(2)}, u32[]{:S(2)}) %collective-permute-start.10) | collective-permute-done | bytes 131104 | tf_op jit(solution)/shard_map/ppermute | solution.py:14
  56.0 7.7 %collective-permute-done.13 = bf16[1,128,1024]{2,1,0:T(8,128)(2,1)S(1)} collective-permute-done((bf16[1,128,1024]{2,1,0:T(8,128)(2,1)S(1)}, bf16[1,128,1024]{2,1,0:T(8,128)(2,1)S(1)}, u32[]{:S(2)}, u32[]{:S(2)}) %collective-permute-start.13) | collective-permute-done | bytes 262176 | tf_op jit(solution)/shard_map/ppermute | solution.py:115
  64.8 3.4 %collective-permute-start.22 = (bf16[1,128,1024]{2,1,0:T(8,128)(2,1)S(1)}, bf16[1,128,1024]{2,1,0:T(8,128)(2,1)S(1)}, u32[]{:S(2)}, u32[]{:S(2)}) collective-permute-start(bf16[1,128,1024]{2,1,0:T(8,128)(2,1)S(1)} %fusion.95), channel_id=1, source_target_pairs={{0,12},{4,0},{8,4},{12,8},{1,13},{5,1},{9,5},{13,9},{2,14},{6,2},{... | collective-permute-start | bytes 786440 | tf_op jit(solution)/shard_map/ppermute | solution.py:131
  71.2 3.8 %collective-permute-done.16 = bf16[64,1024]{1,0:T(8,128)(2,1)S(1)} collective-permute-done((bf16[64,1024]{1,0:T(8,128)(2,1)S(1)}, bf16[64,1024]{1,0:T(8,128)(2,1)S(1)}, u32[]{:S(2)}, u32[]{:S(2)}) %collective-permute-start.16) | collective-permute-done | bytes 131104 | tf_op jit(solution)/shard_map/ppermute | solution.py:140
  75.0 2.0 %collective-permute-done.17 = bf16[64,1024]{1,0:T(8,128)(2,1)S(1)} collective-permute-done((bf16[64,1024]{1,0:T(8,128)(2,1)S(1)}, bf16[64,1024]{1,0:T(8,128)(2,1)S(1)}, u32[]{:S(2)}, u32[]{:S(2)}) %collective-permute-start.17) | collective-permute-done | bytes 131104 | tf_op jit(solution)/shard_map/ppermute | solution.py:140
  77.2 3.3 %fusion.37 = f32[256,1792]{1,0:T(8,128)S(1)} fusion(bf16[256,1024]{1,0:T(8,128)(2,1)S(1)} %get-tuple-element.62, bf16[1,4096,1792]{2,1,0:T(8,128)(2,1)} %param.20, s32[]{:T(128)S(6)} %select_n.268), kind=kOutput, calls=%fused_computation.32 | convolution fusion | flops 939524096 | bytes 6029316 | tf_op jit(solution)/shard_map/dot_general | solution.py:153
  82.3 2.8 %collective-permute-done.26 = bf16[1,128,1024]{2,1,0:T(8,128)(2,1)S(1)} collective-permute-done((bf16[1,128,1024]{2,1,0:T(8,128)(2,1)S(1)}, bf16[1,128,1024]{2,1,0:T(8,128)(2,1)S(1)}, u32[]{:S(2)}, u32[]{:S(2)}) %collective-permute-start.26) | collective-permute-done | bytes 262176 | tf_op jit(solution)/shard_map/ppermute | solution.py:131
  87.7 1.8 %collective-permute-start.20 = (bf16[64,1024]{1,0:T(8,128)(2,1)S(1)}, bf16[64,1024]{1,0:T(8,128)(2,1)S(1)}, u32[]{:S(2)}, u32[]{:S(2)}) collective-permute-start(bf16[64,1024]{1,0:T(8,128)(2,1)S(1)} %convolution_convert_fusion.13), channel_id=1, source_target_pairs={{0,2},{1,3},{2,0},{3,1},{4,6},{5,7},{6,4},{7,5},{8,10},{9,11},{10,... | collective-permute-start | bytes 393224 | tf_op jit(solution)/shard_map/ppermute | solution.py:140
  92.1 3.9 %collective-permute-done.20 = bf16[64,1024]{1,0:T(8,128)(2,1)S(1)} collective-permute-done((bf16[64,1024]{1,0:T(8,128)(2,1)S(1)}, bf16[64,1024]{1,0:T(8,128)(2,1)S(1)}, u32[]{:S(2)}, u32[]{:S(2)}) %collective-permute-start.20) | collective-permute-done | bytes 131104 | tf_op jit(solution)/shard_map/ppermute | solution.py:140
  96.1 2.0 %collective-permute-done.21 = bf16[64,1024]{1,0:T(8,128)(2,1)S(1)} collective-permute-done((bf16[64,1024]{1,0:T(8,128)(2,1)S(1)}, bf16[64,1024]{1,0:T(8,128)(2,1)S(1)}, u32[]{:S(2)}, u32[]{:S(2)}) %collective-permute-start.21) | collective-permute-done | bytes 131104 | tf_op jit(solution)/shard_map/ppermute | solution.py:140
  107.2 1.8 %multiply_reduce_fusion = (f32[256]{0:T(256)S(1)}, bf16[256,1024]{1,0:T(8,128)(2,1)S(1)}) fusion(bf16[64,1024]{1,0:T(8,128)(2,1)} %collective-permute-done.29, bf16[64,1024]{1,0:T(8,128)(2,1)} %collective-permute-done.28, bf16[64,1024]{1,0:T(8,128)(2,1)S(1)} %collective-permute-done.27, bf16[64,1024]{1,0:T(8,128)(2,1)S(1)} %convolution_convert_fusion.7), kind=kLoop, calls=%fused_computation.92 | loop fusion | flops 2883328 | bytes 1049600 | tf_op jit(solution)/shard_map/reduce_sum | solution.py:154
  111.5 3.3 %fusion.61 = f32[256,1792]{1,0:T(8,128)S(1)} fusion(f32[256,1792]{1,0:T(8,128)S(1)} %fusion.55, bf16[256,1024]{1,0:T(8,128)(2,1)S(1)} %get-tuple-element.56, bf16[1,4096,1792]{2,1,0:T(8,128)(2,1)} %param.19, s32[]{:T(128)S(6)} %select_n.271), kind=kOutput, calls=%fused_computation.48 | convolution fusion | flops 939982848 | bytes 7864324 | tf_op jit(solution)/shard_map/dot_general | solution.py:152
  115.6 2.9 %fusion.21 = bf16[64,4096]{1,0:T(8,128)(2,1)S(1)} fusion(bf16[1,1792,4096]{2,1,0:T(8,128)(2,1)S(1)} %bitcast.282, bf16[256,1792]{1,0:T(8,128)(2,1)S(1)} %multiply_convert_fusion, s32[]{:T(128)S(6)} %select_n.273), kind=kOutput, calls=%fused_computation.16 | convolution fusion | flops 939786240 | bytes 15433732 | tf_op jit(solution)/shard_map/dot_general | solution.py:219
  119.0 2.7 %fusion.18 = bf16[64,4096]{1,0:T(8,128)(2,1)S(1)} fusion(bf16[1,1792,4096]{2,1,0:T(8,128)(2,1)S(1)} %bitcast.282, f32[64]{0:T(128)S(1)} %add_divide_fusion.2, bf16[256,1792]{1,0:T(8,128)(2,1)S(1)} %multiply_convert_fusion, s32[]{:T(128)S(6)} %select_n.275), kind=kOutput, calls=%fused_computation.15 | convolution fusion | flops 940048384 | bytes 15434244 | tf_op jit(solution)/shard_map/dot_general | solution.py:225
  126.0 2.7 %fusion.15 = bf16[64,4096]{1,0:T(8,128)(2,1)S(1)} fusion(bf16[1,1792,4096]{2,1,0:T(8,128)(2,1)S(1)} %bitcast.282, f32[64]{0:T(128)S(1)} %add_divide_fusion.1, bf16[256,1792]{1,0:T(8,128)(2,1)S(1)} %multiply_convert_fusion, s32[]{:T(128)S(6)} %select_n.279), kind=kOutput, calls=%fused_computation.14 | convolution fusion | flops 940048384 | bytes 15434244 | tf_op jit(solution)/shard_map/dot_general | solution.py:225
  129.0 3.9 %collective-permute-done.31 = bf16[1,32,4096]{2,1,0:T(8,128)(2,1)S(1)} collective-permute-done((bf16[1,32,4096]{2,1,0:T(8,128)(2,1)S(1)}, bf16[1,32,4096]{2,1,0:T(8,128)(2,1)S(1)}, u32[]{:S(2)}, u32[]{:S(2)}) %collective-permute-start.31) | collective-permute-done | bytes 262176 | tf_op jit(solution)/shard_map/ppermute | solution.py:211
  132.9 2.4 %collective-permute-start.32 = (bf16[32,4096]{1,0:T(8,128)(2,1)S(1)}, bf16[32,4096]{1,0:T(8,128)(2,1)S(1)}, u32[]{:S(2)}, u32[]{:S(2)}) collective-permute-start(bf16[32,4096]{1,0:T(8,128)(2,1)S(1)} %fusion.109), channel_id=1, source_target_pairs={{0,8},{4,12},{8,0},{12,4},{1,9},{5,13},{9,1},{13,5},{2,10},{6,14},... | collective-permute-start | bytes 786440 | tf_op jit(solution)/shard_map/ppermute | solution.py:228
  136.1 2.7 %fusion.1 = f32[64,4096]{1,0:T(8,128)S(1)} fusion(bf16[1,1792,4096]{2,1,0:T(8,128)(2,1)S(1)} %bitcast.282, bf16[256,1792]{1,0:T(8,128)(2,1)S(1)} %multiply_convert_fusion, s32[]{:T(128)S(6)} %select_n.281), kind=kOutput, calls=%fused_computation.1 | convolution fusion | flops 939524096 | bytes 15958020 | tf_op jit(solution)/shard_map/dot_general | solution.py:230
  139.5 3.5 %collective-permute-done.34 = bf16[1,32,4096]{2,1,0:T(8,128)(2,1)S(1)} collective-permute-done((bf16[1,32,4096]{2,1,0:T(8,128)(2,1)S(1)}, bf16[1,32,4096]{2,1,0:T(8,128)(2,1)S(1)}, u32[]{:S(2)}, u32[]{:S(2)}) %collective-permute-start.34) | collective-permute-done | bytes 262176 | tf_op jit(solution)/shard_map/ppermute | solution.py:211
  143.0 2.0 %collective-permute-start.35 = (bf16[32,4096]{1,0:T(8,128)(2,1)S(1)}, bf16[32,4096]{1,0:T(8,128)(2,1)S(1)}, u32[]{:S(2)}, u32[]{:S(2)}) collective-permute-start(bf16[32,4096]{1,0:T(8,128)(2,1)S(1)} %fusion.110), channel_id=1, source_target_pairs={{0,12},{4,0},{8,4},{12,8},{1,13},{5,1},{9,5},{13,9},{2,14},{6,2},{... | collective-permute-start | bytes 786440 | tf_op jit(solution)/shard_map/ppermute | solution.py:228
  146.7 2.0 %collective-permute-done.32 = bf16[32,4096]{1,0:T(8,128)(2,1)S(1)} collective-permute-done((bf16[32,4096]{1,0:T(8,128)(2,1)S(1)}, bf16[32,4096]{1,0:T(8,128)(2,1)S(1)}, u32[]{:S(2)}, u32[]{:S(2)}) %collective-permute-start.32) | collective-permute-done | bytes 262176 | tf_op jit(solution)/shard_map/ppermute | solution.py:228
  148.6 4.2 %collective-permute-done.35 = bf16[32,4096]{1,0:T(8,128)(2,1)S(1)} collective-permute-done((bf16[32,4096]{1,0:T(8,128)(2,1)S(1)}, bf16[32,4096]{1,0:T(8,128)(2,1)S(1)}, u32[]{:S(2)}, u32[]{:S(2)}) %collective-permute-start.35) | collective-permute-done | bytes 262176 | tf_op jit(solution)/shard_map/ppermute | solution.py:228
  (216 shorter events, 52.0 us)
Async XLA Ops:
  0.0 23.2 %collective-permute-start.6 = (bf16[512,128]{1,0:T(8,128)(2,1)}, bf16[512,128]{1,0:T(8,128)(2,1)S(1)}, u32[]{:S(2)}, u32[]{:S(2)}) collective-permute-start(bf16[512,128]{1,0:T(8,128)(2,1)} %param.12), channel_id=1, source_target_pairs={{0,4},{4,8},{8,12},{12,0},{1,5},{5,9},{9,13},{13,1},{2,6},{6,10},{... | collective-permute-start | bytes 393224 | tf_op jit(solution)/shard_map/ppermute | solution.py:14
  3.0 20.5 %collective-permute-start.7 = (bf16[512,128]{1,0:T(8,128)(2,1)}, bf16[512,128]{1,0:T(8,128)(2,1)S(1)}, u32[]{:S(2)}, u32[]{:S(2)}) collective-permute-start(bf16[512,128]{1,0:T(8,128)(2,1)} %param.12), channel_id=1, source_target_pairs={{0,8},{4,12},{8,0},{12,4},{1,9},{5,13},{9,1},{13,5},{2,10},{6,14},... | collective-permute-start | bytes 393224 | tf_op jit(solution)/shard_map/ppermute | solution.py:14
  5.6 9.1 %collective-permute-start.1 = (s32[128,2]{0,1:T(2,128)}, s32[128,2]{0,1:T(2,128)S(1)}, u32[]{:S(2)}, u32[]{:S(2)}) collective-permute-start(s32[128,2]{0,1:T(2,128)} %param.17), channel_id=1, source_target_pairs={{0,4},{4,8},{8,12},{12,0},{1,5},{5,9},{9,13},{13,1},{2,6},{6,10},{... | collective-permute-start | bytes 3080 | tf_op jit(solution)/shard_map/ppermute | solution.py:14
  5.7 9.7 %collective-permute-start = (s32[128,2]{0,1:T(2,128)}, s32[128,2]{0,1:T(2,128)S(1)}, u32[]{:S(2)}, u32[]{:S(2)}) collective-permute-start(s32[128,2]{0,1:T(2,128)} %param.17), channel_id=1, source_target_pairs={{0,8},{4,12},{8,0},{12,4},{1,9},{5,13},{9,1},{13,5},{2,10},{6,14},... | collective-permute-start | bytes 3080 | tf_op jit(solution)/shard_map/ppermute | solution.py:14
  7.5 9.2 %collective-permute-start.2 = (s32[128,2]{0,1:T(2,128)}, s32[128,2]{0,1:T(2,128)S(1)}, u32[]{:S(2)}, u32[]{:S(2)}) collective-permute-start(s32[128,2]{0,1:T(2,128)} %param.17), channel_id=1, source_target_pairs={{0,12},{4,0},{8,4},{12,8},{1,13},{5,1},{9,5},{13,9},{2,14},{6,2},{... | collective-permute-start | bytes 3080 | tf_op jit(solution)/shard_map/ppermute | solution.py:14
  14.7 10.5 %collective-permute-start.8 = (bf16[512,128]{1,0:T(8,128)(2,1)}, bf16[512,128]{1,0:T(8,128)(2,1)S(1)}, u32[]{:S(2)}, u32[]{:S(2)}) collective-permute-start(bf16[512,128]{1,0:T(8,128)(2,1)} %param.12), channel_id=1, source_target_pairs={{0,12},{4,0},{8,4},{12,8},{1,13},{5,1},{9,5},{13,9},{2,14},{6,2},{... | collective-permute-start | bytes 393224 | tf_op jit(solution)/shard_map/ppermute | solution.py:14
  15.4 15.0 %collective-permute-start.3 = (bf16[512,128]{0,1:T(8,128)(2,1)S(1)}, bf16[512,128]{0,1:T(8,128)(2,1)S(1)}, u32[]{:S(2)}, u32[]{:S(2)}) collective-permute-start(bf16[512,128]{0,1:T(8,128)(2,1)S(1)} %copy.29), channel_id=1, source_target_pairs={{0,4},{4,8},{8,12},{12,0},{1,5},{5,9},{9,13},{13,1},{2,6},{6,10},{... | collective-permute-start | bytes 393224 | tf_op jit(solution)/shard_map/ppermute | solution.py:14
  16.8 18.6 %collective-permute-start.4 = (bf16[512,128]{0,1:T(8,128)(2,1)S(1)}, bf16[512,128]{0,1:T(8,128)(2,1)S(1)}, u32[]{:S(2)}, u32[]{:S(2)}) collective-permute-start(bf16[512,128]{0,1:T(8,128)(2,1)S(1)} %copy.29), channel_id=1, source_target_pairs={{0,8},{4,12},{8,0},{12,4},{1,9},{5,13},{9,1},{13,5},{2,10},{6,14},... | collective-permute-start | bytes 393224 | tf_op jit(solution)/shard_map/ppermute | solution.py:14
  23.2 12.2 %collective-permute-start.5 = (bf16[512,128]{0,1:T(8,128)(2,1)S(1)}, bf16[512,128]{0,1:T(8,128)(2,1)S(1)}, u32[]{:S(2)}, u32[]{:S(2)}) collective-permute-start(bf16[512,128]{0,1:T(8,128)(2,1)S(1)} %copy.29), channel_id=1, source_target_pairs={{0,12},{4,0},{8,4},{12,8},{1,13},{5,1},{9,5},{13,9},{2,14},{6,2},{... | collective-permute-start | bytes 393224 | tf_op jit(solution)/shard_map/ppermute | solution.py:14
  23.6 32.4 %collective-permute-start.14 = (bf16[128,1024]{1,0:T(8,128)(2,1)}, bf16[128,1024]{1,0:T(8,128)(2,1)S(1)}, u32[]{:S(2)}, u32[]{:S(2)}) collective-permute-start(bf16[128,1024]{1,0:T(8,128)(2,1)} %param.15), channel_id=1, source_target_pairs={{0,0},{1,4},{2,8},{3,12},{4,1},{5,5},{6,9},{7,13},{8,2},{9,6},{10,... | collective-permute-start | bytes 786440 | tf_op jit(solution)/shard_map/ppermute | solution.py:62
  37.5 7.6 %collective-permute-start.9 = (bf16[128,512]{0,1:T(8,128)(2,1)S(1)}, bf16[128,512]{0,1:T(8,128)(2,1)S(1)}, u32[]{:S(2)}, u32[]{:S(2)}) collective-permute-start(bf16[128,512]{0,1:T(8,128)(2,1)S(1)} %bitcast.293), channel_id=1, source_target_pairs={{0,4},{4,8},{8,12},{12,0},{1,5},{5,9},{9,13},{13,1},{2,6},{6,10},{... | collective-permute-start | bytes 393224 | tf_op jit(solution)/shard_map/ppermute | solution.py:14
  40.9 11.3 %collective-permute-start.10 = (bf16[128,512]{0,1:T(8,128)(2,1)S(1)}, bf16[128,512]{0,1:T(8,128)(2,1)S(1)}, u32[]{:S(2)}, u32[]{:S(2)}) collective-permute-start(bf16[128,512]{0,1:T(8,128)(2,1)S(1)} %bitcast.294), channel_id=1, source_target_pairs={{0,8},{4,12},{8,0},{12,4},{1,9},{5,13},{9,1},{13,5},{2,10},{6,14},... | collective-permute-start | bytes 393224 | tf_op jit(solution)/shard_map/ppermute | solution.py:14
  40.9 11.3 %collective-permute-start.11 = (bf16[128,512]{0,1:T(8,128)(2,1)S(1)}, bf16[128,512]{0,1:T(8,128)(2,1)S(1)}, u32[]{:S(2)}, u32[]{:S(2)}) collective-permute-start(bf16[128,512]{0,1:T(8,128)(2,1)S(1)} %bitcast.295), channel_id=1, source_target_pairs={{0,12},{4,0},{8,4},{12,8},{1,13},{5,1},{9,5},{13,9},{2,14},{6,2},{... | collective-permute-start | bytes 393224 | tf_op jit(solution)/shard_map/ppermute | solution.py:14
  55.3 8.4 %collective-permute-start.13 = (bf16[1,128,1024]{2,1,0:T(8,128)(2,1)S(1)}, bf16[1,128,1024]{2,1,0:T(8,128)(2,1)S(1)}, u32[]{:S(2)}, u32[]{:S(2)}) collective-permute-start(bf16[1,128,1024]{2,1,0:T(8,128)(2,1)S(1)} %fusion.105), channel_id=1, source_target_pairs={{0,2},{1,3},{2,0},{3,1},{4,6},{5,7},{6,4},{7,5},{8,10},{9,11},{10,... | collective-permute-start | bytes 786440 | tf_op jit(solution)/shard_map/ppermute | solution.py:115
  63.8 21.3 %collective-permute-start.26 = (bf16[1,128,1024]{2,1,0:T(8,128)(2,1)S(1)}, bf16[1,128,1024]{2,1,0:T(8,128)(2,1)S(1)}, u32[]{:S(2)}, u32[]{:S(2)}) collective-permute-start(bf16[1,128,1024]{2,1,0:T(8,128)(2,1)S(1)} %fusion.95), channel_id=1, source_target_pairs={{0,8},{4,12},{8,0},{12,4},{1,9},{5,13},{9,1},{13,5},{2,10},{6,14},... | collective-permute-start | bytes 786440 | tf_op jit(solution)/shard_map/ppermute | solution.py:131
  64.8 25.9 %collective-permute-start.22 = (bf16[1,128,1024]{2,1,0:T(8,128)(2,1)S(1)}, bf16[1,128,1024]{2,1,0:T(8,128)(2,1)S(1)}, u32[]{:S(2)}, u32[]{:S(2)}) collective-permute-start(bf16[1,128,1024]{2,1,0:T(8,128)(2,1)S(1)} %fusion.95), channel_id=1, source_target_pairs={{0,12},{4,0},{8,4},{12,8},{1,13},{5,1},{9,5},{13,9},{2,14},{6,2},{... | collective-permute-start | bytes 786440 | tf_op jit(solution)/shard_map/ppermute | solution.py:131
  68.6 6.4 %collective-permute-start.16 = (bf16[64,1024]{1,0:T(8,128)(2,1)S(1)}, bf16[64,1024]{1,0:T(8,128)(2,1)S(1)}, u32[]{:S(2)}, u32[]{:S(2)}) collective-permute-start(bf16[64,1024]{1,0:T(8,128)(2,1)S(1)} %convolution_convert_fusion.17), channel_id=1, source_target_pairs={{0,2},{1,3},{2,0},{3,1},{4,6},{5,7},{6,4},{7,5},{8,10},{9,11},{10,... | collective-permute-start | bytes 393224 | tf_op jit(solution)/shard_map/ppermute | solution.py:140
  69.2 7.8 %collective-permute-start.17 = (bf16[64,1024]{1,0:T(8,128)(2,1)S(1)}, bf16[64,1024]{1,0:T(8,128)(2,1)S(1)}, u32[]{:S(2)}, u32[]{:S(2)}) collective-permute-start(bf16[64,1024]{1,0:T(8,128)(2,1)S(1)} %convolution_convert_fusion.16), channel_id=1, source_target_pairs={{0,3},{1,2},{2,1},{3,0},{4,7},{5,6},{6,5},{7,4},{8,11},{9,10},{10,... | collective-permute-start | bytes 393224 | tf_op jit(solution)/shard_map/ppermute | solution.py:140
  71.0 15.8 %collective-permute-start.18 = (bf16[1,128,1024]{2,1,0:T(8,128)(2,1)S(1)}, bf16[1,128,1024]{2,1,0:T(8,128)(2,1)S(1)}, u32[]{:S(2)}, u32[]{:S(2)}) collective-permute-start(bf16[1,128,1024]{2,1,0:T(8,128)(2,1)S(1)} %fusion.95), channel_id=1, source_target_pairs={{0,4},{4,8},{8,12},{12,0},{1,5},{5,9},{9,13},{13,1},{2,6},{6,10},{... | collective-permute-start | bytes 786440 | tf_op jit(solution)/shard_map/ppermute | solution.py:131
  85.9 20.8 %collective-permute-start.27 = (bf16[64,1024]{1,0:T(8,128)(2,1)}, bf16[64,1024]{1,0:T(8,128)(2,1)S(1)}, u32[]{:S(2)}, u32[]{:S(2)}) collective-permute-start(bf16[64,1024]{1,0:T(8,128)(2,1)} %convolution_convert_fusion.6), channel_id=1, source_target_pairs={{0,1},{1,0},{2,3},{3,2},{4,5},{5,4},{6,7},{7,6},{8,9},{9,8},{10,11... | collective-permute-start | bytes 393224 | tf_op jit(solution)/shard_map/ppermute | solution.py:140
  86.7 20.0 %collective-permute-start.28 = (bf16[64,1024]{1,0:T(8,128)(2,1)}, bf16[64,1024]{1,0:T(8,128)(2,1)}, u32[]{:S(2)}, u32[]{:S(2)}) collective-permute-start(bf16[64,1024]{1,0:T(8,128)(2,1)} %convolution_convert_fusion.5), channel_id=1, source_target_pairs={{0,2},{1,3},{2,0},{3,1},{4,6},{5,7},{6,4},{7,5},{8,10},{9,11},{10,... | collective-permute-start | bytes 393224 | tf_op jit(solution)/shard_map/ppermute | solution.py:140
  87.7 8.4 %collective-permute-start.20 = (bf16[64,1024]{1,0:T(8,128)(2,1)S(1)}, bf16[64,1024]{1,0:T(8,128)(2,1)S(1)}, u32[]{:S(2)}, u32[]{:S(2)}) collective-permute-start(bf16[64,1024]{1,0:T(8,128)(2,1)S(1)} %convolution_convert_fusion.13), channel_id=1, source_target_pairs={{0,2},{1,3},{2,0},{3,1},{4,6},{5,7},{6,4},{7,5},{8,10},{9,11},{10,... | collective-permute-start | bytes 393224 | tf_op jit(solution)/shard_map/ppermute | solution.py:140
  90.7 7.4 %collective-permute-start.21 = (bf16[64,1024]{1,0:T(8,128)(2,1)S(1)}, bf16[64,1024]{1,0:T(8,128)(2,1)S(1)}, u32[]{:S(2)}, u32[]{:S(2)}) collective-permute-start(bf16[64,1024]{1,0:T(8,128)(2,1)S(1)} %convolution_convert_fusion.12), channel_id=1, source_target_pairs={{0,3},{1,2},{2,1},{3,0},{4,7},{5,6},{6,5},{7,4},{8,11},{9,10},{10,... | collective-permute-start | bytes 393224 | tf_op jit(solution)/shard_map/ppermute | solution.py:140
  91.7 9.8 %collective-permute-start.23 = (bf16[64,1024]{1,0:T(8,128)(2,1)S(1)}, bf16[64,1024]{1,0:T(8,128)(2,1)S(1)}, u32[]{:S(2)}, u32[]{:S(2)}) collective-permute-start(bf16[64,1024]{1,0:T(8,128)(2,1)S(1)} %convolution_convert_fusion.10), channel_id=1, source_target_pairs={{0,1},{1,0},{2,3},{3,2},{4,5},{5,4},{6,7},{7,6},{8,9},{9,8},{10,11... | collective-permute-start | bytes 393224 | tf_op jit(solution)/shard_map/ppermute | solution.py:140
  96.0 7.0 %collective-permute-start.24 = (bf16[64,1024]{1,0:T(8,128)(2,1)S(1)}, bf16[64,1024]{1,0:T(8,128)(2,1)S(1)}, u32[]{:S(2)}, u32[]{:S(2)}) collective-permute-start(bf16[64,1024]{1,0:T(8,128)(2,1)S(1)} %convolution_convert_fusion.9), channel_id=1, source_target_pairs={{0,2},{1,3},{2,0},{3,1},{4,6},{5,7},{6,4},{7,5},{8,10},{9,11},{10,... | collective-permute-start | bytes 393224 | tf_op jit(solution)/shard_map/ppermute | solution.py:140
  118.5 20.3 %collective-permute-start.36 = (bf16[64,4096]{1,0:T(8,128)(2,1)S(1)}, bf16[64,4096]{1,0:T(8,128)(2,1)S(1)}, u32[]{:S(2)}, u32[]{:S(2)}) collective-permute-start(bf16[64,4096]{1,0:T(8,128)(2,1)S(1)} %fusion.21), channel_id=1, source_target_pairs={{0,4},{4,8},{8,12},{12,0},{1,5},{5,9},{9,13},{13,1},{2,6},{6,10},{... | collective-permute-start | bytes 1572872 | tf_op jit(solution)/shard_map/ppermute | solution.py:222
  124.3 8.6 %collective-permute-start.31 = (bf16[1,32,4096]{2,1,0:T(8,128)(2,1)S(1)}, bf16[1,32,4096]{2,1,0:T(8,128)(2,1)S(1)}, u32[]{:S(2)}, u32[]{:S(2)}) collective-permute-start(bf16[1,32,4096]{2,1,0:T(8,128)(2,1)S(1)} %fusion.106), channel_id=1, source_target_pairs={{0,2},{1,3},{2,0},{3,1},{4,6},{5,7},{6,4},{7,5},{8,10},{9,11},{10,... | collective-permute-start | bytes 786440 | tf_op jit(solution)/shard_map/ppermute | solution.py:211
  128.9 6.4 %collective-permute-start.33 = (bf16[64,4096]{1,0:T(8,128)(2,1)S(1)}, bf16[64,4096]{1,0:T(8,128)(2,1)S(1)}, u32[]{:S(2)}, u32[]{:S(2)}) collective-permute-start(bf16[64,4096]{1,0:T(8,128)(2,1)S(1)} %convolution_convert_fusion.1), channel_id=1, source_target_pairs={{0,1},{1,0},{2,3},{3,2},{4,5},{5,4},{6,7},{7,6},{8,9},{9,8},{10,11... | collective-permute-start | bytes 1572872 | tf_op jit(solution)/shard_map/ppermute | solution.py:202
  132.9 15.7 %collective-permute-start.32 = (bf16[32,4096]{1,0:T(8,128)(2,1)S(1)}, bf16[32,4096]{1,0:T(8,128)(2,1)S(1)}, u32[]{:S(2)}, u32[]{:S(2)}) collective-permute-start(bf16[32,4096]{1,0:T(8,128)(2,1)S(1)} %fusion.109), channel_id=1, source_target_pairs={{0,8},{4,12},{8,0},{12,4},{1,9},{5,13},{9,1},{13,5},{2,10},{6,14},... | collective-permute-start | bytes 786440 | tf_op jit(solution)/shard_map/ppermute | solution.py:228
  135.7 7.3 %collective-permute-start.34 = (bf16[1,32,4096]{2,1,0:T(8,128)(2,1)S(1)}, bf16[1,32,4096]{2,1,0:T(8,128)(2,1)S(1)}, u32[]{:S(2)}, u32[]{:S(2)}) collective-permute-start(bf16[1,32,4096]{2,1,0:T(8,128)(2,1)S(1)} %fusion.107), channel_id=1, source_target_pairs={{0,2},{1,3},{2,0},{3,1},{4,6},{5,7},{6,4},{7,5},{8,10},{9,11},{10,... | collective-permute-start | bytes 786440 | tf_op jit(solution)/shard_map/ppermute | solution.py:211
  143.0 9.9 %collective-permute-start.35 = (bf16[32,4096]{1,0:T(8,128)(2,1)S(1)}, bf16[32,4096]{1,0:T(8,128)(2,1)S(1)}, u32[]{:S(2)}, u32[]{:S(2)}) collective-permute-start(bf16[32,4096]{1,0:T(8,128)(2,1)S(1)} %fusion.110), channel_id=1, source_target_pairs={{0,12},{4,0},{8,4},{12,8},{1,13},{5,1},{9,5},{13,9},{2,14},{6,2},{... | collective-permute-start | bytes 786440 | tf_op jit(solution)/shard_map/ppermute | solution.py:228
  145.4 7.5 %collective-permute-start.38 = (bf16[1,32,4096]{2,1,0:T(8,128)(2,1)S(1)}, bf16[1,32,4096]{2,1,0:T(8,128)(2,1)S(1)}, u32[]{:S(2)}, u32[]{:S(2)}) collective-permute-start(bf16[1,32,4096]{2,1,0:T(8,128)(2,1)S(1)} %fusion.108), channel_id=1, source_target_pairs={{0,2},{1,3},{2,0},{3,1},{4,6},{5,7},{6,4},{7,5},{8,10},{9,11},{10,... | collective-permute-start | bytes 786440 | tf_op jit(solution)/shard_map/ppermute | solution.py:211
  (27 other events, 310.9 us)

commit v3 on v2

--- a/solution.py
+++ b/solution.py
@@ -126,9 +126,14 @@
             pickers.append(picker_of(jnp.any(block == (e ^ k), axis=1), capacity).astype(bf16))
     pickers = lax.optimization_barrier(pickers)
     turns = sorted(range(ctx_count), key=lambda k: min(k, ctx_count - k))
-    chunks = {}
+    chunks, moved = {}, {}
     for k in turns:
-        chunk = lax.ppermute(stream, "ctx", rotation(ctx_count, k)) if k else stream
+        if k == turns[-1] and ctx_count > 2:
+            chunk = lax.optimization_barrier((stream, moved[turns[0]][exp_count // 2]))[0]
+        else:
+            chunk = stream
+        if k:
+            chunk = lax.ppermute(chunk, "ctx", rotation(ctx_count, k))
         pieces = []
         for m in range(exp_count):
             picked = [
@@ -139,6 +144,7 @@
             if m:
                 piece = lax.ppermute(piece, "exp", [(i, i ^ m) for i in range(exp_count)])
             pieces.append(piece)
+        moved[k] = pieces
         chunks[k] = jnp.concatenate(pieces)
 
     gate_here, up_here, down_here = expert_gate[0], expert_up[0], expert_down[0]

time: 154 us -> 153 us (level)
    ppermute x12, waiting for transfers between devices: 12.7 us -> 8.24 us  [local(): piece = lax.ppermute(piece, 'exp', [(i, i ^ m) for i in range(exp_count)])]
    ppermute x3, waiting for transfers between devices: 2.82 us -> 5.5 us  [local(): chunk = lax.ppermute(chunk, 'ctx', rotation(ctx_count, k))]
    ppermute x12, starting transfers between devices: 6.84 us -> 8.98 us  [local(): piece = lax.ppermute(piece, 'exp', [(i, i ^ m) for i in range(exp_count)])]
    ppermute x3, starting transfers between devices: 3.4 us -> 1.5 us  [contribution(): lax.ppermute(sent, 'exp', [(i, i ^ 1 << level) for i in range(exp_count)])]
  transfers between devices with their start and end apart: 39 -> 39, of which waited for: 17 -> 15; matrix products, arithmetic and copies ran while one was open for 30% -> 31% of each run, Pallas kernels for 0% -> 0%
where the time goes in v3:
time: 153 us; the launch traced here: 152 us
  waiting for transfers between devices  52.2 us (34%)
  matrix products  41.8 us (27%)
  starting transfers between devices  40.3 us (26%)
  other arithmetic  13.6 us (9%)
  local copies, waits for them, and re-layouts  3.03 us (2%)
    ppermute x12, starting transfers between devices, gather_rotated(): lax.ppermute(block, 'ctx', rotation(count, k))  19.8 us
    ppermute x12, waiting for transfers between devices, gather_rotated(): lax.ppermute(block, 'ctx', rotation(count, k))  13.8 us
    ppermute x12, starting transfers between devices, local(): piece = lax.ppermute(piece, 'exp', [(i, i ^ m) for i in range(exp_count)])  8.98 us
    ppermute x12, waiting for transfers between devices, local(): piece = lax.ppermute(piece, 'exp', [(i, i ^ m) for i in range(exp_count)])  8.24 us
    ppermute x3, waiting for transfers between devices, contribution(): lax.ppermute(sent, 'exp', [(i, i ^ 1 << level) for i in range(exp_count)])  8.21 us
    dot_general x3, matrix products, local(): gives = jnp.dot(rows, down_here, preferred_element_type=f32)  8.09 us
    ppermute x1, waiting for transfers between devices, local(): lax.ppermute(sent, 'exp', [(i, i ^ 1 << level) for i in range(exp_count)])  7.16 us
    ppermute x2, waiting for transfers between devices, local(): output += lax.ppermute(part, 'ctx', rotation(ctx_count, k)).astype(f32)  7.05 us
  transfers between devices with their start and end apart: 39, of which 15 were waited for; matrix products, arithmetic and copies ran while one was open for 31% of the time, Pallas kernels for 0%

profile of v3, /device:TPU:0, one launch (start us, length us, event | category | flops | bytes accessed | tf_op | source)
XLA Modules:
  0.0 152.1 jit_solution(1725409102596300919)
XLA Ops:
  0.0 3.0 %collective-permute-start.6 = (bf16[512,128]{1,0:T(8,128)(2,1)}, bf16[512,128]{1,0:T(8,128)(2,1)S(1)}, u32[]{:S(2)}, u32[]{:S(2)}) collective-permute-start(bf16[512,128]{1,0:T(8,128)(2,1)} %param.12), channel_id=1, source_target_pairs={{0,4},{4,8},{8,12},{12,0},{1,5},{5,9},{9,13},{13,1},{2,6},{6,10},{... | collective-permute-start | bytes 393224 | tf_op jit(solution)/shard_map/ppermute | solution.py:14
  3.0 2.6 %collective-permute-start.7 = (bf16[512,128]{1,0:T(8,128)(2,1)}, bf16[512,128]{1,0:T(8,128)(2,1)S(1)}, u32[]{:S(2)}, u32[]{:S(2)}) collective-permute-start(bf16[512,128]{1,0:T(8,128)(2,1)} %param.12), channel_id=1, source_target_pairs={{0,8},{4,12},{8,0},{12,4},{1,9},{5,13},{9,1},{13,5},{2,10},{6,14},... | collective-permute-start | bytes 393224 | tf_op jit(solution)/shard_map/ppermute | solution.py:14
  5.7 1.8 %collective-permute-start = (s32[128,2]{0,1:T(2,128)}, s32[128,2]{0,1:T(2,128)S(1)}, u32[]{:S(2)}, u32[]{:S(2)}) collective-permute-start(s32[128,2]{0,1:T(2,128)} %param.17), channel_id=1, source_target_pairs={{0,8},{4,12},{8,0},{12,4},{1,9},{5,13},{9,1},{13,5},{2,10},{6,14},... | collective-permute-start | bytes 3080 | tf_op jit(solution)/shard_map/ppermute | solution.py:14
  7.5 1.9 %collective-permute-start.2 = (s32[128,2]{0,1:T(2,128)}, s32[128,2]{0,1:T(2,128)S(1)}, u32[]{:S(2)}, u32[]{:S(2)}) collective-permute-start(s32[128,2]{0,1:T(2,128)} %param.17), channel_id=1, source_target_pairs={{0,12},{4,0},{8,4},{12,8},{1,13},{5,1},{9,5},{13,9},{2,14},{6,2},{... | collective-permute-start | bytes 3080 | tf_op jit(solution)/shard_map/ppermute | solution.py:14
  16.8 2.0 %collective-permute-start.4 = (bf16[512,128]{0,1:T(8,128)(2,1)S(1)}, bf16[512,128]{0,1:T(8,128)(2,1)S(1)}, u32[]{:S(2)}, u32[]{:S(2)}) collective-permute-start(bf16[512,128]{0,1:T(8,128)(2,1)S(1)} %copy.29), channel_id=1, source_target_pairs={{0,8},{4,12},{8,0},{12,4},{1,9},{5,13},{9,1},{13,5},{2,10},{6,14},... | collective-permute-start | bytes 393224 | tf_op jit(solution)/shard_map/ppermute | solution.py:14
  23.6 1.6 %collective-permute-start.14 = (bf16[128,1024]{1,0:T(8,128)(2,1)}, bf16[128,1024]{1,0:T(8,128)(2,1)S(1)}, u32[]{:S(2)}, u32[]{:S(2)}) collective-permute-start(bf16[128,1024]{1,0:T(8,128)(2,1)} %param.15), channel_id=1, source_target_pairs={{0,0},{1,4},{2,8},{3,12},{4,1},{5,5},{6,9},{7,13},{8,2},{9,6},{10,... | collective-permute-start | bytes 786440 | tf_op jit(solution)/shard_map/ppermute | solution.py:62
  26.2 4.3 %fusion.204 = (f32[4,128]{1,0:T(4,128)S(1)}, bf16[4,128,2048]{1,2,0:T(8,128)(2,1)}) fusion(pred[128,2048]{0,1:T(8,128)(4,1)S(1)} %broadcast_compare_fusion, bf16[2048,128]{1,0:T(8,128)(2,1)S(1)} %pad_maximum_fusion, bf16[128,512]{1,0:T(8,128)(2,1)} %param.11), kind=kOutput, calls=%fused_computation.302 | convolution fusion | flops 274728960 | bytes 3016704 | tf_op jit(solution)/shard_map/sub | solution.py:84
  30.4 5.0 %collective-permute-done.4 = bf16[512,128]{0,1:T(8,128)(2,1)S(1)} collective-permute-done((bf16[512,128]{0,1:T(8,128)(2,1)S(1)}, bf16[512,128]{0,1:T(8,128)(2,1)S(1)}, u32[]{:S(2)}, u32[]{:S(2)}) %collective-permute-start.4) | collective-permute-done | bytes 131104 | tf_op jit(solution)/shard_map/ppermute | solution.py:14
  35.4 2.0 %fusion.78 = bf16[128,4,128]{0,2,1:T(8,128)(2,1)S(1)} fusion(bf16[4,128,2048]{1,2,0:T(8,128)(2,1)} %get-tuple-element.86, bf16[512,128]{0,1:T(8,128)(2,1)S(1)} %collective-permute-done.5, bf16[512,128]{0,1:T(8,128)(2,1)S(1)} %collective-permute-done.4, bf16[512,128]{0,1:T(8,128)(2,1)S(1)} %collective-permute-done.3, bf16[512,128]{0,1:T(8,128)(2,1)S(1)} %copy.29, ...), kind=kOutput, calls=%fused_computation.59 | convolution fusion | flops 270663680 | bytes 2754560 | tf_op jit(solution)/shard_map/qtj,jd->tqd/dot_general | solution.py:86
  37.5 3.4 %collective-permute-start.9 = (bf16[128,512]{0,1:T(8,128)(2,1)S(1)}, bf16[128,512]{0,1:T(8,128)(2,1)S(1)}, u32[]{:S(2)}, u32[]{:S(2)}) collective-permute-start(bf16[128,512]{0,1:T(8,128)(2,1)S(1)} %bitcast.293), channel_id=1, source_target_pairs={{0,4},{4,8},{8,12},{12,0},{1,5},{5,9},{9,13},{13,1},{2,6},{6,10},{... | collective-permute-start | bytes 393224 | tf_op jit(solution)/shard_map/ppermute | solution.py:14
  40.9 2.4 %collective-permute-start.11 = (bf16[128,512]{0,1:T(8,128)(2,1)S(1)}, bf16[128,512]{0,1:T(8,128)(2,1)S(1)}, u32[]{:S(2)}, u32[]{:S(2)}) collective-permute-start(bf16[128,512]{0,1:T(8,128)(2,1)S(1)} %bitcast.295), channel_id=1, source_target_pairs={{0,12},{4,0},{8,4},{12,8},{1,13},{5,1},{9,5},{13,9},{2,14},{6,2},{... | collective-permute-start | bytes 393224 | tf_op jit(solution)/shard_map/ppermute | solution.py:14
  43.3 1.7 %collective-permute-done.9 = bf16[128,512]{0,1:T(8,128)(2,1)S(1)} collective-permute-done((bf16[128,512]{0,1:T(8,128)(2,1)S(1)}, bf16[128,512]{0,1:T(8,128)(2,1)S(1)}, u32[]{:S(2)}, u32[]{:S(2)}) %collective-permute-start.9) | collective-permute-done | bytes 131104 | tf_op jit(solution)/shard_map/ppermute | solution.py:14
  45.1 7.1 %collective-permute-done.10 = bf16[128,512]{0,1:T(8,128)(2,1)S(1)} collective-permute-done((bf16[128,512]{0,1:T(8,128)(2,1)S(1)}, bf16[128,512]{0,1:T(8,128)(2,1)S(1)}, u32[]{:S(2)}, u32[]{:S(2)}) %collective-permute-start.10) | collective-permute-done | bytes 131104 | tf_op jit(solution)/shard_map/ppermute | solution.py:14
  56.5 7.2 %collective-permute-done.13 = bf16[1,128,1024]{2,1,0:T(8,128)(2,1)S(1)} collective-permute-done((bf16[1,128,1024]{2,1,0:T(8,128)(2,1)S(1)}, bf16[1,128,1024]{2,1,0:T(8,128)(2,1)S(1)}, u32[]{:S(2)}, u32[]{:S(2)}) %collective-permute-start.13) | collective-permute-done | bytes 262176 | tf_op jit(solution)/shard_map/ppermute | solution.py:115
  63.8 2.9 %collective-permute-start.22 = (bf16[1,128,1024]{2,1,0:T(8,128)(2,1)S(1)}, bf16[1,128,1024]{2,1,0:T(8,128)(2,1)S(1)}, u32[]{:S(2)}, u32[]{:S(2)}) collective-permute-start(bf16[1,128,1024]{2,1,0:T(8,128)(2,1)S(1)} %fusion.95), channel_id=1, source_target_pairs={{0,12},{4,0},{8,4},{12,8},{1,13},{5,1},{9,5},{13,9},{2,14},{6,2},{... | collective-permute-start | bytes 786440 | tf_op jit(solution)/shard_map/ppermute | solution.py:136
  66.9 1.8 %collective-permute-start.16 = (bf16[64,1024]{1,0:T(8,128)(2,1)S(1)}, bf16[64,1024]{1,0:T(8,128)(2,1)S(1)}, u32[]{:S(2)}, u32[]{:S(2)}) collective-permute-start(bf16[64,1024]{1,0:T(8,128)(2,1)S(1)} %convolution_convert_fusion.17), channel_id=1, source_target_pairs={{0,2},{1,3},{2,0},{3,1},{4,6},{5,7},{6,4},{7,5},{8,10},{9,11},{10,... | collective-permute-start | bytes 393224 | tf_op jit(solution)/shard_map/ppermute | solution.py:145
  69.8 2.5 %collective-permute-done.16 = bf16[64,1024]{1,0:T(8,128)(2,1)S(1)} collective-permute-done((bf16[64,1024]{1,0:T(8,128)(2,1)S(1)}, bf16[64,1024]{1,0:T(8,128)(2,1)S(1)}, u32[]{:S(2)}, u32[]{:S(2)}) %collective-permute-start.16) | collective-permute-done | bytes 131104 | tf_op jit(solution)/shard_map/ppermute | solution.py:145
  74.6 3.3 %fusion.37 = f32[256,1792]{1,0:T(8,128)S(1)} fusion(bf16[256,1024]{1,0:T(8,128)(2,1)S(1)} %get-tuple-element.64, bf16[1,4096,1792]{2,1,0:T(8,128)(2,1)} %param.20, s32[]{:T(128)S(6)} %select_n.268), kind=kOutput, calls=%fused_computation.32 | convolution fusion | flops 939524096 | bytes 6029316 | tf_op jit(solution)/shard_map/dot_general | solution.py:159
  84.1 5.5 %collective-permute-done.26 = bf16[1,128,1024]{2,1,0:T(8,128)(2,1)S(1)} collective-permute-done((bf16[1,128,1024]{2,1,0:T(8,128)(2,1)S(1)}, bf16[1,128,1024]{2,1,0:T(8,128)(2,1)S(1)}, u32[]{:S(2)}, u32[]{:S(2)}) %collective-permute-start.26) | collective-permute-done | bytes 262176 | tf_op jit(solution)/shard_map/ppermute | solution.py:136
  93.1 2.2 %collective-permute-done.21 = bf16[64,1024]{1,0:T(8,128)(2,1)S(1)} collective-permute-done((bf16[64,1024]{1,0:T(8,128)(2,1)S(1)}, bf16[64,1024]{1,0:T(8,128)(2,1)S(1)}, u32[]{:S(2)}, u32[]{:S(2)}) %collective-permute-start.21) | collective-permute-done | bytes 131104 | tf_op jit(solution)/shard_map/ppermute | solution.py:145
  104.4 2.3 %collective-permute-done.29 = bf16[64,1024]{1,0:T(8,128)(2,1)} collective-permute-done((bf16[64,1024]{1,0:T(8,128)(2,1)}, bf16[64,1024]{1,0:T(8,128)(2,1)}, u32[]{:S(2)}, u32[]{:S(2)}) %collective-permute-start.29) | collective-permute-done | bytes 131104 | tf_op jit(solution)/shard_map/ppermute | solution.py:145
  110.3 3.4 %fusion.61 = f32[256,1792]{1,0:T(8,128)S(1)} fusion(f32[256,1792]{1,0:T(8,128)S(1)} %fusion.55, bf16[256,1024]{1,0:T(8,128)(2,1)S(1)} %get-tuple-element.58, bf16[1,4096,1792]{2,1,0:T(8,128)(2,1)} %param.19, s32[]{:T(128)S(6)} %select_n.271), kind=kOutput, calls=%fused_computation.48 | convolution fusion | flops 939982848 | bytes 7864324 | tf_op jit(solution)/shard_map/dot_general | solution.py:158
  114.4 2.9 %fusion.21 = bf16[64,4096]{1,0:T(8,128)(2,1)S(1)} fusion(bf16[1,1792,4096]{2,1,0:T(8,128)(2,1)S(1)} %bitcast.282, bf16[256,1792]{1,0:T(8,128)(2,1)S(1)} %multiply_convert_fusion, s32[]{:T(128)S(6)} %select_n.273), kind=kOutput, calls=%fused_computation.16 | convolution fusion | flops 939786240 | bytes 15433732 | tf_op jit(solution)/shard_map/dot_general | solution.py:225
  117.8 2.7 %fusion.18 = bf16[64,4096]{1,0:T(8,128)(2,1)S(1)} fusion(bf16[1,1792,4096]{2,1,0:T(8,128)(2,1)S(1)} %bitcast.282, f32[64]{0:T(128)S(1)} %add_divide_fusion.2, bf16[256,1792]{1,0:T(8,128)(2,1)S(1)} %multiply_convert_fusion, s32[]{:T(128)S(6)} %select_n.275), kind=kOutput, calls=%fused_computation.15 | convolution fusion | flops 940048384 | bytes 15434244 | tf_op jit(solution)/shard_map/dot_general | solution.py:231
  123.6 2.7 %fusion.15 = bf16[64,4096]{1,0:T(8,128)(2,1)S(1)} fusion(bf16[1,1792,4096]{2,1,0:T(8,128)(2,1)S(1)} %bitcast.282, f32[64]{0:T(128)S(1)} %add_divide_fusion.1, bf16[256,1792]{1,0:T(8,128)(2,1)S(1)} %multiply_convert_fusion, s32[]{:T(128)S(6)} %select_n.279), kind=kOutput, calls=%fused_computation.14 | convolution fusion | flops 940048384 | bytes 15434244 | tf_op jit(solution)/shard_map/dot_general | solution.py:231
  126.6 4.9 %collective-permute-done.31 = bf16[1,32,4096]{2,1,0:T(8,128)(2,1)S(1)} collective-permute-done((bf16[1,32,4096]{2,1,0:T(8,128)(2,1)S(1)}, bf16[1,32,4096]{2,1,0:T(8,128)(2,1)S(1)}, u32[]{:S(2)}, u32[]{:S(2)}) %collective-permute-start.31) | collective-permute-done | bytes 262176 | tf_op jit(solution)/shard_map/ppermute | solution.py:217
  131.6 2.6 %collective-permute-start.32 = (bf16[32,4096]{1,0:T(8,128)(2,1)S(1)}, bf16[32,4096]{1,0:T(8,128)(2,1)S(1)}, u32[]{:S(2)}, u32[]{:S(2)}) collective-permute-start(bf16[32,4096]{1,0:T(8,128)(2,1)S(1)} %fusion.109), channel_id=1, source_target_pairs={{0,8},{4,12},{8,0},{12,4},{1,9},{5,13},{9,1},{13,5},{2,10},{6,14},... | collective-permute-start | bytes 786440 | tf_op jit(solution)/shard_map/ppermute | solution.py:234
  135.2 2.7 %fusion.1 = f32[64,4096]{1,0:T(8,128)S(1)} fusion(bf16[1,1792,4096]{2,1,0:T(8,128)(2,1)S(1)} %bitcast.282, bf16[256,1792]{1,0:T(8,128)(2,1)S(1)} %multiply_convert_fusion, s32[]{:T(128)S(6)} %select_n.281), kind=kOutput, calls=%fused_computation.1 | convolution fusion | flops 939524096 | bytes 15958020 | tf_op jit(solution)/shard_map/dot_general | solution.py:236
  138.6 3.3 %collective-permute-done.34 = bf16[1,32,4096]{2,1,0:T(8,128)(2,1)S(1)} collective-permute-done((bf16[1,32,4096]{2,1,0:T(8,128)(2,1)S(1)}, bf16[1,32,4096]{2,1,0:T(8,128)(2,1)S(1)}, u32[]{:S(2)}, u32[]{:S(2)}) %collective-permute-start.34) | collective-permute-done | bytes 262176 | tf_op jit(solution)/shard_map/ppermute | solution.py:217
  141.9 1.6 %collective-permute-start.35 = (bf16[32,4096]{1,0:T(8,128)(2,1)S(1)}, bf16[32,4096]{1,0:T(8,128)(2,1)S(1)}, u32[]{:S(2)}, u32[]{:S(2)}) collective-permute-start(bf16[32,4096]{1,0:T(8,128)(2,1)S(1)} %fusion.110), channel_id=1, source_target_pairs={{0,12},{4,0},{8,4},{12,8},{1,13},{5,1},{9,5},{13,9},{2,14},{6,2},{... | collective-permute-start | bytes 786440 | tf_op jit(solution)/shard_map/ppermute | solution.py:234
  144.3 2.8 %collective-permute-done.32 = bf16[32,4096]{1,0:T(8,128)(2,1)S(1)} collective-permute-done((bf16[32,4096]{1,0:T(8,128)(2,1)S(1)}, bf16[32,4096]{1,0:T(8,128)(2,1)S(1)}, u32[]{:S(2)}, u32[]{:S(2)}) %collective-permute-start.32) | collective-permute-done | bytes 262176 | tf_op jit(solution)/shard_map/ppermute | solution.py:234
  147.0 4.3 %collective-permute-done.35 = bf16[32,4096]{1,0:T(8,128)(2,1)S(1)} collective-permute-done((bf16[32,4096]{1,0:T(8,128)(2,1)S(1)}, bf16[32,4096]{1,0:T(8,128)(2,1)S(1)}, u32[]{:S(2)}, u32[]{:S(2)}) %collective-permute-start.35) | collective-permute-done | bytes 262176 | tf_op jit(solution)/shard_map/ppermute | solution.py:234
  (224 shorter events, 50.6 us)
Async XLA Ops:
  0.0 23.3 %collective-permute-start.6 = (bf16[512,128]{1,0:T(8,128)(2,1)}, bf16[512,128]{1,0:T(8,128)(2,1)S(1)}, u32[]{:S(2)}, u32[]{:S(2)}) collective-permute-start(bf16[512,128]{1,0:T(8,128)(2,1)} %param.12), channel_id=1, source_target_pairs={{0,4},{4,8},{8,12},{12,0},{1,5},{5,9},{9,13},{13,1},{2,6},{6,10},{... | collective-permute-start | bytes 393224 | tf_op jit(solution)/shard_map/ppermute | solution.py:14
  3.0 20.6 %collective-permute-start.7 = (bf16[512,128]{1,0:T(8,128)(2,1)}, bf16[512,128]{1,0:T(8,128)(2,1)S(1)}, u32[]{:S(2)}, u32[]{:S(2)}) collective-permute-start(bf16[512,128]{1,0:T(8,128)(2,1)} %param.12), channel_id=1, source_target_pairs={{0,8},{4,12},{8,0},{12,4},{1,9},{5,13},{9,1},{13,5},{2,10},{6,14},... | collective-permute-start | bytes 393224 | tf_op jit(solution)/shard_map/ppermute | solution.py:14
  5.6 9.1 %collective-permute-start.1 = (s32[128,2]{0,1:T(2,128)}, s32[128,2]{0,1:T(2,128)S(1)}, u32[]{:S(2)}, u32[]{:S(2)}) collective-permute-start(s32[128,2]{0,1:T(2,128)} %param.17), channel_id=1, source_target_pairs={{0,4},{4,8},{8,12},{12,0},{1,5},{5,9},{9,13},{13,1},{2,6},{6,10},{... | collective-permute-start | bytes 3080 | tf_op jit(solution)/shard_map/ppermute | solution.py:14
  5.7 9.7 %collective-permute-start = (s32[128,2]{0,1:T(2,128)}, s32[128,2]{0,1:T(2,128)S(1)}, u32[]{:S(2)}, u32[]{:S(2)}) collective-permute-start(s32[128,2]{0,1:T(2,128)} %param.17), channel_id=1, source_target_pairs={{0,8},{4,12},{8,0},{12,4},{1,9},{5,13},{9,1},{13,5},{2,10},{6,14},... | collective-permute-start | bytes 3080 | tf_op jit(solution)/shard_map/ppermute | solution.py:14
  7.5 9.2 %collective-permute-start.2 = (s32[128,2]{0,1:T(2,128)}, s32[128,2]{0,1:T(2,128)S(1)}, u32[]{:S(2)}, u32[]{:S(2)}) collective-permute-start(s32[128,2]{0,1:T(2,128)} %param.17), channel_id=1, source_target_pairs={{0,12},{4,0},{8,4},{12,8},{1,13},{5,1},{9,5},{13,9},{2,14},{6,2},{... | collective-permute-start | bytes 3080 | tf_op jit(solution)/shard_map/ppermute | solution.py:14
  14.7 10.6 %collective-permute-start.8 = (bf16[512,128]{1,0:T(8,128)(2,1)}, bf16[512,128]{1,0:T(8,128)(2,1)S(1)}, u32[]{:S(2)}, u32[]{:S(2)}) collective-permute-start(bf16[512,128]{1,0:T(8,128)(2,1)} %param.12), channel_id=1, source_target_pairs={{0,12},{4,0},{8,4},{12,8},{1,13},{5,1},{9,5},{13,9},{2,14},{6,2},{... | collective-permute-start | bytes 393224 | tf_op jit(solution)/shard_map/ppermute | solution.py:14
  15.4 15.1 %collective-permute-start.3 = (bf16[512,128]{0,1:T(8,128)(2,1)S(1)}, bf16[512,128]{0,1:T(8,128)(2,1)S(1)}, u32[]{:S(2)}, u32[]{:S(2)}) collective-permute-start(bf16[512,128]{0,1:T(8,128)(2,1)S(1)} %copy.29), channel_id=1, source_target_pairs={{0,4},{4,8},{8,12},{12,0},{1,5},{5,9},{9,13},{13,1},{2,6},{6,10},{... | collective-permute-start | bytes 393224 | tf_op jit(solution)/shard_map/ppermute | solution.py:14
  16.8 18.6 %collective-permute-start.4 = (bf16[512,128]{0,1:T(8,128)(2,1)S(1)}, bf16[512,128]{0,1:T(8,128)(2,1)S(1)}, u32[]{:S(2)}, u32[]{:S(2)}) collective-permute-start(bf16[512,128]{0,1:T(8,128)(2,1)S(1)} %copy.29), channel_id=1, source_target_pairs={{0,8},{4,12},{8,0},{12,4},{1,9},{5,13},{9,1},{13,5},{2,10},{6,14},... | collective-permute-start | bytes 393224 | tf_op jit(solution)/shard_map/ppermute | solution.py:14
  23.3 12.1 %collective-permute-start.5 = (bf16[512,128]{0,1:T(8,128)(2,1)S(1)}, bf16[512,128]{0,1:T(8,128)(2,1)S(1)}, u32[]{:S(2)}, u32[]{:S(2)}) collective-permute-start(bf16[512,128]{0,1:T(8,128)(2,1)S(1)} %copy.29), channel_id=1, source_target_pairs={{0,12},{4,0},{8,4},{12,8},{1,13},{5,1},{9,5},{13,9},{2,14},{6,2},{... | collective-permute-start | bytes 393224 | tf_op jit(solution)/shard_map/ppermute | solution.py:14
  23.6 32.9 %collective-permute-start.14 = (bf16[128,1024]{1,0:T(8,128)(2,1)}, bf16[128,1024]{1,0:T(8,128)(2,1)S(1)}, u32[]{:S(2)}, u32[]{:S(2)}) collective-permute-start(bf16[128,1024]{1,0:T(8,128)(2,1)} %param.15), channel_id=1, source_target_pairs={{0,0},{1,4},{2,8},{3,12},{4,1},{5,5},{6,9},{7,13},{8,2},{9,6},{10,... | collective-permute-start | bytes 786440 | tf_op jit(solution)/shard_map/ppermute | solution.py:62
  37.5 7.6 %collective-permute-start.9 = (bf16[128,512]{0,1:T(8,128)(2,1)S(1)}, bf16[128,512]{0,1:T(8,128)(2,1)S(1)}, u32[]{:S(2)}, u32[]{:S(2)}) collective-permute-start(bf16[128,512]{0,1:T(8,128)(2,1)S(1)} %bitcast.293), channel_id=1, source_target_pairs={{0,4},{4,8},{8,12},{12,0},{1,5},{5,9},{9,13},{13,1},{2,6},{6,10},{... | collective-permute-start | bytes 393224 | tf_op jit(solution)/shard_map/ppermute | solution.py:14
  40.9 11.3 %collective-permute-start.10 = (bf16[128,512]{0,1:T(8,128)(2,1)S(1)}, bf16[128,512]{0,1:T(8,128)(2,1)S(1)}, u32[]{:S(2)}, u32[]{:S(2)}) collective-permute-start(bf16[128,512]{0,1:T(8,128)(2,1)S(1)} %bitcast.294), channel_id=1, source_target_pairs={{0,8},{4,12},{8,0},{12,4},{1,9},{5,13},{9,1},{13,5},{2,10},{6,14},... | collective-permute-start | bytes 393224 | tf_op jit(solution)/shard_map/ppermute | solution.py:14
  40.9 11.3 %collective-permute-start.11 = (bf16[128,512]{0,1:T(8,128)(2,1)S(1)}, bf16[128,512]{0,1:T(8,128)(2,1)S(1)}, u32[]{:S(2)}, u32[]{:S(2)}) collective-permute-start(bf16[128,512]{0,1:T(8,128)(2,1)S(1)} %bitcast.295), channel_id=1, source_target_pairs={{0,12},{4,0},{8,4},{12,8},{1,13},{5,1},{9,5},{13,9},{2,14},{6,2},{... | collective-permute-start | bytes 393224 | tf_op jit(solution)/shard_map/ppermute | solution.py:14
  55.3 8.4 %collective-permute-start.13 = (bf16[1,128,1024]{2,1,0:T(8,128)(2,1)S(1)}, bf16[1,128,1024]{2,1,0:T(8,128)(2,1)S(1)}, u32[]{:S(2)}, u32[]{:S(2)}) collective-permute-start(bf16[1,128,1024]{2,1,0:T(8,128)(2,1)S(1)} %fusion.105), channel_id=1, source_target_pairs={{0,2},{1,3},{2,0},{3,1},{4,6},{5,7},{6,4},{7,5},{8,10},{9,11},{10,... | collective-permute-start | bytes 786440 | tf_op jit(solution)/shard_map/ppermute | solution.py:115
  63.8 15.8 %collective-permute-start.22 = (bf16[1,128,1024]{2,1,0:T(8,128)(2,1)S(1)}, bf16[1,128,1024]{2,1,0:T(8,128)(2,1)S(1)}, u32[]{:S(2)}, u32[]{:S(2)}) collective-permute-start(bf16[1,128,1024]{2,1,0:T(8,128)(2,1)S(1)} %fusion.95), channel_id=1, source_target_pairs={{0,12},{4,0},{8,4},{12,8},{1,13},{5,1},{9,5},{13,9},{2,14},{6,2},{... | collective-permute-start | bytes 786440 | tf_op jit(solution)/shard_map/ppermute | solution.py:136
  66.7 15.6 %collective-permute-start.18 = (bf16[1,128,1024]{2,1,0:T(8,128)(2,1)S(1)}, bf16[1,128,1024]{2,1,0:T(8,128)(2,1)S(1)}, u32[]{:S(2)}, u32[]{:S(2)}) collective-permute-start(bf16[1,128,1024]{2,1,0:T(8,128)(2,1)S(1)} %fusion.95), channel_id=1, source_target_pairs={{0,4},{4,8},{8,12},{12,0},{1,5},{5,9},{9,13},{13,1},{2,6},{6,10},{... | collective-permute-start | bytes 786440 | tf_op jit(solution)/shard_map/ppermute | solution.py:136
  72.3 17.4 %collective-permute-start.26 = (bf16[1,128,1024]{2,1,0:T(8,128)(2,1)S(1)}, bf16[1,128,1024]{2,1,0:T(8,128)(2,1)S(1)}, u32[]{:S(2)}, u32[]{:S(2)}) collective-permute-start(bf16[1,128,1024]{2,1,0:T(8,128)(2,1)S(1)} %fusion.95), channel_id=1, source_target_pairs={{0,8},{4,12},{8,0},{12,4},{1,9},{5,13},{9,1},{13,5},{2,10},{6,14},... | collective-permute-start | bytes 786440 | tf_op jit(solution)/shard_map/ppermute | solution.py:136
  79.8 20.8 %collective-permute-start.23 = (bf16[64,1024]{1,0:T(8,128)(2,1)S(1)}, bf16[64,1024]{1,0:T(8,128)(2,1)S(1)}, u32[]{:S(2)}, u32[]{:S(2)}) collective-permute-start(bf16[64,1024]{1,0:T(8,128)(2,1)S(1)} %convolution_convert_fusion.10), channel_id=1, source_target_pairs={{0,1},{1,0},{2,3},{3,2},{4,5},{5,4},{6,7},{7,6},{8,9},{9,8},{10,11... | collective-permute-start | bytes 393224 | tf_op jit(solution)/shard_map/ppermute | solution.py:145
  80.8 20.2 %collective-permute-start.24 = (bf16[64,1024]{1,0:T(8,128)(2,1)S(1)}, bf16[64,1024]{1,0:T(8,128)(2,1)S(1)}, u32[]{:S(2)}, u32[]{:S(2)}) collective-permute-start(bf16[64,1024]{1,0:T(8,128)(2,1)S(1)} %convolution_convert_fusion.9), channel_id=1, source_target_pairs={{0,2},{1,3},{2,0},{3,1},{4,6},{5,7},{6,4},{7,5},{8,10},{9,11},{10,... | collective-permute-start | bytes 393224 | tf_op jit(solution)/shard_map/ppermute | solution.py:145
  82.5 9.5 %collective-permute-start.19 = (bf16[64,1024]{1,0:T(8,128)(2,1)S(1)}, bf16[64,1024]{1,0:T(8,128)(2,1)S(1)}, u32[]{:S(2)}, u32[]{:S(2)}) collective-permute-start(bf16[64,1024]{1,0:T(8,128)(2,1)S(1)} %convolution_convert_fusion.14), channel_id=1, source_target_pairs={{0,1},{1,0},{2,3},{3,2},{4,5},{5,4},{6,7},{7,6},{8,9},{9,8},{10,11... | collective-permute-start | bytes 393224 | tf_op jit(solution)/shard_map/ppermute | solution.py:145
  82.8 10.3 %collective-permute-start.20 = (bf16[64,1024]{1,0:T(8,128)(2,1)S(1)}, bf16[64,1024]{1,0:T(8,128)(2,1)S(1)}, u32[]{:S(2)}, u32[]{:S(2)}) collective-permute-start(bf16[64,1024]{1,0:T(8,128)(2,1)S(1)} %convolution_convert_fusion.13), channel_id=1, source_target_pairs={{0,2},{1,3},{2,0},{3,1},{4,6},{5,7},{6,4},{7,5},{8,10},{9,11},{10,... | collective-permute-start | bytes 393224 | tf_op jit(solution)/shard_map/ppermute | solution.py:145
  92.0 9.0 %collective-permute-start.25 = (bf16[64,1024]{1,0:T(8,128)(2,1)S(1)}, bf16[64,1024]{1,0:T(8,128)(2,1)S(1)}, u32[]{:S(2)}, u32[]{:S(2)}) collective-permute-start(bf16[64,1024]{1,0:T(8,128)(2,1)S(1)} %convolution_convert_fusion.8), channel_id=1, source_target_pairs={{0,3},{1,2},{2,1},{3,0},{4,7},{5,6},{6,5},{7,4},{8,11},{9,10},{10,... | collective-permute-start | bytes 393224 | tf_op jit(solution)/shard_map/ppermute | solution.py:145
  93.0 11.3 %collective-permute-start.27 = (bf16[64,1024]{1,0:T(8,128)(2,1)}, bf16[64,1024]{1,0:T(8,128)(2,1)}, u32[]{:S(2)}, u32[]{:S(2)}) collective-permute-start(bf16[64,1024]{1,0:T(8,128)(2,1)} %convolution_convert_fusion.6), channel_id=1, source_target_pairs={{0,1},{1,0},{2,3},{3,2},{4,5},{5,4},{6,7},{7,6},{8,9},{9,8},{10,11... | collective-permute-start | bytes 393224 | tf_op jit(solution)/shard_map/ppermute | solution.py:145
  95.2 9.1 %collective-permute-start.28 = (bf16[64,1024]{1,0:T(8,128)(2,1)}, bf16[64,1024]{1,0:T(8,128)(2,1)}, u32[]{:S(2)}, u32[]{:S(2)}) collective-permute-start(bf16[64,1024]{1,0:T(8,128)(2,1)} %convolution_convert_fusion.5), channel_id=1, source_target_pairs={{0,2},{1,3},{2,0},{3,1},{4,6},{5,7},{6,4},{7,5},{8,10},{9,11},{10,... | collective-permute-start | bytes 393224 | tf_op jit(solution)/shard_map/ppermute | solution.py:145
  100.6 6.0 %collective-permute-start.29 = (bf16[64,1024]{1,0:T(8,128)(2,1)}, bf16[64,1024]{1,0:T(8,128)(2,1)}, u32[]{:S(2)}, u32[]{:S(2)}) collective-permute-start(bf16[64,1024]{1,0:T(8,128)(2,1)} %convolution_convert_fusion.4), channel_id=1, source_target_pairs={{0,3},{1,2},{2,1},{3,0},{4,7},{5,6},{6,5},{7,4},{8,11},{9,10},{10,... | collective-permute-start | bytes 393224 | tf_op jit(solution)/shard_map/ppermute | solution.py:145
  117.4 20.6 %collective-permute-start.36 = (bf16[64,4096]{1,0:T(8,128)(2,1)S(1)}, bf16[64,4096]{1,0:T(8,128)(2,1)S(1)}, u32[]{:S(2)}, u32[]{:S(2)}) collective-permute-start(bf16[64,4096]{1,0:T(8,128)(2,1)S(1)} %fusion.21), channel_id=1, source_target_pairs={{0,4},{4,8},{8,12},{12,0},{1,5},{5,9},{9,13},{13,1},{2,6},{6,10},{... | collective-permute-start | bytes 1572872 | tf_op jit(solution)/shard_map/ppermute | solution.py:228
  123.1 8.4 %collective-permute-start.31 = (bf16[1,32,4096]{2,1,0:T(8,128)(2,1)S(1)}, bf16[1,32,4096]{2,1,0:T(8,128)(2,1)S(1)}, u32[]{:S(2)}, u32[]{:S(2)}) collective-permute-start(bf16[1,32,4096]{2,1,0:T(8,128)(2,1)S(1)} %fusion.106), channel_id=1, source_target_pairs={{0,2},{1,3},{2,0},{3,1},{4,6},{5,7},{6,4},{7,5},{8,10},{9,11},{10,... | collective-permute-start | bytes 786440 | tf_op jit(solution)/shard_map/ppermute | solution.py:217
  126.6 7.7 %collective-permute-start.33 = (bf16[64,4096]{1,0:T(8,128)(2,1)S(1)}, bf16[64,4096]{1,0:T(8,128)(2,1)S(1)}, u32[]{:S(2)}, u32[]{:S(2)}) collective-permute-start(bf16[64,4096]{1,0:T(8,128)(2,1)S(1)} %convolution_convert_fusion.1), channel_id=1, source_target_pairs={{0,1},{1,0},{2,3},{3,2},{4,5},{5,4},{6,7},{7,6},{8,9},{9,8},{10,11... | collective-permute-start | bytes 1572872 | tf_op jit(solution)/shard_map/ppermute | solution.py:208
  131.6 15.4 %collective-permute-start.32 = (bf16[32,4096]{1,0:T(8,128)(2,1)S(1)}, bf16[32,4096]{1,0:T(8,128)(2,1)S(1)}, u32[]{:S(2)}, u32[]{:S(2)}) collective-permute-start(bf16[32,4096]{1,0:T(8,128)(2,1)S(1)} %fusion.109), channel_id=1, source_target_pairs={{0,8},{4,12},{8,0},{12,4},{1,9},{5,13},{9,1},{13,5},{2,10},{6,14},... | collective-permute-start | bytes 786440 | tf_op jit(solution)/shard_map/ppermute | solution.py:234
  134.6 7.3 %collective-permute-start.34 = (bf16[1,32,4096]{2,1,0:T(8,128)(2,1)S(1)}, bf16[1,32,4096]{2,1,0:T(8,128)(2,1)S(1)}, u32[]{:S(2)}, u32[]{:S(2)}) collective-permute-start(bf16[1,32,4096]{2,1,0:T(8,128)(2,1)S(1)} %fusion.107), channel_id=1, source_target_pairs={{0,2},{1,3},{2,0},{3,1},{4,6},{5,7},{6,4},{7,5},{8,10},{9,11},{10,... | collective-permute-start | bytes 786440 | tf_op jit(solution)/shard_map/ppermute | solution.py:217
  141.9 9.4 %collective-permute-start.35 = (bf16[32,4096]{1,0:T(8,128)(2,1)S(1)}, bf16[32,4096]{1,0:T(8,128)(2,1)S(1)}, u32[]{:S(2)}, u32[]{:S(2)}) collective-permute-start(bf16[32,4096]{1,0:T(8,128)(2,1)S(1)} %fusion.110), channel_id=1, source_target_pairs={{0,12},{4,0},{8,4},{12,8},{1,13},{5,1},{9,5},{13,9},{2,14},{6,2},{... | collective-permute-start | bytes 786440 | tf_op jit(solution)/shard_map/ppermute | solution.py:234
  143.8 7.5 %collective-permute-start.38 = (bf16[1,32,4096]{2,1,0:T(8,128)(2,1)S(1)}, bf16[1,32,4096]{2,1,0:T(8,128)(2,1)S(1)}, u32[]{:S(2)}, u32[]{:S(2)}) collective-permute-start(bf16[1,32,4096]{2,1,0:T(8,128)(2,1)S(1)} %fusion.108), channel_id=1, source_target_pairs={{0,2},{1,3},{2,0},{3,1},{4,6},{5,7},{6,4},{7,5},{8,10},{9,11},{10,... | collective-permute-start | bytes 786440 | tf_op jit(solution)/shard_map/ppermute | solution.py:217
  (31 other events, 329.5 us)

commit v4 on v3

--- a/solution.py
+++ b/solution.py
@@ -148,6 +148,8 @@
         chunks[k] = jnp.concatenate(pieces)
 
     gate_here, up_here, down_here = expert_gate[0], expert_up[0], expert_down[0]
+    for k in turns[-1:]:
+        chunks[k] = lax.optimization_barrier(chunks[k])
     gate_proj = up_proj = squares = logits = 0.0
     for k in turns:
         chunk = chunks[k]

time: 153 us -> 149 us (0.974)
  starting transfers between devices: 40.3 us -> 45.7 us
  other arithmetic: 13.6 us -> 9.52 us
  matrix products: 41.8 us -> 39.1 us
  waiting for transfers between devices: 52.2 us -> 50.6 us
    ppermute x12, starting transfers between devices: 19.8 us -> 24 us  [gather_rotated(): lax.ppermute(block, 'ctx', rotation(count, k))]
    ppermute x12, waiting for transfers between devices: 13.8 us -> 10.4 us  [gather_rotated(): lax.ppermute(block, 'ctx', rotation(count, k))]
    dot_general x16, matrix products: 4.77 us -> 2.8 us  [local(): jnp.dot(pickers[m * per_share + j], chunk[j], preferred_element_type=f32)]
    sub x7, other arithmetic: 2.04 us -> 0.49 us  [picker_of(): slot = jnp.cumsum(named.astype(jnp.int32)) - 1]
  transfers between devices with their start and end apart: 39 -> 39, of which waited for: 15 -> 16; matrix products, arithmetic and copies ran while one was open for 31% -> 28% of each run, Pallas kernels for 0% -> 0%
where the time goes in v4:
time: 149 us; the launch traced here: 148 us
  waiting for transfers between devices  50.6 us (34%)
  starting transfers between devices  45.7 us (31%)
  matrix products  39.1 us (26%)
  other arithmetic  9.52 us (6%)
  local copies, waits for them, and re-layouts  2.4 us (2%)
    ppermute x12, starting transfers between devices, gather_rotated(): lax.ppermute(block, 'ctx', rotation(count, k))  24 us
    ppermute x12, waiting for transfers between devices, gather_rotated(): lax.ppermute(block, 'ctx', rotation(count, k))  10.4 us
    ppermute x12, starting transfers between devices, local(): piece = lax.ppermute(piece, 'exp', [(i, i ^ m) for i in range(exp_count)])  9.33 us
    ppermute x12, waiting for transfers between devices, local(): piece = lax.ppermute(piece, 'exp', [(i, i ^ m) for i in range(exp_count)])  8.8 us
    ppermute x1, waiting for transfers between devices, local(): lax.ppermute(sent, 'exp', [(i, i ^ 1 << level) for i in range(exp_count)])  8.25 us
    dot_general x3, matrix products, local(): gives = jnp.dot(rows, down_here, preferred_element_type=f32)  8.11 us
    ppermute x3, waiting for transfers between devices, contribution(): lax.ppermute(sent, 'exp', [(i, i ^ 1 << level) for i in range(exp_count)])  7.54 us
    ppermute x2, waiting for transfers between devices, local(): output += lax.ppermute(part, 'ctx', rotation(ctx_count, k)).astype(f32)  7.18 us
  transfers between devices with their start and end apart: 39, of which 16 were waited for; matrix products, arithmetic and copies ran while one was open for 28% of the time, Pallas kernels for 0%

profile of v4, /device:TPU:0, one launch (start us, length us, event | category | flops | bytes accessed | tf_op | source)
XLA Modules:
  0.0 148.4 jit_solution(6008886980317711055)
XLA Ops:
  0.0 3.0 %collective-permute-start.6 = (bf16[512,128]{1,0:T(8,128)(2,1)}, bf16[512,128]{1,0:T(8,128)(2,1)S(1)}, u32[]{:S(2)}, u32[]{:S(2)}) collective-permute-start(bf16[512,128]{1,0:T(8,128)(2,1)} %param.12), channel_id=1, source_target_pairs={{0,4},{4,8},{8,12},{12,0},{1,5},{5,9},{9,13},{13,1},{2,6},{6,10},{... | collective-permute-start | bytes 393224 | tf_op jit(solution)/shard_map/ppermute | solution.py:14
  3.0 2.6 %collective-permute-start.7 = (bf16[512,128]{1,0:T(8,128)(2,1)}, bf16[512,128]{1,0:T(8,128)(2,1)S(1)}, u32[]{:S(2)}, u32[]{:S(2)}) collective-permute-start(bf16[512,128]{1,0:T(8,128)(2,1)} %param.12), channel_id=1, source_target_pairs={{0,8},{4,12},{8,0},{12,4},{1,9},{5,13},{9,1},{13,5},{2,10},{6,14},... | collective-permute-start | bytes 393224 | tf_op jit(solution)/shard_map/ppermute | solution.py:14
  5.7 1.8 %collective-permute-start = (s32[128,2]{0,1:T(2,128)}, s32[128,2]{0,1:T(2,128)S(1)}, u32[]{:S(2)}, u32[]{:S(2)}) collective-permute-start(s32[128,2]{0,1:T(2,128)} %param.17), channel_id=1, source_target_pairs={{0,8},{4,12},{8,0},{12,4},{1,9},{5,13},{9,1},{13,5},{2,10},{6,14},... | collective-permute-start | bytes 3080 | tf_op jit(solution)/shard_map/ppermute | solution.py:14
  7.5 1.9 %collective-permute-start.2 = (s32[128,2]{0,1:T(2,128)}, s32[128,2]{0,1:T(2,128)S(1)}, u32[]{:S(2)}, u32[]{:S(2)}) collective-permute-start(s32[128,2]{0,1:T(2,128)} %param.17), channel_id=1, source_target_pairs={{0,12},{4,0},{8,4},{12,8},{1,13},{5,1},{9,5},{13,9},{2,14},{6,2},{... | collective-permute-start | bytes 3080 | tf_op jit(solution)/shard_map/ppermute | solution.py:14
  15.8 2.0 %collective-permute-start.4 = (bf16[512,128]{0,1:T(8,128)(2,1)S(1)}, bf16[512,128]{0,1:T(8,128)(2,1)S(1)}, u32[]{:S(2)}, u32[]{:S(2)}) collective-permute-start(bf16[512,128]{0,1:T(8,128)(2,1)S(1)} %copy.29), channel_id=1, source_target_pairs={{0,8},{4,12},{8,0},{12,4},{1,9},{5,13},{9,1},{13,5},{2,10},{6,14},... | collective-permute-start | bytes 393224 | tf_op jit(solution)/shard_map/ppermute | solution.py:14
  21.6 1.6 %collective-permute-start.14 = (bf16[128,1024]{1,0:T(8,128)(2,1)}, bf16[128,1024]{1,0:T(8,128)(2,1)S(1)}, u32[]{:S(2)}, u32[]{:S(2)}) collective-permute-start(bf16[128,1024]{1,0:T(8,128)(2,1)} %param.15), channel_id=1, source_target_pairs={{0,0},{1,4},{2,8},{3,12},{4,1},{5,5},{6,9},{7,13},{8,2},{9,6},{10,... | collective-permute-start | bytes 786440 | tf_op jit(solution)/shard_map/ppermute | solution.py:62
  24.1 4.3 %fusion.204 = (f32[4,128]{1,0:T(4,128)S(1)}, bf16[4,128,2048]{1,2,0:T(8,128)(2,1)}) fusion(pred[128,2048]{0,1:T(8,128)(4,1)S(1)} %broadcast_compare_fusion, bf16[2048,128]{1,0:T(8,128)(2,1)S(1)} %pad_maximum_fusion, bf16[128,512]{1,0:T(8,128)(2,1)} %param.11), kind=kOutput, calls=%fused_computation.302 | convolution fusion | flops 274728960 | bytes 3016704 | tf_op jit(solution)/shard_map/sub | solution.py:84
  29.7 2.0 %fusion.78 = bf16[128,4,128]{0,2,1:T(8,128)(2,1)S(1)} fusion(bf16[4,128,2048]{1,2,0:T(8,128)(2,1)} %get-tuple-element.84, bf16[512,128]{0,1:T(8,128)(2,1)S(1)} %collective-permute-done.5, bf16[512,128]{0,1:T(8,128)(2,1)S(1)} %collective-permute-done.4, bf16[512,128]{0,1:T(8,128)(2,1)S(1)} %collective-permute-done.3, bf16[512,128]{0,1:T(8,128)(2,1)S(1)} %copy.29, ...), kind=kOutput, calls=%fused_computation.59 | convolution fusion | flops 270663680 | bytes 2754560 | tf_op jit(solution)/shard_map/qtj,jd->tqd/dot_general | solution.py:86
  31.7 7.8 %collective-permute-start.9 = (bf16[128,512]{0,1:T(8,128)(2,1)S(1)}, bf16[128,512]{0,1:T(8,128)(2,1)S(1)}, u32[]{:S(2)}, u32[]{:S(2)}) collective-permute-start(bf16[128,512]{0,1:T(8,128)(2,1)S(1)} %bitcast.293), channel_id=1, source_target_pairs={{0,4},{4,8},{8,12},{12,0},{1,5},{5,9},{9,13},{13,1},{2,6},{6,10},{... | collective-permute-start | bytes 393224 | tf_op jit(solution)/shard_map/ppermute | solution.py:14
  39.5 2.4 %collective-permute-start.11 = (bf16[128,512]{0,1:T(8,128)(2,1)S(1)}, bf16[128,512]{0,1:T(8,128)(2,1)S(1)}, u32[]{:S(2)}, u32[]{:S(2)}) collective-permute-start(bf16[128,512]{0,1:T(8,128)(2,1)S(1)} %bitcast.295), channel_id=1, source_target_pairs={{0,12},{4,0},{8,4},{12,8},{1,13},{5,1},{9,5},{13,9},{2,14},{6,2},{... | collective-permute-start | bytes 393224 | tf_op jit(solution)/shard_map/ppermute | solution.py:14
  43.3 7.6 %collective-permute-done.10 = bf16[128,512]{0,1:T(8,128)(2,1)S(1)} collective-permute-done((bf16[128,512]{0,1:T(8,128)(2,1)S(1)}, bf16[128,512]{0,1:T(8,128)(2,1)S(1)}, u32[]{:S(2)}, u32[]{:S(2)}) %collective-permute-start.10) | collective-permute-done | bytes 131104 | tf_op jit(solution)/shard_map/ppermute | solution.py:14
  51.8 1.7 %collective-permute-done.12 = bf16[256,1024]{1,0:T(8,128)(2,1)S(1)} collective-permute-done((bf16[256,1024]{1,0:T(8,128)(2,1)S(1)}, bf16[256,1024]{1,0:T(8,128)(2,1)S(1)}, u32[]{:S(2)}, u32[]{:S(2)}) %collective-permute-start.12) | collective-permute-done | bytes 524320 | tf_op jit(solution)/shard_map/ppermute | solution.py:107
  54.2 8.2 %collective-permute-done.13 = bf16[1,128,1024]{2,1,0:T(8,128)(2,1)S(1)} collective-permute-done((bf16[1,128,1024]{2,1,0:T(8,128)(2,1)S(1)}, bf16[1,128,1024]{2,1,0:T(8,128)(2,1)S(1)}, u32[]{:S(2)}, u32[]{:S(2)}) %collective-permute-start.13) | collective-permute-done | bytes 262176 | tf_op jit(solution)/shard_map/ppermute | solution.py:115
  62.5 3.1 %collective-permute-start.22 = (bf16[1,128,1024]{2,1,0:T(8,128)(2,1)S(1)}, bf16[1,128,1024]{2,1,0:T(8,128)(2,1)S(1)}, u32[]{:S(2)}, u32[]{:S(2)}) collective-permute-start(bf16[1,128,1024]{2,1,0:T(8,128)(2,1)S(1)} %fusion.95), channel_id=1, source_target_pairs={{0,12},{4,0},{8,4},{12,8},{1,13},{5,1},{9,5},{13,9},{2,14},{6,2},{... | collective-permute-start | bytes 786440 | tf_op jit(solution)/shard_map/ppermute | solution.py:136
  65.8 1.8 %collective-permute-start.16 = (bf16[64,1024]{1,0:T(8,128)(2,1)S(1)}, bf16[64,1024]{1,0:T(8,128)(2,1)S(1)}, u32[]{:S(2)}, u32[]{:S(2)}) collective-permute-start(bf16[64,1024]{1,0:T(8,128)(2,1)S(1)} %convolution_convert_fusion.17), channel_id=1, source_target_pairs={{0,2},{1,3},{2,0},{3,1},{4,6},{5,7},{6,4},{7,5},{8,10},{9,11},{10,... | collective-permute-start | bytes 393224 | tf_op jit(solution)/shard_map/ppermute | solution.py:145
  68.7 2.5 %collective-permute-done.16 = bf16[64,1024]{1,0:T(8,128)(2,1)S(1)} collective-permute-done((bf16[64,1024]{1,0:T(8,128)(2,1)S(1)}, bf16[64,1024]{1,0:T(8,128)(2,1)S(1)}, u32[]{:S(2)}, u32[]{:S(2)}) %collective-permute-start.16) | collective-permute-done | bytes 131104 | tf_op jit(solution)/shard_map/ppermute | solution.py:145
  73.5 3.3 %fusion.37 = f32[256,1792]{1,0:T(8,128)S(1)} fusion(bf16[256,1024]{1,0:T(8,128)(2,1)S(1)} %get-tuple-element.62, bf16[1,4096,1792]{2,1,0:T(8,128)(2,1)} %param.20, s32[]{:T(128)S(6)} %select_n.268), kind=kOutput, calls=%fused_computation.32 | convolution fusion | flops 939524096 | bytes 6029316 | tf_op jit(solution)/shard_map/dot_general | solution.py:161
  79.7 1.5 %collective-permute-start.24 = (bf16[64,1024]{1,0:T(8,128)(2,1)S(1)}, bf16[64,1024]{1,0:T(8,128)(2,1)S(1)}, u32[]{:S(2)}, u32[]{:S(2)}) collective-permute-start(bf16[64,1024]{1,0:T(8,128)(2,1)S(1)} %convolution_convert_fusion.9), channel_id=1, source_target_pairs={{0,2},{1,3},{2,0},{3,1},{4,6},{5,7},{6,4},{7,5},{8,10},{9,11},{10,... | collective-permute-start | bytes 393224 | tf_op jit(solution)/shard_map/ppermute | solution.py:145
  83.0 5.6 %collective-permute-done.26 = bf16[1,128,1024]{2,1,0:T(8,128)(2,1)S(1)} collective-permute-done((bf16[1,128,1024]{2,1,0:T(8,128)(2,1)S(1)}, bf16[1,128,1024]{2,1,0:T(8,128)(2,1)S(1)}, u32[]{:S(2)}, u32[]{:S(2)}) %collective-permute-start.26) | collective-permute-done | bytes 262176 | tf_op jit(solution)/shard_map/ppermute | solution.py:136
  91.0 3.2 %collective-permute-done.21 = bf16[64,1024]{1,0:T(8,128)(2,1)S(1)} collective-permute-done((bf16[64,1024]{1,0:T(8,128)(2,1)S(1)}, bf16[64,1024]{1,0:T(8,128)(2,1)S(1)}, u32[]{:S(2)}, u32[]{:S(2)}) %collective-permute-start.21) | collective-permute-done | bytes 131104 | tf_op jit(solution)/shard_map/ppermute | solution.py:145
  102.9 1.7 %collective-permute-done.29 = bf16[64,1024]{1,0:T(8,128)(2,1)S(1)} collective-permute-done((bf16[64,1024]{1,0:T(8,128)(2,1)S(1)}, bf16[64,1024]{1,0:T(8,128)(2,1)S(1)}, u32[]{:S(2)}, u32[]{:S(2)}) %collective-permute-start.29) | collective-permute-done | bytes 131104 | tf_op jit(solution)/shard_map/ppermute | solution.py:145
  106.6 3.3 %fusion.61 = f32[256,1792]{1,0:T(8,128)S(1)} fusion(f32[256,1792]{1,0:T(8,128)S(1)} %fusion.55, bf16[256,1024]{1,0:T(8,128)(2,1)S(1)} %pad_maximum_fusion.5, bf16[1,4096,1792]{2,1,0:T(8,128)(2,1)} %param.19, s32[]{:T(128)S(6)} %select_n.271), kind=kOutput, calls=%fused_computation.48 | convolution fusion | flops 939982848 | bytes 7864324 | tf_op jit(solution)/shard_map/dot_general | solution.py:160
  110.7 2.9 %fusion.21 = bf16[64,4096]{1,0:T(8,128)(2,1)S(1)} fusion(bf16[1,1792,4096]{2,1,0:T(8,128)(2,1)S(1)} %bitcast.282, bf16[256,1792]{1,0:T(8,128)(2,1)S(1)} %multiply_convert_fusion, s32[]{:T(128)S(6)} %select_n.273), kind=kOutput, calls=%fused_computation.16 | convolution fusion | flops 939786240 | bytes 15433732 | tf_op jit(solution)/shard_map/dot_general | solution.py:227
  114.0 2.7 %fusion.18 = bf16[64,4096]{1,0:T(8,128)(2,1)S(1)} fusion(bf16[1,1792,4096]{2,1,0:T(8,128)(2,1)S(1)} %bitcast.282, f32[64]{0:T(128)S(1)} %add_divide_fusion.2, bf16[256,1792]{1,0:T(8,128)(2,1)S(1)} %multiply_convert_fusion, s32[]{:T(128)S(6)} %select_n.275), kind=kOutput, calls=%fused_computation.15 | convolution fusion | flops 940048384 | bytes 15434244 | tf_op jit(solution)/shard_map/dot_general | solution.py:233
  120.4 2.7 %fusion.15 = bf16[64,4096]{1,0:T(8,128)(2,1)S(1)} fusion(bf16[1,1792,4096]{2,1,0:T(8,128)(2,1)S(1)} %bitcast.282, f32[64]{0:T(128)S(1)} %add_divide_fusion.1, bf16[256,1792]{1,0:T(8,128)(2,1)S(1)} %multiply_convert_fusion, s32[]{:T(128)S(6)} %select_n.279), kind=kOutput, calls=%fused_computation.14 | convolution fusion | flops 940048384 | bytes 15434244 | tf_op jit(solution)/shard_map/dot_general | solution.py:233
  123.5 4.3 %collective-permute-done.31 = bf16[1,32,4096]{2,1,0:T(8,128)(2,1)S(1)} collective-permute-done((bf16[1,32,4096]{2,1,0:T(8,128)(2,1)S(1)}, bf16[1,32,4096]{2,1,0:T(8,128)(2,1)S(1)}, u32[]{:S(2)}, u32[]{:S(2)}) %collective-permute-start.31) | collective-permute-done | bytes 262176 | tf_op jit(solution)/shard_map/ppermute | solution.py:219
  127.8 2.8 %collective-permute-start.32 = (bf16[32,4096]{1,0:T(8,128)(2,1)S(1)}, bf16[32,4096]{1,0:T(8,128)(2,1)S(1)}, u32[]{:S(2)}, u32[]{:S(2)}) collective-permute-start(bf16[32,4096]{1,0:T(8,128)(2,1)S(1)} %fusion.109), channel_id=1, source_target_pairs={{0,8},{4,12},{8,0},{12,4},{1,9},{5,13},{9,1},{13,5},{2,10},{6,14},... | collective-permute-start | bytes 786440 | tf_op jit(solution)/shard_map/ppermute | solution.py:236
  131.6 2.7 %fusion.1 = f32[64,4096]{1,0:T(8,128)S(1)} fusion(bf16[1,1792,4096]{2,1,0:T(8,128)(2,1)S(1)} %bitcast.282, bf16[256,1792]{1,0:T(8,128)(2,1)S(1)} %multiply_convert_fusion, s32[]{:T(128)S(6)} %select_n.281), kind=kOutput, calls=%fused_computation.1 | convolution fusion | flops 939524096 | bytes 15958020 | tf_op jit(solution)/shard_map/dot_general | solution.py:238
  134.9 3.3 %collective-permute-done.34 = bf16[1,32,4096]{2,1,0:T(8,128)(2,1)S(1)} collective-permute-done((bf16[1,32,4096]{2,1,0:T(8,128)(2,1)S(1)}, bf16[1,32,4096]{2,1,0:T(8,128)(2,1)S(1)}, u32[]{:S(2)}, u32[]{:S(2)}) %collective-permute-start.34) | collective-permute-done | bytes 262176 | tf_op jit(solution)/shard_map/ppermute | solution.py:219
  138.3 1.4 collective-permute-start.35
  140.4 2.8 %collective-permute-done.32 = bf16[32,4096]{1,0:T(8,128)(2,1)S(1)} collective-permute-done((bf16[32,4096]{1,0:T(8,128)(2,1)S(1)}, bf16[32,4096]{1,0:T(8,128)(2,1)S(1)}, u32[]{:S(2)}, u32[]{:S(2)}) %collective-permute-start.32) | collective-permute-done | bytes 262176 | tf_op jit(solution)/shard_map/ppermute | solution.py:236
  143.2 4.3 %collective-permute-done.35 = bf16[32,4096]{1,0:T(8,128)(2,1)S(1)} collective-permute-done((bf16[32,4096]{1,0:T(8,128)(2,1)S(1)}, bf16[32,4096]{1,0:T(8,128)(2,1)S(1)}, u32[]{:S(2)}, u32[]{:S(2)}) %collective-permute-start.35) | collective-permute-done | bytes 262176 | tf_op jit(solution)/shard_map/ppermute | solution.py:236
  (201 shorter events, 44.1 us)
Async XLA Ops:
  0.0 21.2 %collective-permute-start.6 = (bf16[512,128]{1,0:T(8,128)(2,1)}, bf16[512,128]{1,0:T(8,128)(2,1)S(1)}, u32[]{:S(2)}, u32[]{:S(2)}) collective-permute-start(bf16[512,128]{1,0:T(8,128)(2,1)} %param.12), channel_id=1, source_target_pairs={{0,4},{4,8},{8,12},{12,0},{1,5},{5,9},{9,13},{13,1},{2,6},{6,10},{... | collective-permute-start | bytes 393224 | tf_op jit(solution)/shard_map/ppermute | solution.py:14
  3.0 18.5 %collective-permute-start.7 = (bf16[512,128]{1,0:T(8,128)(2,1)}, bf16[512,128]{1,0:T(8,128)(2,1)S(1)}, u32[]{:S(2)}, u32[]{:S(2)}) collective-permute-start(bf16[512,128]{1,0:T(8,128)(2,1)} %param.12), channel_id=1, source_target_pairs={{0,8},{4,12},{8,0},{12,4},{1,9},{5,13},{9,1},{13,5},{2,10},{6,14},... | collective-permute-start | bytes 393224 | tf_op jit(solution)/shard_map/ppermute | solution.py:14
  5.6 8.0 %collective-permute-start.1 = (s32[128,2]{0,1:T(2,128)}, s32[128,2]{0,1:T(2,128)S(1)}, u32[]{:S(2)}, u32[]{:S(2)}) collective-permute-start(s32[128,2]{0,1:T(2,128)} %param.17), channel_id=1, source_target_pairs={{0,4},{4,8},{8,12},{12,0},{1,5},{5,9},{9,13},{13,1},{2,6},{6,10},{... | collective-permute-start | bytes 3080 | tf_op jit(solution)/shard_map/ppermute | solution.py:14
  5.7 8.8 %collective-permute-start = (s32[128,2]{0,1:T(2,128)}, s32[128,2]{0,1:T(2,128)S(1)}, u32[]{:S(2)}, u32[]{:S(2)}) collective-permute-start(s32[128,2]{0,1:T(2,128)} %param.17), channel_id=1, source_target_pairs={{0,8},{4,12},{8,0},{12,4},{1,9},{5,13},{9,1},{13,5},{2,10},{6,14},... | collective-permute-start | bytes 3080 | tf_op jit(solution)/shard_map/ppermute | solution.py:14
  7.5 8.2 %collective-permute-start.2 = (s32[128,2]{0,1:T(2,128)}, s32[128,2]{0,1:T(2,128)S(1)}, u32[]{:S(2)}, u32[]{:S(2)}) collective-permute-start(s32[128,2]{0,1:T(2,128)} %param.17), channel_id=1, source_target_pairs={{0,12},{4,0},{8,4},{12,8},{1,13},{5,1},{9,5},{13,9},{2,14},{6,2},{... | collective-permute-start | bytes 3080 | tf_op jit(solution)/shard_map/ppermute | solution.py:14
  13.7 9.5 %collective-permute-start.8 = (bf16[512,128]{1,0:T(8,128)(2,1)}, bf16[512,128]{1,0:T(8,128)(2,1)S(1)}, u32[]{:S(2)}, u32[]{:S(2)}) collective-permute-start(bf16[512,128]{1,0:T(8,128)(2,1)} %param.12), channel_id=1, source_target_pairs={{0,12},{4,0},{8,4},{12,8},{1,13},{5,1},{9,5},{13,9},{2,14},{6,2},{... | collective-permute-start | bytes 393224 | tf_op jit(solution)/shard_map/ppermute | solution.py:14
  14.5 13.9 %collective-permute-start.3 = (bf16[512,128]{0,1:T(8,128)(2,1)S(1)}, bf16[512,128]{0,1:T(8,128)(2,1)S(1)}, u32[]{:S(2)}, u32[]{:S(2)}) collective-permute-start(bf16[512,128]{0,1:T(8,128)(2,1)S(1)} %copy.29), channel_id=1, source_target_pairs={{0,4},{4,8},{8,12},{12,0},{1,5},{5,9},{9,13},{13,1},{2,6},{6,10},{... | collective-permute-start | bytes 393224 | tf_op jit(solution)/shard_map/ppermute | solution.py:14
  15.8 13.9 %collective-permute-start.4 = (bf16[512,128]{0,1:T(8,128)(2,1)S(1)}, bf16[512,128]{0,1:T(8,128)(2,1)S(1)}, u32[]{:S(2)}, u32[]{:S(2)}) collective-permute-start(bf16[512,128]{0,1:T(8,128)(2,1)S(1)} %copy.29), channel_id=1, source_target_pairs={{0,8},{4,12},{8,0},{12,4},{1,9},{5,13},{9,1},{13,5},{2,10},{6,14},... | collective-permute-start | bytes 393224 | tf_op jit(solution)/shard_map/ppermute | solution.py:14
  21.2 8.5 %collective-permute-start.5 = (bf16[512,128]{0,1:T(8,128)(2,1)S(1)}, bf16[512,128]{0,1:T(8,128)(2,1)S(1)}, u32[]{:S(2)}, u32[]{:S(2)}) collective-permute-start(bf16[512,128]{0,1:T(8,128)(2,1)S(1)} %copy.29), channel_id=1, source_target_pairs={{0,12},{4,0},{8,4},{12,8},{1,13},{5,1},{9,5},{13,9},{2,14},{6,2},{... | collective-permute-start | bytes 393224 | tf_op jit(solution)/shard_map/ppermute | solution.py:14
  21.6 32.6 %collective-permute-start.14 = (bf16[128,1024]{1,0:T(8,128)(2,1)}, bf16[128,1024]{1,0:T(8,128)(2,1)S(1)}, u32[]{:S(2)}, u32[]{:S(2)}) collective-permute-start(bf16[128,1024]{1,0:T(8,128)(2,1)} %param.15), channel_id=1, source_target_pairs={{0,0},{1,4},{2,8},{3,12},{4,1},{5,5},{6,9},{7,13},{8,2},{9,6},{10,... | collective-permute-start | bytes 786440 | tf_op jit(solution)/shard_map/ppermute | solution.py:62
  31.7 11.5 %collective-permute-start.9 = (bf16[128,512]{0,1:T(8,128)(2,1)S(1)}, bf16[128,512]{0,1:T(8,128)(2,1)S(1)}, u32[]{:S(2)}, u32[]{:S(2)}) collective-permute-start(bf16[128,512]{0,1:T(8,128)(2,1)S(1)} %bitcast.293), channel_id=1, source_target_pairs={{0,4},{4,8},{8,12},{12,0},{1,5},{5,9},{9,13},{13,1},{2,6},{6,10},{... | collective-permute-start | bytes 393224 | tf_op jit(solution)/shard_map/ppermute | solution.py:14
  39.5 11.4 %collective-permute-start.10 = (bf16[128,512]{0,1:T(8,128)(2,1)S(1)}, bf16[128,512]{0,1:T(8,128)(2,1)S(1)}, u32[]{:S(2)}, u32[]{:S(2)}) collective-permute-start(bf16[128,512]{0,1:T(8,128)(2,1)S(1)} %bitcast.294), channel_id=1, source_target_pairs={{0,8},{4,12},{8,0},{12,4},{1,9},{5,13},{9,1},{13,5},{2,10},{6,14},... | collective-permute-start | bytes 393224 | tf_op jit(solution)/shard_map/ppermute | solution.py:14
  39.5 11.4 %collective-permute-start.11 = (bf16[128,512]{0,1:T(8,128)(2,1)S(1)}, bf16[128,512]{0,1:T(8,128)(2,1)S(1)}, u32[]{:S(2)}, u32[]{:S(2)}) collective-permute-start(bf16[128,512]{0,1:T(8,128)(2,1)S(1)} %bitcast.295), channel_id=1, source_target_pairs={{0,12},{4,0},{8,4},{12,8},{1,13},{5,1},{9,5},{13,9},{2,14},{6,2},{... | collective-permute-start | bytes 393224 | tf_op jit(solution)/shard_map/ppermute | solution.py:14
  54.0 8.4 %collective-permute-start.13 = (bf16[1,128,1024]{2,1,0:T(8,128)(2,1)S(1)}, bf16[1,128,1024]{2,1,0:T(8,128)(2,1)S(1)}, u32[]{:S(2)}, u32[]{:S(2)}) collective-permute-start(bf16[1,128,1024]{2,1,0:T(8,128)(2,1)S(1)} %fusion.105), channel_id=1, source_target_pairs={{0,2},{1,3},{2,0},{3,1},{4,6},{5,7},{6,4},{7,5},{8,10},{9,11},{10,... | collective-permute-start | bytes 786440 | tf_op jit(solution)/shard_map/ppermute | solution.py:115
  62.5 16.0 %collective-permute-start.22 = (bf16[1,128,1024]{2,1,0:T(8,128)(2,1)S(1)}, bf16[1,128,1024]{2,1,0:T(8,128)(2,1)S(1)}, u32[]{:S(2)}, u32[]{:S(2)}) collective-permute-start(bf16[1,128,1024]{2,1,0:T(8,128)(2,1)S(1)} %fusion.95), channel_id=1, source_target_pairs={{0,12},{4,0},{8,4},{12,8},{1,13},{5,1},{9,5},{13,9},{2,14},{6,2},{... | collective-permute-start | bytes 786440 | tf_op jit(solution)/shard_map/ppermute | solution.py:136
  65.6 15.6 %collective-permute-start.18 = (bf16[1,128,1024]{2,1,0:T(8,128)(2,1)S(1)}, bf16[1,128,1024]{2,1,0:T(8,128)(2,1)S(1)}, u32[]{:S(2)}, u32[]{:S(2)}) collective-permute-start(bf16[1,128,1024]{2,1,0:T(8,128)(2,1)S(1)} %fusion.95), channel_id=1, source_target_pairs={{0,4},{4,8},{8,12},{12,0},{1,5},{5,9},{9,13},{13,1},{2,6},{6,10},{... | collective-permute-start | bytes 786440 | tf_op jit(solution)/shard_map/ppermute | solution.py:136
  71.2 17.5 %collective-permute-start.26 = (bf16[1,128,1024]{2,1,0:T(8,128)(2,1)S(1)}, bf16[1,128,1024]{2,1,0:T(8,128)(2,1)S(1)}, u32[]{:S(2)}, u32[]{:S(2)}) collective-permute-start(bf16[1,128,1024]{2,1,0:T(8,128)(2,1)S(1)} %fusion.95), channel_id=1, source_target_pairs={{0,8},{4,12},{8,0},{12,4},{1,9},{5,13},{9,1},{13,5},{2,10},{6,14},... | collective-permute-start | bytes 786440 | tf_op jit(solution)/shard_map/ppermute | solution.py:136
  78.7 20.2 %collective-permute-start.23 = (bf16[64,1024]{1,0:T(8,128)(2,1)S(1)}, bf16[64,1024]{1,0:T(8,128)(2,1)S(1)}, u32[]{:S(2)}, u32[]{:S(2)}) collective-permute-start(bf16[64,1024]{1,0:T(8,128)(2,1)S(1)} %convolution_convert_fusion.10), channel_id=1, source_target_pairs={{0,1},{1,0},{2,3},{3,2},{4,5},{5,4},{6,7},{7,6},{8,9},{9,8},{10,11... | collective-permute-start | bytes 393224 | tf_op jit(solution)/shard_map/ppermute | solution.py:145
  79.7 19.9 %collective-permute-start.24 = (bf16[64,1024]{1,0:T(8,128)(2,1)S(1)}, bf16[64,1024]{1,0:T(8,128)(2,1)S(1)}, u32[]{:S(2)}, u32[]{:S(2)}) collective-permute-start(bf16[64,1024]{1,0:T(8,128)(2,1)S(1)} %convolution_convert_fusion.9), channel_id=1, source_target_pairs={{0,2},{1,3},{2,0},{3,1},{4,6},{5,7},{6,4},{7,5},{8,10},{9,11},{10,... | collective-permute-start | bytes 393224 | tf_op jit(solution)/shard_map/ppermute | solution.py:145
  81.4 8.2 %collective-permute-start.19 = (bf16[64,1024]{1,0:T(8,128)(2,1)S(1)}, bf16[64,1024]{1,0:T(8,128)(2,1)S(1)}, u32[]{:S(2)}, u32[]{:S(2)}) collective-permute-start(bf16[64,1024]{1,0:T(8,128)(2,1)S(1)} %convolution_convert_fusion.14), channel_id=1, source_target_pairs={{0,1},{1,0},{2,3},{3,2},{4,5},{5,4},{6,7},{7,6},{8,9},{9,8},{10,11... | collective-permute-start | bytes 393224 | tf_op jit(solution)/shard_map/ppermute | solution.py:145
  81.7 9.2 %collective-permute-start.20 = (bf16[64,1024]{1,0:T(8,128)(2,1)S(1)}, bf16[64,1024]{1,0:T(8,128)(2,1)S(1)}, u32[]{:S(2)}, u32[]{:S(2)}) collective-permute-start(bf16[64,1024]{1,0:T(8,128)(2,1)S(1)} %convolution_convert_fusion.13), channel_id=1, source_target_pairs={{0,2},{1,3},{2,0},{3,1},{4,6},{5,7},{6,4},{7,5},{8,10},{9,11},{10,... | collective-permute-start | bytes 393224 | tf_op jit(solution)/shard_map/ppermute | solution.py:145
  89.7 9.9 %collective-permute-start.25 = (bf16[64,1024]{1,0:T(8,128)(2,1)S(1)}, bf16[64,1024]{1,0:T(8,128)(2,1)S(1)}, u32[]{:S(2)}, u32[]{:S(2)}) collective-permute-start(bf16[64,1024]{1,0:T(8,128)(2,1)S(1)} %convolution_convert_fusion.8), channel_id=1, source_target_pairs={{0,3},{1,2},{2,1},{3,0},{4,7},{5,6},{6,5},{7,4},{8,11},{9,10},{10,... | collective-permute-start | bytes 393224 | tf_op jit(solution)/shard_map/ppermute | solution.py:145
  90.9 12.0 %collective-permute-start.27 = (bf16[64,1024]{1,0:T(8,128)(2,1)S(1)}, bf16[64,1024]{1,0:T(8,128)(2,1)S(1)}, u32[]{:S(2)}, u32[]{:S(2)}) collective-permute-start(bf16[64,1024]{1,0:T(8,128)(2,1)S(1)} %convolution_convert_fusion.6), channel_id=1, source_target_pairs={{0,1},{1,0},{2,3},{3,2},{4,5},{5,4},{6,7},{7,6},{8,9},{9,8},{10,11... | collective-permute-start | bytes 393224 | tf_op jit(solution)/shard_map/ppermute | solution.py:145
  94.2 8.7 %collective-permute-start.28 = (bf16[64,1024]{1,0:T(8,128)(2,1)S(1)}, bf16[64,1024]{1,0:T(8,128)(2,1)S(1)}, u32[]{:S(2)}, u32[]{:S(2)}) collective-permute-start(bf16[64,1024]{1,0:T(8,128)(2,1)S(1)} %convolution_convert_fusion.5), channel_id=1, source_target_pairs={{0,2},{1,3},{2,0},{3,1},{4,6},{5,7},{6,4},{7,5},{8,10},{9,11},{10,... | collective-permute-start | bytes 393224 | tf_op jit(solution)/shard_map/ppermute | solution.py:145
  98.9 5.8 %collective-permute-start.29 = (bf16[64,1024]{1,0:T(8,128)(2,1)S(1)}, bf16[64,1024]{1,0:T(8,128)(2,1)S(1)}, u32[]{:S(2)}, u32[]{:S(2)}) collective-permute-start(bf16[64,1024]{1,0:T(8,128)(2,1)S(1)} %convolution_convert_fusion.4), channel_id=1, source_target_pairs={{0,3},{1,2},{2,1},{3,0},{4,7},{5,6},{6,5},{7,4},{8,11},{9,10},{10,... | collective-permute-start | bytes 393224 | tf_op jit(solution)/shard_map/ppermute | solution.py:145
  113.7 20.6 %collective-permute-start.36 = (bf16[64,4096]{1,0:T(8,128)(2,1)S(1)}, bf16[64,4096]{1,0:T(8,128)(2,1)S(1)}, u32[]{:S(2)}, u32[]{:S(2)}) collective-permute-start(bf16[64,4096]{1,0:T(8,128)(2,1)S(1)} %fusion.21), channel_id=1, source_target_pairs={{0,4},{4,8},{8,12},{12,0},{1,5},{5,9},{9,13},{13,1},{2,6},{6,10},{... | collective-permute-start | bytes 1572872 | tf_op jit(solution)/shard_map/ppermute | solution.py:230
  119.3 8.4 %collective-permute-start.31 = (bf16[1,32,4096]{2,1,0:T(8,128)(2,1)S(1)}, bf16[1,32,4096]{2,1,0:T(8,128)(2,1)S(1)}, u32[]{:S(2)}, u32[]{:S(2)}) collective-permute-start(bf16[1,32,4096]{2,1,0:T(8,128)(2,1)S(1)} %fusion.106), channel_id=1, source_target_pairs={{0,2},{1,3},{2,0},{3,1},{4,6},{5,7},{6,4},{7,5},{8,10},{9,11},{10,... | collective-permute-start | bytes 786440 | tf_op jit(solution)/shard_map/ppermute | solution.py:219
  123.3 7.2 %collective-permute-start.33 = (bf16[64,4096]{1,0:T(8,128)(2,1)S(1)}, bf16[64,4096]{1,0:T(8,128)(2,1)S(1)}, u32[]{:S(2)}, u32[]{:S(2)}) collective-permute-start(bf16[64,4096]{1,0:T(8,128)(2,1)S(1)} %convolution_convert_fusion.1), channel_id=1, source_target_pairs={{0,1},{1,0},{2,3},{3,2},{4,5},{5,4},{6,7},{7,6},{8,9},{9,8},{10,11... | collective-permute-start | bytes 1572872 | tf_op jit(solution)/shard_map/ppermute | solution.py:210
  127.8 15.5 %collective-permute-start.32 = (bf16[32,4096]{1,0:T(8,128)(2,1)S(1)}, bf16[32,4096]{1,0:T(8,128)(2,1)S(1)}, u32[]{:S(2)}, u32[]{:S(2)}) collective-permute-start(bf16[32,4096]{1,0:T(8,128)(2,1)S(1)} %fusion.109), channel_id=1, source_target_pairs={{0,8},{4,12},{8,0},{12,4},{1,9},{5,13},{9,1},{13,5},{2,10},{6,14},... | collective-permute-start | bytes 786440 | tf_op jit(solution)/shard_map/ppermute | solution.py:236
  130.9 7.3 %collective-permute-start.34 = (bf16[1,32,4096]{2,1,0:T(8,128)(2,1)S(1)}, bf16[1,32,4096]{2,1,0:T(8,128)(2,1)S(1)}, u32[]{:S(2)}, u32[]{:S(2)}) collective-permute-start(bf16[1,32,4096]{2,1,0:T(8,128)(2,1)S(1)} %fusion.107), channel_id=1, source_target_pairs={{0,2},{1,3},{2,0},{3,1},{4,6},{5,7},{6,4},{7,5},{8,10},{9,11},{10,... | collective-permute-start | bytes 786440 | tf_op jit(solution)/shard_map/ppermute | solution.py:219
  138.3 9.3 %collective-permute-start.35 = (bf16[32,4096]{1,0:T(8,128)(2,1)S(1)}, bf16[32,4096]{1,0:T(8,128)(2,1)S(1)}, u32[]{:S(2)}, u32[]{:S(2)}) collective-permute-start(bf16[32,4096]{1,0:T(8,128)(2,1)S(1)} %fusion.110), channel_id=1, source_target_pairs={{0,12},{4,0},{8,4},{12,8},{1,13},{5,1},{9,5},{13,9},{2,14},{6,2},{... | collective-permute-start | bytes 786440 | tf_op jit(solution)/shard_map/ppermute | solution.py:236
  140.0 7.6 %collective-permute-start.38 = (bf16[1,32,4096]{2,1,0:T(8,128)(2,1)S(1)}, bf16[1,32,4096]{2,1,0:T(8,128)(2,1)S(1)}, u32[]{:S(2)}, u32[]{:S(2)}) collective-permute-start(bf16[1,32,4096]{2,1,0:T(8,128)(2,1)S(1)} %fusion.108), channel_id=1, source_target_pairs={{0,2},{1,3},{2,0},{3,1},{4,6},{5,7},{6,4},{7,5},{8,10},{9,11},{10,... | collective-permute-start | bytes 786440 | tf_op jit(solution)/shard_map/ppermute | solution.py:219
  (19 other events, 281.3 us)

commit v5 on v4

--- a/solution.py
+++ b/solution.py
@@ -185,7 +185,7 @@
     mine = (experts == e).astype(f32)[None, :]
     own_share = tok // exp_count
 
-    def contribution(k, gives):
+    def contribution(k, gives, gated=False):
         block = (c + k) % ctx_count
         block_routes = routes_all[-k % ctx_count]
         picker = picker_of(jnp.any(block_routes == e, axis=1), capacity).astype(f32)
@@ -194,7 +194,10 @@
         gate = jax.nn.sigmoid(
             jnp.sum(rows_of(logits, block) * (mine - other_slot), axis=1, keepdims=True)
         )
-        gives *= gate
+        if gives is None:
+            return gate
+        if not gated:
+            gives *= gate
         if k == 0:
             gives += 0.5 * stream_rows.astype(f32)
         gives = gives.astype(bf16)
@@ -223,15 +226,21 @@
     direct = [k for k in (1,) if k < ctx_count]
     others = [k for k in reversed(turns) if k and k not in direct]
     added, output, after = 0.0, 0.0, ()
+    together = direct + others[:1]
+    rows = jnp.concatenate([rows_of(act, (c + k) % ctx_count) for k in together])
+    plain = jnp.ones((capacity, 1), f32)
+    factor = jnp.concatenate([plain if k in direct else contribution(k, None) for k in together])
+    shared = factor * jnp.dot(rows, down_here, preferred_element_type=f32)
+    shared = dict(zip(together, jnp.split(shared.astype(bf16), len(together))))
     for k in direct:
-        part = jnp.dot(rows_of(act, (c + k) % ctx_count), down_here, preferred_element_type=f32)
-        part = part.astype(bf16)
-        after += (part,)
-        added += lax.ppermute(part, "ctx", rotation(ctx_count, k)).astype(f32)
+        added += lax.ppermute(shared[k], "ctx", rotation(ctx_count, k)).astype(f32)
     for k in others:
-        rows = rows_of(lax.optimization_barrier((act, after))[0], (c + k) % ctx_count)
-        gives = jnp.dot(rows, down_here, preferred_element_type=f32)
-        part, after = contribution(k, gives)
+        if k in shared:
+            part, after = contribution(k, shared[k], gated=True)
+        else:
+            rows = rows_of(lax.optimization_barrier((act, after))[0], (c + k) % ctx_count)
+            gives = jnp.dot(rows, down_here, preferred_element_type=f32)
+            part, after = contribution(k, gives)
         part = part.astype(bf16)
         output += lax.ppermute(part, "ctx", rotation(ctx_count, k)).astype(f32)
     rows = rows_of(lax.optimization_barrier((act, after))[0], c)

time: 149 us -> 147 us (0.987)
  matrix products: 39.1 us -> 35.7 us
  waiting for transfers between devices: 50.6 us -> 53.1 us
    dot_general x3 -> x2, matrix products: 8.11 us -> 5.4 us  [local(): gives = jnp.dot(rows, down_here, preferred_element_type=f32)]
    ppermute x2, waiting for transfers between devices: 7.18 us -> 9.04 us  [local(): output += lax.ppermute(part, 'ctx', rotation(ctx_count, k)).astype(f32)]
  transfers between devices with their start and end apart: 39 -> 39, of which waited for: 16 -> 17; matrix products, arithmetic and copies ran while one was open for 28% -> 26% of each run, Pallas kernels for 0% -> 0%
where the time goes in v5:
time: 147 us
  waiting for transfers between devices  53.1 us (36%)
  starting transfers between devices  44.7 us (30%)
  matrix products  35.7 us (24%)
  other arithmetic  9.57 us (7%)
  local copies, waits for them, and re-layouts  2.55 us (2%)
    ppermute x12, starting transfers between devices, gather_rotated(): lax.ppermute(block, 'ctx', rotation(count, k))  24 us
    ppermute x12, waiting for transfers between devices, gather_rotated(): lax.ppermute(block, 'ctx', rotation(count, k))  10.4 us
    ppermute x12, starting transfers between devices, local(): piece = lax.ppermute(piece, 'exp', [(i, i ^ m) for i in range(exp_count)])  9.34 us
    ppermute x2, waiting for transfers between devices, local(): output += lax.ppermute(part, 'ctx', rotation(ctx_count, k)).astype(f32)  9.04 us
    ppermute x12, waiting for transfers between devices, local(): piece = lax.ppermute(piece, 'exp', [(i, i ^ m) for i in range(exp_count)])  8.84 us
    ppermute x1, waiting for transfers between devices, local(): lax.ppermute(sent, 'exp', [(i, i ^ 1 << level) for i in range(exp_count)])  8.25 us
    ppermute x3, waiting for transfers between devices, contribution(): lax.ppermute(sent, 'exp', [(i, i ^ 1 << level) for i in range(exp_count)])  7.53 us
    dot_general x4, matrix products, local(): up_proj += jnp.dot(chunk, up_rows, preferred_element_type=f32)  6.76 us
  transfers between devices with their start and end apart: 39, of which 17 were waited for; matrix products, arithmetic and copies ran while one was open for 26% of the time, Pallas kernels for 0%

profile of v5, /device:TPU:0, one launch (start us, length us, event | category | flops | bytes accessed | tf_op | source)
XLA Modules:
  0.0 146.6 jit_solution(17692142539313566503)
XLA Ops:
  0.0 3.0 %collective-permute-start.6 = (bf16[512,128]{1,0:T(8,128)(2,1)}, bf16[512,128]{1,0:T(8,128)(2,1)S(1)}, u32[]{:S(2)}, u32[]{:S(2)}) collective-permute-start(bf16[512,128]{1,0:T(8,128)(2,1)} %param.12), channel_id=1, source_target_pairs={{0,4},{4,8},{8,12},{12,0},{1,5},{5,9},{9,13},{13,1},{2,6},{6,10},{... | collective-permute-start | bytes 393224 | tf_op jit(solution)/shard_map/ppermute | solution.py:14
  3.0 2.6 %collective-permute-start.7 = (bf16[512,128]{1,0:T(8,128)(2,1)}, bf16[512,128]{1,0:T(8,128)(2,1)S(1)}, u32[]{:S(2)}, u32[]{:S(2)}) collective-permute-start(bf16[512,128]{1,0:T(8,128)(2,1)} %param.12), channel_id=1, source_target_pairs={{0,8},{4,12},{8,0},{12,4},{1,9},{5,13},{9,1},{13,5},{2,10},{6,14},... | collective-permute-start | bytes 393224 | tf_op jit(solution)/shard_map/ppermute | solution.py:14
  5.7 1.8 %collective-permute-start = (s32[128,2]{0,1:T(2,128)}, s32[128,2]{0,1:T(2,128)S(1)}, u32[]{:S(2)}, u32[]{:S(2)}) collective-permute-start(s32[128,2]{0,1:T(2,128)} %param.17), channel_id=1, source_target_pairs={{0,8},{4,12},{8,0},{12,4},{1,9},{5,13},{9,1},{13,5},{2,10},{6,14},... | collective-permute-start | bytes 3080 | tf_op jit(solution)/shard_map/ppermute | solution.py:14
  7.5 1.9 %collective-permute-start.2 = (s32[128,2]{0,1:T(2,128)}, s32[128,2]{0,1:T(2,128)S(1)}, u32[]{:S(2)}, u32[]{:S(2)}) collective-permute-start(s32[128,2]{0,1:T(2,128)} %param.17), channel_id=1, source_target_pairs={{0,12},{4,0},{8,4},{12,8},{1,13},{5,1},{9,5},{13,9},{2,14},{6,2},{... | collective-permute-start | bytes 3080 | tf_op jit(solution)/shard_map/ppermute | solution.py:14
  15.8 2.0 %collective-permute-start.4 = (bf16[512,128]{0,1:T(8,128)(2,1)S(1)}, bf16[512,128]{0,1:T(8,128)(2,1)S(1)}, u32[]{:S(2)}, u32[]{:S(2)}) collective-permute-start(bf16[512,128]{0,1:T(8,128)(2,1)S(1)} %copy.29), channel_id=1, source_target_pairs={{0,8},{4,12},{8,0},{12,4},{1,9},{5,13},{9,1},{13,5},{2,10},{6,14},... | collective-permute-start | bytes 393224 | tf_op jit(solution)/shard_map/ppermute | solution.py:14
  21.6 1.6 %collective-permute-start.14 = (bf16[128,1024]{1,0:T(8,128)(2,1)}, bf16[128,1024]{1,0:T(8,128)(2,1)S(1)}, u32[]{:S(2)}, u32[]{:S(2)}) collective-permute-start(bf16[128,1024]{1,0:T(8,128)(2,1)} %param.15), channel_id=1, source_target_pairs={{0,0},{1,4},{2,8},{3,12},{4,1},{5,5},{6,9},{7,13},{8,2},{9,6},{10,... | collective-permute-start | bytes 786440 | tf_op jit(solution)/shard_map/ppermute | solution.py:62
  24.1 4.3 %fusion.204 = (f32[4,128]{1,0:T(4,128)S(1)}, bf16[4,128,2048]{1,2,0:T(8,128)(2,1)}) fusion(pred[128,2048]{0,1:T(8,128)(4,1)S(1)} %broadcast_compare_fusion, bf16[2048,128]{1,0:T(8,128)(2,1)S(1)} %pad_maximum_fusion, bf16[128,512]{1,0:T(8,128)(2,1)} %param.11), kind=kOutput, calls=%fused_computation.305 | convolution fusion | flops 274728960 | bytes 3016704 | tf_op jit(solution)/shard_map/sub | solution.py:84
  29.7 2.0 %fusion.73 = bf16[128,4,128]{0,2,1:T(8,128)(2,1)S(1)} fusion(bf16[4,128,2048]{1,2,0:T(8,128)(2,1)} %get-tuple-element.84, bf16[512,128]{0,1:T(8,128)(2,1)S(1)} %collective-permute-done.5, bf16[512,128]{0,1:T(8,128)(2,1)S(1)} %collective-permute-done.4, bf16[512,128]{0,1:T(8,128)(2,1)S(1)} %collective-permute-done.3, bf16[512,128]{0,1:T(8,128)(2,1)S(1)} %copy.29, ...), kind=kOutput, calls=%fused_computation.56 | convolution fusion | flops 270663680 | bytes 2754560 | tf_op jit(solution)/shard_map/qtj,jd->tqd/dot_general | solution.py:86
  31.7 7.8 %collective-permute-start.9 = (bf16[128,512]{0,1:T(8,128)(2,1)S(1)}, bf16[128,512]{0,1:T(8,128)(2,1)S(1)}, u32[]{:S(2)}, u32[]{:S(2)}) collective-permute-start(bf16[128,512]{0,1:T(8,128)(2,1)S(1)} %bitcast.291), channel_id=1, source_target_pairs={{0,4},{4,8},{8,12},{12,0},{1,5},{5,9},{9,13},{13,1},{2,6},{6,10},{... | collective-permute-start | bytes 393224 | tf_op jit(solution)/shard_map/ppermute | solution.py:14
  39.5 2.4 %collective-permute-start.11 = (bf16[128,512]{0,1:T(8,128)(2,1)S(1)}, bf16[128,512]{0,1:T(8,128)(2,1)S(1)}, u32[]{:S(2)}, u32[]{:S(2)}) collective-permute-start(bf16[128,512]{0,1:T(8,128)(2,1)S(1)} %bitcast.293), channel_id=1, source_target_pairs={{0,12},{4,0},{8,4},{12,8},{1,13},{5,1},{9,5},{13,9},{2,14},{6,2},{... | collective-permute-start | bytes 393224 | tf_op jit(solution)/shard_map/ppermute | solution.py:14
  43.3 7.6 %collective-permute-done.10 = bf16[128,512]{0,1:T(8,128)(2,1)S(1)} collective-permute-done((bf16[128,512]{0,1:T(8,128)(2,1)S(1)}, bf16[128,512]{0,1:T(8,128)(2,1)S(1)}, u32[]{:S(2)}, u32[]{:S(2)}) %collective-permute-start.10) | collective-permute-done | bytes 131104 | tf_op jit(solution)/shard_map/ppermute | solution.py:14
  51.8 1.7 %collective-permute-done.12 = bf16[256,1024]{1,0:T(8,128)(2,1)S(1)} collective-permute-done((bf16[256,1024]{1,0:T(8,128)(2,1)S(1)}, bf16[256,1024]{1,0:T(8,128)(2,1)S(1)}, u32[]{:S(2)}, u32[]{:S(2)}) %collective-permute-start.12) | collective-permute-done | bytes 524320 | tf_op jit(solution)/shard_map/ppermute | solution.py:107
  54.2 8.2 %collective-permute-done.13 = bf16[1,128,1024]{2,1,0:T(8,128)(2,1)S(1)} collective-permute-done((bf16[1,128,1024]{2,1,0:T(8,128)(2,1)S(1)}, bf16[1,128,1024]{2,1,0:T(8,128)(2,1)S(1)}, u32[]{:S(2)}, u32[]{:S(2)}) %collective-permute-start.13) | collective-permute-done | bytes 262176 | tf_op jit(solution)/shard_map/ppermute | solution.py:115
  62.5 3.1 %collective-permute-start.22 = (bf16[1,128,1024]{2,1,0:T(8,128)(2,1)S(1)}, bf16[1,128,1024]{2,1,0:T(8,128)(2,1)S(1)}, u32[]{:S(2)}, u32[]{:S(2)}) collective-permute-start(bf16[1,128,1024]{2,1,0:T(8,128)(2,1)S(1)} %fusion.90), channel_id=1, source_target_pairs={{0,12},{4,0},{8,4},{12,8},{1,13},{5,1},{9,5},{13,9},{2,14},{6,2},{... | collective-permute-start | bytes 786440 | tf_op jit(solution)/shard_map/ppermute | solution.py:136
  65.8 1.8 %collective-permute-start.16 = (bf16[64,1024]{1,0:T(8,128)(2,1)S(1)}, bf16[64,1024]{1,0:T(8,128)(2,1)S(1)}, u32[]{:S(2)}, u32[]{:S(2)}) collective-permute-start(bf16[64,1024]{1,0:T(8,128)(2,1)S(1)} %convolution_convert_fusion.17), channel_id=1, source_target_pairs={{0,2},{1,3},{2,0},{3,1},{4,6},{5,7},{6,4},{7,5},{8,10},{9,11},{10,... | collective-permute-start | bytes 393224 | tf_op jit(solution)/shard_map/ppermute | solution.py:145
  68.7 2.5 %collective-permute-done.16 = bf16[64,1024]{1,0:T(8,128)(2,1)S(1)} collective-permute-done((bf16[64,1024]{1,0:T(8,128)(2,1)S(1)}, bf16[64,1024]{1,0:T(8,128)(2,1)S(1)}, u32[]{:S(2)}, u32[]{:S(2)}) %collective-permute-start.16) | collective-permute-done | bytes 131104 | tf_op jit(solution)/shard_map/ppermute | solution.py:145
  73.5 3.3 %fusion.32 = f32[256,1792]{1,0:T(8,128)S(1)} fusion(bf16[256,1024]{1,0:T(8,128)(2,1)S(1)} %get-tuple-element.60, bf16[1,4096,1792]{2,1,0:T(8,128)(2,1)} %param.20, s32[]{:T(128)S(6)} %select_n.268), kind=kOutput, calls=%fused_computation.29 | convolution fusion | flops 939524096 | bytes 6029316 | tf_op jit(solution)/shard_map/dot_general | solution.py:161
  79.7 1.5 %collective-permute-start.24 = (bf16[64,1024]{1,0:T(8,128)(2,1)S(1)}, bf16[64,1024]{1,0:T(8,128)(2,1)S(1)}, u32[]{:S(2)}, u32[]{:S(2)}) collective-permute-start(bf16[64,1024]{1,0:T(8,128)(2,1)S(1)} %convolution_convert_fusion.9), channel_id=1, source_target_pairs={{0,2},{1,3},{2,0},{3,1},{4,6},{5,7},{6,4},{7,5},{8,10},{9,11},{10,... | collective-permute-start | bytes 393224 | tf_op jit(solution)/shard_map/ppermute | solution.py:145
  83.0 5.6 %collective-permute-done.26 = bf16[1,128,1024]{2,1,0:T(8,128)(2,1)S(1)} collective-permute-done((bf16[1,128,1024]{2,1,0:T(8,128)(2,1)S(1)}, bf16[1,128,1024]{2,1,0:T(8,128)(2,1)S(1)}, u32[]{:S(2)}, u32[]{:S(2)}) %collective-permute-start.26) | collective-permute-done | bytes 262176 | tf_op jit(solution)/shard_map/ppermute | solution.py:136
  91.0 3.2 %collective-permute-done.21 = bf16[64,1024]{1,0:T(8,128)(2,1)S(1)} collective-permute-done((bf16[64,1024]{1,0:T(8,128)(2,1)S(1)}, bf16[64,1024]{1,0:T(8,128)(2,1)S(1)}, u32[]{:S(2)}, u32[]{:S(2)}) %collective-permute-start.21) | collective-permute-done | bytes 131104 | tf_op jit(solution)/shard_map/ppermute | solution.py:145
  94.2 1.4 collective-permute-start.28
  102.8 1.8 %collective-permute-done.29 = bf16[64,1024]{1,0:T(8,128)(2,1)S(1)} collective-permute-done((bf16[64,1024]{1,0:T(8,128)(2,1)S(1)}, bf16[64,1024]{1,0:T(8,128)(2,1)S(1)}, u32[]{:S(2)}, u32[]{:S(2)}) %collective-permute-start.29) | collective-permute-done | bytes 131104 | tf_op jit(solution)/shard_map/ppermute | solution.py:145
  106.6 3.3 %fusion.56 = f32[256,1792]{1,0:T(8,128)S(1)} fusion(f32[256,1792]{1,0:T(8,128)S(1)} %fusion.50, bf16[256,1024]{1,0:T(8,128)(2,1)S(1)} %pad_maximum_fusion.5, bf16[1,4096,1792]{2,1,0:T(8,128)(2,1)} %param.19, s32[]{:T(128)S(6)} %select_n.271), kind=kOutput, calls=%fused_computation.45 | convolution fusion | flops 939982848 | bytes 7864324 | tf_op jit(solution)/shard_map/dot_general | solution.py:160
  111.1 2.3 %fusion.10 = bf16[128,4096]{1,0:T(8,128)(2,1)S(1)} fusion(bf16[1,1792,4096]{2,1,0:T(8,128)(2,1)S(1)} %bitcast.280, f32[128]{0:T(128)S(1)} %pad_bitcast_fusion, bf16[64,1792]{1,0:T(8,128)(2,1)S(1)} %get-tuple-element.62, bf16[64,1792]{1,0:T(8,128)(2,1)S(1)} %get-tuple-element.61), kind=kOutput, calls=%fused_computation.8 | convolution fusion | flops 1881014272 | bytes 16187904 | tf_op jit(solution)/shard_map/dot_general | solution.py:233
  116.5 2.7 %fusion.16 = bf16[64,4096]{1,0:T(8,128)(2,1)S(1)} fusion(bf16[1,1792,4096]{2,1,0:T(8,128)(2,1)S(1)} %bitcast.280, f32[64]{0:T(128)S(1)} %add_divide_fusion.1, bf16[256,1792]{1,0:T(8,128)(2,1)S(1)} %multiply_convert_fusion, s32[]{:T(128)S(6)} %select_n.279), kind=kOutput, calls=%fused_computation.13 | convolution fusion | flops 940048384 | bytes 15434244 | tf_op jit(solution)/shard_map/dot_general | solution.py:242
  119.6 4.9 %collective-permute-done.31 = bf16[1,32,4096]{2,1,0:T(8,128)(2,1)S(1)} collective-permute-done((bf16[1,32,4096]{2,1,0:T(8,128)(2,1)S(1)}, bf16[1,32,4096]{2,1,0:T(8,128)(2,1)S(1)}, u32[]{:S(2)}, u32[]{:S(2)}) %collective-permute-start.31) | collective-permute-done | bytes 262176 | tf_op jit(solution)/shard_map/ppermute | solution.py:222
  124.5 1.7 %collective-permute-start.32 = (bf16[32,4096]{1,0:T(8,128)(2,1)S(1)}, bf16[32,4096]{1,0:T(8,128)(2,1)S(1)}, u32[]{:S(2)}, u32[]{:S(2)}) collective-permute-start(bf16[32,4096]{1,0:T(8,128)(2,1)S(1)} %fusion.112), channel_id=1, source_target_pairs={{0,8},{4,12},{8,0},{12,4},{1,9},{5,13},{9,1},{13,5},{2,10},{6,14},... | collective-permute-start | bytes 786440 | tf_op jit(solution)/shard_map/ppermute | solution.py:245
  127.2 2.7 %fusion.1 = f32[64,4096]{1,0:T(8,128)S(1)} fusion(bf16[1,1792,4096]{2,1,0:T(8,128)(2,1)S(1)} %bitcast.280, bf16[256,1792]{1,0:T(8,128)(2,1)S(1)} %multiply_convert_fusion, s32[]{:T(128)S(6)} %select_n.281), kind=kOutput, calls=%fused_computation.1 | convolution fusion | flops 939524096 | bytes 15958020 | tf_op jit(solution)/shard_map/dot_general | solution.py:247
  131.2 2.6 %collective-permute-done.34 = bf16[1,32,4096]{2,1,0:T(8,128)(2,1)S(1)} collective-permute-done((bf16[1,32,4096]{2,1,0:T(8,128)(2,1)S(1)}, bf16[1,32,4096]{2,1,0:T(8,128)(2,1)S(1)}, u32[]{:S(2)}, u32[]{:S(2)}) %collective-permute-start.34) | collective-permute-done | bytes 262176 | tf_op jit(solution)/shard_map/ppermute | solution.py:222
  133.9 1.3 collective-permute-start.35
  136.8 4.5 %collective-permute-done.32 = bf16[32,4096]{1,0:T(8,128)(2,1)S(1)} collective-permute-done((bf16[32,4096]{1,0:T(8,128)(2,1)S(1)}, bf16[32,4096]{1,0:T(8,128)(2,1)S(1)}, u32[]{:S(2)}, u32[]{:S(2)}) %collective-permute-start.32) | collective-permute-done | bytes 262176 | tf_op jit(solution)/shard_map/ppermute | solution.py:245
  141.3 4.5 %collective-permute-done.35 = bf16[32,4096]{1,0:T(8,128)(2,1)S(1)} collective-permute-done((bf16[32,4096]{1,0:T(8,128)(2,1)S(1)}, bf16[32,4096]{1,0:T(8,128)(2,1)S(1)}, u32[]{:S(2)}, u32[]{:S(2)}) %collective-permute-start.35) | collective-permute-done | bytes 262176 | tf_op jit(solution)/shard_map/ppermute | solution.py:245
  (203 shorter events, 43.6 us)
Async XLA Ops:
  0.0 21.2 %collective-permute-start.6 = (bf16[512,128]{1,0:T(8,128)(2,1)}, bf16[512,128]{1,0:T(8,128)(2,1)S(1)}, u32[]{:S(2)}, u32[]{:S(2)}) collective-permute-start(bf16[512,128]{1,0:T(8,128)(2,1)} %param.12), channel_id=1, source_target_pairs={{0,4},{4,8},{8,12},{12,0},{1,5},{5,9},{9,13},{13,1},{2,6},{6,10},{... | collective-permute-start | bytes 393224 | tf_op jit(solution)/shard_map/ppermute | solution.py:14
  3.0 18.5 %collective-permute-start.7 = (bf16[512,128]{1,0:T(8,128)(2,1)}, bf16[512,128]{1,0:T(8,128)(2,1)S(1)}, u32[]{:S(2)}, u32[]{:S(2)}) collective-permute-start(bf16[512,128]{1,0:T(8,128)(2,1)} %param.12), channel_id=1, source_target_pairs={{0,8},{4,12},{8,0},{12,4},{1,9},{5,13},{9,1},{13,5},{2,10},{6,14},... | collective-permute-start | bytes 393224 | tf_op jit(solution)/shard_map/ppermute | solution.py:14
  5.6 8.0 %collective-permute-start.1 = (s32[128,2]{0,1:T(2,128)}, s32[128,2]{0,1:T(2,128)S(1)}, u32[]{:S(2)}, u32[]{:S(2)}) collective-permute-start(s32[128,2]{0,1:T(2,128)} %param.17), channel_id=1, source_target_pairs={{0,4},{4,8},{8,12},{12,0},{1,5},{5,9},{9,13},{13,1},{2,6},{6,10},{... | collective-permute-start | bytes 3080 | tf_op jit(solution)/shard_map/ppermute | solution.py:14
  5.7 8.8 %collective-permute-start = (s32[128,2]{0,1:T(2,128)}, s32[128,2]{0,1:T(2,128)S(1)}, u32[]{:S(2)}, u32[]{:S(2)}) collective-permute-start(s32[128,2]{0,1:T(2,128)} %param.17), channel_id=1, source_target_pairs={{0,8},{4,12},{8,0},{12,4},{1,9},{5,13},{9,1},{13,5},{2,10},{6,14},... | collective-permute-start | bytes 3080 | tf_op jit(solution)/shard_map/ppermute | solution.py:14
  7.5 8.2 %collective-permute-start.2 = (s32[128,2]{0,1:T(2,128)}, s32[128,2]{0,1:T(2,128)S(1)}, u32[]{:S(2)}, u32[]{:S(2)}) collective-permute-start(s32[128,2]{0,1:T(2,128)} %param.17), channel_id=1, source_target_pairs={{0,12},{4,0},{8,4},{12,8},{1,13},{5,1},{9,5},{13,9},{2,14},{6,2},{... | collective-permute-start | bytes 3080 | tf_op jit(solution)/shard_map/ppermute | solution.py:14
  13.7 9.5 %collective-permute-start.8 = (bf16[512,128]{1,0:T(8,128)(2,1)}, bf16[512,128]{1,0:T(8,128)(2,1)S(1)}, u32[]{:S(2)}, u32[]{:S(2)}) collective-permute-start(bf16[512,128]{1,0:T(8,128)(2,1)} %param.12), channel_id=1, source_target_pairs={{0,12},{4,0},{8,4},{12,8},{1,13},{5,1},{9,5},{13,9},{2,14},{6,2},{... | collective-permute-start | bytes 393224 | tf_op jit(solution)/shard_map/ppermute | solution.py:14
  14.5 13.9 %collective-permute-start.3 = (bf16[512,128]{0,1:T(8,128)(2,1)S(1)}, bf16[512,128]{0,1:T(8,128)(2,1)S(1)}, u32[]{:S(2)}, u32[]{:S(2)}) collective-permute-start(bf16[512,128]{0,1:T(8,128)(2,1)S(1)} %copy.29), channel_id=1, source_target_pairs={{0,4},{4,8},{8,12},{12,0},{1,5},{5,9},{9,13},{13,1},{2,6},{6,10},{... | collective-permute-start | bytes 393224 | tf_op jit(solution)/shard_map/ppermute | solution.py:14
  15.8 13.9 %collective-permute-start.4 = (bf16[512,128]{0,1:T(8,128)(2,1)S(1)}, bf16[512,128]{0,1:T(8,128)(2,1)S(1)}, u32[]{:S(2)}, u32[]{:S(2)}) collective-permute-start(bf16[512,128]{0,1:T(8,128)(2,1)S(1)} %copy.29), channel_id=1, source_target_pairs={{0,8},{4,12},{8,0},{12,4},{1,9},{5,13},{9,1},{13,5},{2,10},{6,14},... | collective-permute-start | bytes 393224 | tf_op jit(solution)/shard_map/ppermute | solution.py:14
  21.2 8.5 %collective-permute-start.5 = (bf16[512,128]{0,1:T(8,128)(2,1)S(1)}, bf16[512,128]{0,1:T(8,128)(2,1)S(1)}, u32[]{:S(2)}, u32[]{:S(2)}) collective-permute-start(bf16[512,128]{0,1:T(8,128)(2,1)S(1)} %copy.29), channel_id=1, source_target_pairs={{0,12},{4,0},{8,4},{12,8},{1,13},{5,1},{9,5},{13,9},{2,14},{6,2},{... | collective-permute-start | bytes 393224 | tf_op jit(solution)/shard_map/ppermute | solution.py:14
  21.6 32.6 %collective-permute-start.14 = (bf16[128,1024]{1,0:T(8,128)(2,1)}, bf16[128,1024]{1,0:T(8,128)(2,1)S(1)}, u32[]{:S(2)}, u32[]{:S(2)}) collective-permute-start(bf16[128,1024]{1,0:T(8,128)(2,1)} %param.15), channel_id=1, source_target_pairs={{0,0},{1,4},{2,8},{3,12},{4,1},{5,5},{6,9},{7,13},{8,2},{9,6},{10,... | collective-permute-start | bytes 786440 | tf_op jit(solution)/shard_map/ppermute | solution.py:62
  31.7 11.5 %collective-permute-start.9 = (bf16[128,512]{0,1:T(8,128)(2,1)S(1)}, bf16[128,512]{0,1:T(8,128)(2,1)S(1)}, u32[]{:S(2)}, u32[]{:S(2)}) collective-permute-start(bf16[128,512]{0,1:T(8,128)(2,1)S(1)} %bitcast.291), channel_id=1, source_target_pairs={{0,4},{4,8},{8,12},{12,0},{1,5},{5,9},{9,13},{13,1},{2,6},{6,10},{... | collective-permute-start | bytes 393224 | tf_op jit(solution)/shard_map/ppermute | solution.py:14
  39.5 11.4 %collective-permute-start.10 = (bf16[128,512]{0,1:T(8,128)(2,1)S(1)}, bf16[128,512]{0,1:T(8,128)(2,1)S(1)}, u32[]{:S(2)}, u32[]{:S(2)}) collective-permute-start(bf16[128,512]{0,1:T(8,128)(2,1)S(1)} %bitcast.292), channel_id=1, source_target_pairs={{0,8},{4,12},{8,0},{12,4},{1,9},{5,13},{9,1},{13,5},{2,10},{6,14},... | collective-permute-start | bytes 393224 | tf_op jit(solution)/shard_map/ppermute | solution.py:14
  39.5 11.4 %collective-permute-start.11 = (bf16[128,512]{0,1:T(8,128)(2,1)S(1)}, bf16[128,512]{0,1:T(8,128)(2,1)S(1)}, u32[]{:S(2)}, u32[]{:S(2)}) collective-permute-start(bf16[128,512]{0,1:T(8,128)(2,1)S(1)} %bitcast.293), channel_id=1, source_target_pairs={{0,12},{4,0},{8,4},{12,8},{1,13},{5,1},{9,5},{13,9},{2,14},{6,2},{... | collective-permute-start | bytes 393224 | tf_op jit(solution)/shard_map/ppermute | solution.py:14
  54.0 8.4 %collective-permute-start.13 = (bf16[1,128,1024]{2,1,0:T(8,128)(2,1)S(1)}, bf16[1,128,1024]{2,1,0:T(8,128)(2,1)S(1)}, u32[]{:S(2)}, u32[]{:S(2)}) collective-permute-start(bf16[1,128,1024]{2,1,0:T(8,128)(2,1)S(1)} %fusion.108), channel_id=1, source_target_pairs={{0,2},{1,3},{2,0},{3,1},{4,6},{5,7},{6,4},{7,5},{8,10},{9,11},{10,... | collective-permute-start | bytes 786440 | tf_op jit(solution)/shard_map/ppermute | solution.py:115
  62.5 16.0 %collective-permute-start.22 = (bf16[1,128,1024]{2,1,0:T(8,128)(2,1)S(1)}, bf16[1,128,1024]{2,1,0:T(8,128)(2,1)S(1)}, u32[]{:S(2)}, u32[]{:S(2)}) collective-permute-start(bf16[1,128,1024]{2,1,0:T(8,128)(2,1)S(1)} %fusion.90), channel_id=1, source_target_pairs={{0,12},{4,0},{8,4},{12,8},{1,13},{5,1},{9,5},{13,9},{2,14},{6,2},{... | collective-permute-start | bytes 786440 | tf_op jit(solution)/shard_map/ppermute | solution.py:136
  65.6 15.6 %collective-permute-start.18 = (bf16[1,128,1024]{2,1,0:T(8,128)(2,1)S(1)}, bf16[1,128,1024]{2,1,0:T(8,128)(2,1)S(1)}, u32[]{:S(2)}, u32[]{:S(2)}) collective-permute-start(bf16[1,128,1024]{2,1,0:T(8,128)(2,1)S(1)} %fusion.90), channel_id=1, source_target_pairs={{0,4},{4,8},{8,12},{12,0},{1,5},{5,9},{9,13},{13,1},{2,6},{6,10},{... | collective-permute-start | bytes 786440 | tf_op jit(solution)/shard_map/ppermute | solution.py:136
  71.2 17.5 %collective-permute-start.26 = (bf16[1,128,1024]{2,1,0:T(8,128)(2,1)S(1)}, bf16[1,128,1024]{2,1,0:T(8,128)(2,1)S(1)}, u32[]{:S(2)}, u32[]{:S(2)}) collective-permute-start(bf16[1,128,1024]{2,1,0:T(8,128)(2,1)S(1)} %fusion.90), channel_id=1, source_target_pairs={{0,8},{4,12},{8,0},{12,4},{1,9},{5,13},{9,1},{13,5},{2,10},{6,14},... | collective-permute-start | bytes 786440 | tf_op jit(solution)/shard_map/ppermute | solution.py:136
  78.7 20.1 %collective-permute-start.23 = (bf16[64,1024]{1,0:T(8,128)(2,1)S(1)}, bf16[64,1024]{1,0:T(8,128)(2,1)S(1)}, u32[]{:S(2)}, u32[]{:S(2)}) collective-permute-start(bf16[64,1024]{1,0:T(8,128)(2,1)S(1)} %convolution_convert_fusion.10), channel_id=1, source_target_pairs={{0,1},{1,0},{2,3},{3,2},{4,5},{5,4},{6,7},{7,6},{8,9},{9,8},{10,11... | collective-permute-start | bytes 393224 | tf_op jit(solution)/shard_map/ppermute | solution.py:145
  79.7 19.8 %collective-permute-start.24 = (bf16[64,1024]{1,0:T(8,128)(2,1)S(1)}, bf16[64,1024]{1,0:T(8,128)(2,1)S(1)}, u32[]{:S(2)}, u32[]{:S(2)}) collective-permute-start(bf16[64,1024]{1,0:T(8,128)(2,1)S(1)} %convolution_convert_fusion.9), channel_id=1, source_target_pairs={{0,2},{1,3},{2,0},{3,1},{4,6},{5,7},{6,4},{7,5},{8,10},{9,11},{10,... | collective-permute-start | bytes 393224 | tf_op jit(solution)/shard_map/ppermute | solution.py:145
  81.4 8.2 %collective-permute-start.19 = (bf16[64,1024]{1,0:T(8,128)(2,1)S(1)}, bf16[64,1024]{1,0:T(8,128)(2,1)S(1)}, u32[]{:S(2)}, u32[]{:S(2)}) collective-permute-start(bf16[64,1024]{1,0:T(8,128)(2,1)S(1)} %convolution_convert_fusion.14), channel_id=1, source_target_pairs={{0,1},{1,0},{2,3},{3,2},{4,5},{5,4},{6,7},{7,6},{8,9},{9,8},{10,11... | collective-permute-start | bytes 393224 | tf_op jit(solution)/shard_map/ppermute | solution.py:145
  81.7 9.2 %collective-permute-start.20 = (bf16[64,1024]{1,0:T(8,128)(2,1)S(1)}, bf16[64,1024]{1,0:T(8,128)(2,1)S(1)}, u32[]{:S(2)}, u32[]{:S(2)}) collective-permute-start(bf16[64,1024]{1,0:T(8,128)(2,1)S(1)} %convolution_convert_fusion.13), channel_id=1, source_target_pairs={{0,2},{1,3},{2,0},{3,1},{4,6},{5,7},{6,4},{7,5},{8,10},{9,11},{10,... | collective-permute-start | bytes 393224 | tf_op jit(solution)/shard_map/ppermute | solution.py:145
  89.7 9.9 %collective-permute-start.25 = (bf16[64,1024]{1,0:T(8,128)(2,1)S(1)}, bf16[64,1024]{1,0:T(8,128)(2,1)S(1)}, u32[]{:S(2)}, u32[]{:S(2)}) collective-permute-start(bf16[64,1024]{1,0:T(8,128)(2,1)S(1)} %convolution_convert_fusion.8), channel_id=1, source_target_pairs={{0,3},{1,2},{2,1},{3,0},{4,7},{5,6},{6,5},{7,4},{8,11},{9,10},{10,... | collective-permute-start | bytes 393224 | tf_op jit(solution)/shard_map/ppermute | solution.py:145
  90.9 11.9 %collective-permute-start.27 = (bf16[64,1024]{1,0:T(8,128)(2,1)S(1)}, bf16[64,1024]{1,0:T(8,128)(2,1)S(1)}, u32[]{:S(2)}, u32[]{:S(2)}) collective-permute-start(bf16[64,1024]{1,0:T(8,128)(2,1)S(1)} %convolution_convert_fusion.6), channel_id=1, source_target_pairs={{0,1},{1,0},{2,3},{3,2},{4,5},{5,4},{6,7},{7,6},{8,9},{9,8},{10,11... | collective-permute-start | bytes 393224 | tf_op jit(solution)/shard_map/ppermute | solution.py:145
  94.2 8.6 %collective-permute-start.28 = (bf16[64,1024]{1,0:T(8,128)(2,1)S(1)}, bf16[64,1024]{1,0:T(8,128)(2,1)S(1)}, u32[]{:S(2)}, u32[]{:S(2)}) collective-permute-start(bf16[64,1024]{1,0:T(8,128)(2,1)S(1)} %convolution_convert_fusion.5), channel_id=1, source_target_pairs={{0,2},{1,3},{2,0},{3,1},{4,6},{5,7},{6,4},{7,5},{8,10},{9,11},{10,... | collective-permute-start | bytes 393224 | tf_op jit(solution)/shard_map/ppermute | solution.py:145
  98.9 5.8 %collective-permute-start.29 = (bf16[64,1024]{1,0:T(8,128)(2,1)S(1)}, bf16[64,1024]{1,0:T(8,128)(2,1)S(1)}, u32[]{:S(2)}, u32[]{:S(2)}) collective-permute-start(bf16[64,1024]{1,0:T(8,128)(2,1)S(1)} %convolution_convert_fusion.4), channel_id=1, source_target_pairs={{0,3},{1,2},{2,1},{3,0},{4,7},{5,6},{6,5},{7,4},{8,11},{9,10},{10,... | collective-permute-start | bytes 393224 | tf_op jit(solution)/shard_map/ppermute | solution.py:145
  113.9 16.7 %collective-permute-start.36 = (bf16[64,4096]{1,0:T(8,128)(2,1)S(1)}, bf16[64,4096]{1,0:T(8,128)(2,1)S(1)}, u32[]{:S(2)}, u32[]{:S(2)}) collective-permute-start(bf16[64,4096]{1,0:T(8,128)(2,1)S(1)} %split.9), channel_id=1, source_target_pairs={{0,4},{4,8},{8,12},{12,0},{1,5},{5,9},{9,13},{13,1},{2,6},{6,10},{... | collective-permute-start | bytes 1572872 | tf_op jit(solution)/shard_map/ppermute | solution.py:236
  116.0 8.4 %collective-permute-start.31 = (bf16[1,32,4096]{2,1,0:T(8,128)(2,1)S(1)}, bf16[1,32,4096]{2,1,0:T(8,128)(2,1)S(1)}, u32[]{:S(2)}, u32[]{:S(2)}) collective-permute-start(bf16[1,32,4096]{2,1,0:T(8,128)(2,1)S(1)} %fusion.109), channel_id=1, source_target_pairs={{0,2},{1,3},{2,0},{3,1},{4,6},{5,7},{6,4},{7,5},{8,10},{9,11},{10,... | collective-permute-start | bytes 786440 | tf_op jit(solution)/shard_map/ppermute | solution.py:222
  119.5 6.7 %collective-permute-start.33 = (bf16[64,4096]{1,0:T(8,128)(2,1)S(1)}, bf16[64,4096]{1,0:T(8,128)(2,1)S(1)}, u32[]{:S(2)}, u32[]{:S(2)}) collective-permute-start(bf16[64,4096]{1,0:T(8,128)(2,1)S(1)} %convolution_convert_fusion.1), channel_id=1, source_target_pairs={{0,1},{1,0},{2,3},{3,2},{4,5},{5,4},{6,7},{7,6},{8,9},{9,8},{10,11... | collective-permute-start | bytes 1572872 | tf_op jit(solution)/shard_map/ppermute | solution.py:213
  124.5 16.8 %collective-permute-start.32 = (bf16[32,4096]{1,0:T(8,128)(2,1)S(1)}, bf16[32,4096]{1,0:T(8,128)(2,1)S(1)}, u32[]{:S(2)}, u32[]{:S(2)}) collective-permute-start(bf16[32,4096]{1,0:T(8,128)(2,1)S(1)} %fusion.112), channel_id=1, source_target_pairs={{0,8},{4,12},{8,0},{12,4},{1,9},{5,13},{9,1},{13,5},{2,10},{6,14},... | collective-permute-start | bytes 786440 | tf_op jit(solution)/shard_map/ppermute | solution.py:245
  126.5 7.3 %collective-permute-start.34 = (bf16[1,32,4096]{2,1,0:T(8,128)(2,1)S(1)}, bf16[1,32,4096]{2,1,0:T(8,128)(2,1)S(1)}, u32[]{:S(2)}, u32[]{:S(2)}) collective-permute-start(bf16[1,32,4096]{2,1,0:T(8,128)(2,1)S(1)} %fusion.110), channel_id=1, source_target_pairs={{0,2},{1,3},{2,0},{3,1},{4,6},{5,7},{6,4},{7,5},{8,10},{9,11},{10,... | collective-permute-start | bytes 786440 | tf_op jit(solution)/shard_map/ppermute | solution.py:222
  133.9 11.9 %collective-permute-start.35 = (bf16[32,4096]{1,0:T(8,128)(2,1)S(1)}, bf16[32,4096]{1,0:T(8,128)(2,1)S(1)}, u32[]{:S(2)}, u32[]{:S(2)}) collective-permute-start(bf16[32,4096]{1,0:T(8,128)(2,1)S(1)} %fusion.113), channel_id=1, source_target_pairs={{0,12},{4,0},{8,4},{12,8},{1,13},{5,1},{9,5},{13,9},{2,14},{6,2},{... | collective-permute-start | bytes 786440 | tf_op jit(solution)/shard_map/ppermute | solution.py:245
  135.6 10.2 %collective-permute-start.38 = (bf16[1,32,4096]{2,1,0:T(8,128)(2,1)S(1)}, bf16[1,32,4096]{2,1,0:T(8,128)(2,1)S(1)}, u32[]{:S(2)}, u32[]{:S(2)}) collective-permute-start(bf16[1,32,4096]{2,1,0:T(8,128)(2,1)S(1)} %fusion.111), channel_id=1, source_target_pairs={{0,2},{1,3},{2,0},{3,1},{4,6},{5,7},{6,4},{7,5},{8,10},{9,11},{10,... | collective-permute-start | bytes 786440 | tf_op jit(solution)/shard_map/ppermute | solution.py:222
  (19 other events, 284.2 us)
